TPU v7x, 32 devices: a whole 2x2x4 slice. The times are simulated.
32 devices in a mesh: pair: 4 (over y, x), mode: 8 (over z, core).
Axes of the slice: x: 2, y: 2, z: 4, core: 2. Of those that a mesh axis runs over, the one named last changes fastest.
Arguments:
- phi: bfloat16 [4, 384, 384, 384], P('pair', 'mode'), may hold values from -6 to 6
- eigvecs: bfloat16 [12, 384, 384], replicated, may hold values from -0.3125 to 0.3125
- freqs: float32 [12, 384], replicated, may hold values from 0.5 to 8
- occupations: float32 [12, 384], replicated, may hold values from 0.02 to 4
- smearing: float32 [12, 384], replicated, may hold values from 0.2 to 1
- probes: float32 [4, 2], P('pair'), may hold values from 0.5 to 8
- pair_index: int32 [4, 3], P('pair'), may hold values from 0 to 11
Outputs:
- sigma: float32 [384, 2, 384], P('mode', None, 'pair')
All inputs are finite; a program needn't handle non-finite values.
Results may differ from a plain program's by a relative error of at most 0.0013.
Values may be sent and summed in bfloat16 or wider, within the bound.
No kernel may reach another device: no remote copies, remote signals or barrier semaphores. Data moves between devices by JAX's collectives and lax.ppermute only.
A program may use at most 128 MiB of HBM per device.

v0:
```python
import math

import jax
import jax.numpy as jnp
from jax import lax
from jax.sharding import PartitionSpec as P


def lorentz(offset, eta):
    return eta / (offset * offset + eta * eta)


def weights(f_one, n_one, h_one, f_two, n_two, h_two, omegas):
    total = f_two[:, None] + f_one[None, :]
    differ = f_two[:, None] - f_one[None, :]
    eta = 0.5 * (h_two[:, None] + h_one[None, :])
    bose_sum = 1.0 + n_one[None, :] + n_two[:, None]
    bose_diff = n_one[None, :] - n_two[:, None]
    result = []
    for probe in range(2):
        omega = omegas[probe]
        value = bose_sum * (lorentz(omega - total, eta) - lorentz(omega + total, eta))
        value = value + bose_diff * (lorentz(omega - differ, eta) - lorentz(omega + differ, eta))
        result.append(value)
    return jnp.stack(result)


def shards(phi, eigvecs, freqs, occupations, smearing, probes, pair_index):
    tensor = phi[0]
    slices = tensor.shape[0]
    modes = tensor.shape[1]
    q_one = pair_index[0, 0]
    q_two = pair_index[0, 1]
    q_three = pair_index[0, 2]
    e_one = lax.dynamic_index_in_dim(eigvecs, q_one, 0, keepdims=False)
    e_two = lax.dynamic_index_in_dim(eigvecs, q_two, 0, keepdims=False)
    e_three = lax.dynamic_index_in_dim(eigvecs, q_three, 0, keepdims=False)
    first = jnp.dot(
        tensor.reshape(slices * modes, modes), e_one, preferred_element_type=jnp.float32
    )
    first = first.astype(jnp.bfloat16).reshape(slices, modes, modes)
    second = jnp.einsum("cbi,bj->cji", first, e_two, preferred_element_type=jnp.float32).astype(
        jnp.bfloat16
    )
    arrived = lax.all_to_all(second, "mode", split_axis=1, concat_axis=0, tiled=True)
    span = arrived.shape[1]
    count = arrived.shape[2]
    flat = lax.dot_general(
        e_three,
        arrived.reshape(arrived.shape[0], span * count),
        (((0,), (0,)), ((), ())),
        preferred_element_type=jnp.float32,
    )
    rotated = flat.astype(jnp.bfloat16).reshape(modes, span, count)
    span = rotated.shape[1]
    offset = lax.axis_index("mode") * span
    f_two = lax.dynamic_slice_in_dim(freqs[q_two], offset, span)
    n_two = lax.dynamic_slice_in_dim(occupations[q_two], offset, span)
    h_two = lax.dynamic_slice_in_dim(smearing[q_two], offset, span)
    wgt = weights(freqs[q_one], occupations[q_one], smearing[q_one], f_two, n_two, h_two, probes[0])
    flat_rot = rotated.reshape(modes, span * modes)
    weighted = (wgt.reshape(2, 1, span * modes) * flat_rot.astype(jnp.float32)[None]).astype(
        jnp.bfloat16
    )
    pair_size = lax.axis_size("pair")
    whole = jnp.einsum("wkl,nl->kwn", weighted, flat_rot, preferred_element_type=jnp.float32)
    reduced = lax.psum_scatter(whole, "pair", scatter_dimension=2, tiled=True)
    local = lax.psum_scatter(reduced, "mode", scatter_dimension=0, tiled=True)
    row_count = local.shape[0]
    col_count = local.shape[2]
    row_ids = lax.axis_index("mode") * row_count + jnp.arange(row_count, dtype=jnp.int32)
    col_ids = lax.axis_index("pair") * col_count + jnp.arange(col_count, dtype=jnp.int32)
    offdiag = (row_ids[:, None] != col_ids[None, :]).astype(jnp.float32)
    scale = 1.0 / (modes * math.sqrt(pair_size))
    return local * offdiag[:, None, :] * scale


def solution(mesh):
    return jax.shard_map(
        shards,
        mesh=mesh,
        in_specs=(
            P("pair", "mode", None, None),
            P(),
            P(),
            P(),
            P(),
            P("pair", None),
            P("pair", None),
        ),
        out_specs=P("mode", None, "pair"),
        check_vma=False,
    )
```

profile of v0, /device:TPU:0, one launch (start us, length us, event | category | flops | bytes accessed | tf_op | source)
XLA Modules:
  0.0 562.4 jit_solution(9959764007746708969)
XLA Ops:
  6.5 0.0 copy-start
  6.5 1.5 fusion.21
  11.2 0.0 copy-done
  11.2 21.1 %fusion.3 = bf16[18432,384]{0,1:T(8,128)(2,1)} fusion(bf16[18432,384]{1,0:T(8,128)(2,1)} %bitcast.57, bf16[12,384,384]{2,1,0:T(8,128)(2,1)S(1)} %copy-done, s32[]{:T(128)S(6)} %select_n.27), kind=kOutput, calls=%fused_computation.6 | convolution fusion | flops 5442895872 | bytes 28606468 | tf_op jit(solution)/shard_map/dot_general | solution.py:38
  32.4 18.6 %copy.20 = bf16[18432,384]{1,0:T(8,128)(2,1)} copy(bf16[18432,384]{0,1:T(8,128)(2,1)} %fusion.3) | data formatting | bytes 28311552 | tf_op jit(solution)/shard_map/reshape | solution.py:41
  51.6 15.2 %convert_bitcast_fusion = bf16[48,384,384]{2,1,0:T(8,128)(2,1)} fusion(bf16[48,384,384]{2,1,0:T(8,128)(2,1)} %bitcast.55, bf16[12,384,384]{2,1,0:T(8,128)(2,1)S(1)} %copy-done, s32[]{:T(128)S(6)} %select_n.26), kind=kOutput, calls=%fused_computation.8 | convolution fusion | flops 5442895872 | bytes 28606468 | tf_op jit(solution)/shard_map/cbi,bj->cji/dot_general | solution.py:42
  66.8 31.6 %copy.17 = bf16[48,384,384]{2,0,1:T(8,128)(2,1)} copy(bf16[48,384,384]{2,1,0:T(8,128)(2,1)} %convert_bitcast_fusion) | data formatting | bytes 28311552 | tf_op jit(solution)/shard_map/convert_element_type | solution.py:42
  98.4 0.0 copy-start.2
  98.4 6.4 %all-to-all-start = ((bf16[48,384,384]{2,0,1:T(8,128)(2,1)}), bf16[48,384,384]{2,0,1:T(8,128)(2,1)}, u32[]{:S(2)}, u32[]{:S(2)}) async-start(bf16[48,384,384]{2,0,1:T(8,128)(2,1)} %copy.17), calls=%async_computation | async-start | bytes 28311552 | tf_op jit(solution)/shard_map/all_to_all | solution.py:45
  104.8 0.2 reduce-scatter.2.cloned.1.call-start
  106.4 0.8 dynamic-slice_bitcast_fusion
  107.2 0.7 add.329
  107.9 1.6 add.330
  109.4 0.7 dynamic-slice_reduce_fusion
  110.2 0.6 add.332
  110.8 1.6 add.333
  112.4 0.7 add_reduce_fusion
  113.1 0.6 sub.150
  113.8 1.6 sub.151
  115.4 0.8 dynamic-slice_bitcast_fusion.2
  116.1 0.7 add.320
  116.8 1.6 add.321
  118.4 0.6 add.317
  119.0 1.6 add.318
  120.6 0.7 add.323
  121.3 1.6 add.324
  122.9 0.6 add.326
  123.5 1.6 add.327
  125.8 0.0 copy-done.2
  125.8 0.6 fusion.20
  126.4 3.4 multiply_add_fusion.1
  129.8 0.8 maximum_bitcast_fusion
  130.6 281.9 %all-to-all-done = bf16[48,384,384]{2,0,1:T(8,128)(2,1)} async-done(((bf16[48,384,384]{2,0,1:T(8,128)(2,1)}), bf16[48,384,384]{2,0,1:T(8,128)(2,1)}, u32[]{:S(2)}, u32[]{:S(2)}) %all-to-all-start) | async-done | bytes 14155808 | tf_op jit(solution)/shard_map/all_to_all | solution.py:45
  412.4 8.7 %copy.18 = bf16[48,8,48,384]{3,2,0,1:T(8,128)(2,1)S(1)} copy(bf16[48,8,48,384]{3,0,2,1:T(8,128)(2,1)} %bitcast.11) | data formatting | bytes 28311552 | tf_op jit(solution)/shard_map/all_to_all | solution.py:45
  421.2 6.8 %copy.21 = bf16[48,8,48,384]{3,1,2,0:T(8,128)(2,1)} copy(bf16[48,8,48,384]{3,2,1,0:T(8,128)(2,1)S(1)} %bitcast.56) | data formatting | bytes 28311552
  427.9 21.2 %fusion.22 = (f32[384,18432]{1,0:T(8,128)}, bf16[384,18432]{1,0:T(8,128)(2,1)}) fusion(bf16[384,18432]{1,0:T(8,128)(2,1)} %bitcast.54, bf16[12,384,384]{2,1,0:T(8,128)(2,1)S(1)} %copy-done, s32[]{:T(128)S(6)} %select_n.25), kind=kOutput, calls=%fused_computation.40 | convolution fusion | flops 5449973760 | bytes 56918020 | tf_op jit(solution)/shard_map/dot_general | solution.py:48
  449.2 18.9 %fusion.5 = f32[384,2,384]{0,2,1:T(8,128)} fusion(f32[384,18432]{1,0:T(8,128)} %get-tuple-element.14, f32[2,18432]{1,0:T(2,128)} %maximum_bitcast_fusion, bf16[384,18432]{1,0:T(8,128)(2,1)} %get-tuple-element.15), kind=kOutput, calls=%fused_computation.9 | convolution fusion | flops 10899947520 | bytes 43794432 | tf_op jit(solution)/shard_map/wkl,nl->kwn/dot_general | solution.py:66
  468.1 0.0 reduce-scatter.2.cloned.1.call-update
  468.1 0.0 all-reduce.3.cloned.1.call-start
  468.2 0.0 copy-done.3
  468.2 0.6 dynamic-slice.3
  469.5 26.8 %reduce-scatter.2.cloned.1.call-done = f32[384,2,96]{0,2,1:T(8,128)} async-done(((f32[384,2,384]{0,2,1:T(8,128)}), f32[384,2,96]{0,2,1:T(8,128)}) %reduce-scatter.2.cloned.1.call-update) | async-done | bytes 294928 | tf_op jit(solution)/shard_map/reduce_scatter | solution.py:67
  496.2 1.9 copy.19
  498.1 0.0 all-reduce.3.cloned.1.call-update
  498.1 0.7 compare_convert_fusion
  498.8 55.3 %all-reduce.3.cloned.1.call-done = f32[384,2,96]{2,1,0:T(2,128)} async-done(((f32[384,2,96]{2,1,0:T(2,128)}), f32[384,2,96]{2,1,0:T(2,128)}) %all-reduce.3.cloned.1.call-update) | async-done | bytes 294928
  554.1 1.5 fusion.15
  555.6 0.0 copy-done.1
  (4 shorter events, 0.0 us)
Async XLA Ops:
  6.5 4.7 copy-start
  98.4 27.4 %copy-start.2 = (f32[1,2]{1,0:T(1,128)S(1)}, f32[1,2]{1,0:T(1,128)}, u32[]{:S(2)}) copy-start(f32[1,2]{1,0:T(1,128)} %param.12) | copy-start | bytes 28
  98.4 314.0 %all-to-all-start = ((bf16[48,384,384]{2,0,1:T(8,128)(2,1)}), bf16[48,384,384]{2,0,1:T(8,128)(2,1)}, u32[]{:S(2)}, u32[]{:S(2)}) async-start(bf16[48,384,384]{2,0,1:T(8,128)(2,1)} %copy.17), calls=%async_computation | async-start | bytes 28311552 | tf_op jit(solution)/shard_map/all_to_all | solution.py:45
  104.8 391.4 %reduce-scatter.2.cloned.1.call-start = ((), (), s32[]{:S(2)}) async-start(), calls=%async_computation.2 | async-start | bytes 1474560 | tf_op jit(solution)/shard_map/reduce_scatter | solution.py:67
  449.2 19.0 %copy-start.3 = (u32[32]{0:T(128)S(1)}, u32[32]{0:T(128)}, u32[]{:S(2)}) copy-start(u32[32]{0:T(128)} %constant.72) | copy-start | bytes 388
  449.2 106.4 %copy-start.1 = (bf16[12,384,384]{2,1,0:T(8,128)(2,1)S(1)}, bf16[12,384,384]{2,1,0:T(8,128)(2,1)}, u32[]{:S(2)}) copy-start(bf16[12,384,384]{2,1,0:T(8,128)(2,1)} %param.8) | copy-start | bytes 10616836
  468.1 86.0 %all-reduce.3.cloned.1.call-start = ((), (), s32[]{:S(2)}) async-start(), calls=%async_computation.3 | async-start | bytes 786432
Sparse Core Ops, SparseCore 0:
  468.3 27.9 reduce-scatter.1
  498.5 55.5 all-reduce.2
where the time goes:
time: 564 us; the launch traced here: 562 us
  waiting for transfers between devices  364 us (65%)
  local copies, waits for them, and re-layouts  88.2 us (16%)
  matrix products  76.5 us (14%)
  between operations  19.9 us (4%)
  other arithmetic  7.05 us (1%)
  starting transfers between devices  6.7 us (1%)
    all_to_all x1, waiting for transfers between devices, shards(): lax.all_to_all(second, 'mode', split_axis=1, concat_axis=0, tiled=True)  282 us
    unnamed x3, waiting for transfers between devices  55.4 us
    convert_element_type x1, local copies, waits for them, and re-layouts, shards(): jnp.einsum('cbi,bj->cji', first, e_two, preferred_element_type=jnp.float32)  31.6 us
    reduce_scatter x1, waiting for transfers between devices, shards(): reduced = lax.psum_scatter(whole, 'pair', scatter_dimension=2, tiled=True)  26.8 us
    dot_general x1, matrix products, shards(): lax.dot_general(e_three, arrived.reshape(arrived.shape[0], span * count),...  21.2 us
    dot_general x1, matrix products, shards(): jnp.dot(tensor.reshape(slices * modes, modes), e_one, preferred_element_t...  21.1 us
    dot_general x1, matrix products, shards(): jnp.einsum('wkl,nl->kwn', weighted, flat_rot, preferred_element_type=jnp....  18.9 us
    reshape x1, local copies, waits for them, and re-layouts, shards(): first = first.astype(jnp.bfloat16).reshape(slices, modes, modes)  18.6 us
  transfers between devices with their start and end apart: 3, of which 3 were waited for; matrix products, arithmetic and copies ran while one was open for 4% of the time, Pallas kernels for 0%

commit v1 on v0

v1 whole, which is shorter than its diff:
```python
import math

import jax
import jax.numpy as jnp
from jax import lax
from jax.experimental import pallas as pl
from jax.experimental.pallas import tpu as pltpu
from jax.sharding import PartitionSpec as P

LANES = 128
GROUP = 8
F32 = jnp.float32
BF16 = jnp.bfloat16


def lorentz(offset, eta):
    return eta / (offset * offset + eta * eta)


def weight_pair(f_one, n_one, h_one, f_two, n_two, h_two, omega):
    total = f_two + f_one
    differ = f_two - f_one
    eta = 0.5 * (h_two + h_one)
    value = (1.0 + n_one + n_two) * (lorentz(omega - total, eta) - lorentz(omega + total, eta))
    return value + (n_one - n_two) * (lorentz(omega - differ, eta) - lorentz(omega + differ, eta))


def rotate_kernel(phi_ref, one_ref, two_ref, out_ref, held, turned):
    block, rows, inner = phi_ref.shape
    cols = one_ref.shape[1]
    first = jnp.dot(phi_ref[...].reshape(block * rows, inner), one_ref[...], preferred_element_type=F32)
    first = first.astype(BF16)
    for c in range(block):
        held[:, c * cols : (c + 1) * cols] = first[c * rows : (c + 1) * rows]
    wide = jnp.dot(two_ref[...], held[...], preferred_element_type=F32)
    for c in range(block):
        turned[pl.ds(c, two_ref.shape[0], stride=block), :] = wide[:, c * cols : (c + 1) * cols]
    out_ref[...] = turned[...].reshape(two_ref.shape[0], block, cols).astype(BF16)


def rotate(phi, e_one, e_two_t, block):
    slices, rows, inner = phi.shape
    cols = e_one.shape[1]
    modes = e_two_t.shape[0]
    return pl.pallas_call(
        rotate_kernel,
        grid=(slices // block,),
        in_specs=[
            pl.BlockSpec((block, rows, inner), lambda g: (g, 0, 0)),
            pl.BlockSpec((inner, cols), lambda g: (0, 0)),
            pl.BlockSpec((modes, rows), lambda g: (0, 0)),
        ],
        out_specs=pl.BlockSpec((modes, block, cols), lambda g: (0, g, 0)),
        out_shape=jax.ShapeDtypeStruct((modes, slices, cols), BF16),
        scratch_shapes=[
            pltpu.VMEM((rows, block * cols), BF16),
            pltpu.VMEM((modes * block, cols), F32),
        ],
        compiler_params=pltpu.CompilerParams(vmem_limit_bytes=40 * 2**20),
        cost_estimate=pl.CostEstimate(
            flops=2 * slices * rows * inner * cols + 2 * slices * rows * cols * modes,
            bytes_accessed=slices * rows * inner * 2 + modes * slices * cols * 2,
            transcendentals=0,
        ),
        name="rotate",
    )(phi, e_one, e_two_t)


def gram_kernel(omegas, arr_ref, three_ref, row_ref, col_ref, old_ref, out_ref, side):
    sources, span, slices, cols = arr_ref.shape
    modes = three_ref.shape[0]
    step = pl.program_id(0)

    @pl.when(step == 0)
    def _():
        out_ref[...] = old_ref[...]

    weights = [[], []]
    for g in range(span):
        side[:, g * cols : (g + 1) * cols] = arr_ref[:, g].reshape(modes, cols)
        for w in range(2):
            weights[w].append(
                weight_pair(
                    row_ref[0:1, :], row_ref[1:2, :], row_ref[2:3, :],
                    col_ref[g : g + 1, 0:1], col_ref[g : g + 1, 1:2], col_ref[g : g + 1, 2:3],
                    omegas[0, w],
                )
            )
    rotated = jnp.dot(three_ref[...], side[...], preferred_element_type=F32).astype(BF16)
    wide = rotated.astype(F32)
    for w in range(2):
        scaled = (wide * jnp.concatenate(weights[w], axis=1)).astype(BF16)
        out_ref[w] += lax.dot_general(rotated, scaled, (((1,), (1,)), ((), ())), preferred_element_type=F32)


def gram(arrived, e_three_t, rows, cols, omegas, old, group):
    sources, span, slices, width = arrived.shape
    modes = e_three_t.shape[0]
    return pl.pallas_call(
        gram_kernel,
        grid=(span // group,),
        in_specs=[
            pl.BlockSpec(memory_space=pltpu.SMEM),
            pl.BlockSpec((sources, group, slices, width), lambda g: (0, g, 0, 0)),
            pl.BlockSpec((modes, modes), lambda g: (0, 0)),
            pl.BlockSpec((3, width), lambda g: (0, 0)),
            pl.BlockSpec((group, 3), lambda g: (g, 0)),
            pl.BlockSpec((2, modes, modes), lambda g: (0, 0, 0)),
        ],
        out_specs=pl.BlockSpec((2, modes, modes), lambda g: (0, 0, 0)),
        out_shape=jax.ShapeDtypeStruct((2, modes, modes), F32),
        scratch_shapes=[pltpu.VMEM((modes, group * width), BF16)],
        input_output_aliases={5: 0},
        compiler_params=pltpu.CompilerParams(vmem_limit_bytes=40 * 2**20),
        cost_estimate=pl.CostEstimate(
            flops=2 * modes * modes * span * width * 3,
            bytes_accessed=arrived.size * 2 + modes * modes * 16,
            transcendentals=0,
        ),
        name="gram",
    )(omegas, arrived, e_three_t, rows, cols, old)


def rotate_plain(phi, e_one, e_two_t):
    first = jnp.einsum("cba,ai->cbi", phi, e_one, preferred_element_type=F32).astype(BF16)
    return jnp.einsum("jb,cbi->jci", e_two_t, first, preferred_element_type=F32).astype(BF16)


def gram_plain(arrived, e_three_t, rows, cols, omegas, old):
    sources, span, slices, width = arrived.shape
    modes = e_three_t.shape[0]
    side = jnp.transpose(arrived, (0, 2, 1, 3)).reshape(modes, span * width)
    rotated = jnp.dot(e_three_t, side, preferred_element_type=F32).astype(BF16)
    for w in range(2):
        wgt = weight_pair(
            rows[0:1], rows[1:2], rows[2:3], cols[:, 0:1], cols[:, 1:2], cols[:, 2:3], omegas[0, w]
        ).reshape(1, span * width)
        scaled = (rotated.astype(F32) * wgt).astype(BF16)
        old = old.at[w].add(jnp.einsum("kl,nl->kn", rotated, scaled, preferred_element_type=F32))
    return old


def shards(phi, eigvecs, freqs, occupations, smearing, probes, pair_index):
    tensor = phi[0]
    slices, modes = tensor.shape[0], tensor.shape[1]
    pairs, parts = lax.axis_size("pair"), lax.axis_size("mode")
    span = modes // parts
    q_one, q_two, q_three = pair_index[0, 0], pair_index[0, 1], pair_index[0, 2]
    pick = lambda table, q: lax.dynamic_index_in_dim(table, q, 0, keepdims=False)
    e_one = pick(eigvecs, q_one)
    e_two_t = pick(eigvecs, q_two).T
    e_three_t = pick(eigvecs, q_three).T
    rows = jnp.stack([pick(freqs, q_one), pick(occupations, q_one), pick(smearing, q_one)])
    cols = jnp.stack([pick(freqs, q_two), pick(occupations, q_two), pick(smearing, q_two)])
    place = lax.axis_index("mode")
    cols = lax.dynamic_slice_in_dim(cols, place * span, span, axis=1).T
    tiled = slices % 16 == 0 and span % GROUP == 0
    total = jnp.zeros((2, modes, modes), F32)
    for start in range(0, modes, LANES):
        block = e_one[:, start : start + LANES]
        width = block.shape[1]
        if tiled:
            second = rotate(tensor, block, e_two_t, 16)
        else:
            second = rotate_plain(tensor, block, e_two_t)
        second = second.reshape(parts, span, slices, width)
        arrived = lax.all_to_all(second, "mode", split_axis=0, concat_axis=0, tiled=True)
        head = rows[:, start : start + LANES]
        if tiled:
            total = gram(arrived, e_three_t, head, cols, probes, total, GROUP)
        else:
            total = gram_plain(arrived, e_three_t, head, cols, probes, total)
    core = place % 2
    kept = lax.dynamic_index_in_dim(total, core, 0, keepdims=False)
    given = lax.dynamic_index_in_dim(total, 1 - core, 0, keepdims=False)
    swap = [(i, i ^ 1) for i in range(parts)]
    part = kept + lax.ppermute(given, "mode", swap)
    part = part.reshape(pairs, modes // pairs, modes)
    low, high = part[:, : modes // pairs // 2], part[:, modes // pairs // 2 :]
    distances = [1 << b for b in range(pairs.bit_length() - 1)]
    low = halvings(low, "pair", pairs, distances)
    high = halvings(high, "pair", pairs, distances[::-1])
    part = jnp.concatenate([low[0], high[0]], axis=0).T
    part = part.reshape(parts // 2, 2, span, modes // pairs)
    part = halvings(part, "mode", parts, [2 << b for b in range(parts.bit_length() - 2)])[0]
    kept = lax.dynamic_index_in_dim(part, core, 0, keepdims=False)
    given = lax.dynamic_index_in_dim(part, 1 - core, 0, keepdims=False)
    taken = lax.ppermute(given, "mode", swap)
    local = jnp.stack([jnp.where(core == 0, kept, taken), jnp.where(core == 0, taken, kept)], axis=1)
    row_ids = place * span + jnp.arange(span, dtype=jnp.int32)
    count = modes // pairs
    col_ids = lax.axis_index("pair") * count + jnp.arange(count, dtype=jnp.int32)
    offdiag = (row_ids[:, None] != col_ids[None, :]).astype(F32)
    scale = 1.0 / (modes * math.sqrt(pairs))
    return local * offdiag[:, None, :] * scale


def halvings(x, axis, size, distances):
    place = lax.axis_index(axis)
    low = distances and min(distances)
    bits = [d // low for d in distances]
    left = list(bits)
    for distance, unit in zip(distances, bits):
        order = sorted(left, reverse=True)
        at = order.index(unit)
        outer, inner = 1 << at, 1 << (len(order) - at - 1)
        view = x.reshape(outer, 2, inner, *x.shape[1:])
        bit = (place // distance) % 2
        mine = lax.dynamic_index_in_dim(view, bit, 1, keepdims=False)
        other = lax.dynamic_index_in_dim(view, 1 - bit, 1, keepdims=False)
        got = lax.ppermute(other, axis, [(i, i ^ distance) for i in range(size)])
        x = (mine + got).reshape(outer * inner, *x.shape[1:])
        left.remove(unit)
    return x


def solution(mesh):
    return jax.shard_map(
        shards,
        mesh=mesh,
        in_specs=(
            P("pair", "mode", None, None),
            P(),
            P(),
            P(),
            P(),
            P("pair", None),
            P("pair", None),
        ),
        out_specs=P("mode", None, "pair"),
        check_vma=False,
    )
```

time: 564 us -> 391 us (0.69)
  waiting for transfers between devices: 364 us -> 285 us
  matrix products: 76.5 us -> 0 us
  local copies, waits for them, and re-layouts: 88.2 us -> 11.7 us
  Pallas kernels: 0 us -> 63.8 us
  starting transfers between devices: 6.7 us -> 22.4 us
  between operations: 19.9 us -> 6.09 us
  other arithmetic: 7.05 us -> 1.03 us
    dot_general x4 -> x0, matrix products: 76.5 us -> none  [the longest x1 21.2 us: shards(): lax.dot_general(e_three, arrived.reshape(arrived.shape[0], span * count),...]
    pallas_call x0 -> x6, Pallas kernels: none -> 63.8 us  [the longest x3 33 us: rotate(): pl.pallas_call(rotate_kernel, grid=(slices // block,), in_specs=[pl.Block...]
    unnamed x3 -> x0, waiting for transfers between devices: 55.4 us -> none
    convert_element_type x1 -> x0, local copies, waits for them, and re-layouts: 31.6 us -> none  [shards(): jnp.einsum('cbi,bj->cji', first, e_two, preferred_element_type=jnp.float32)]
    reduce_scatter x1 -> x0, waiting for transfers between devices: 26.8 us -> none  [shards(): reduced = lax.psum_scatter(whole, 'pair', scatter_dimension=2, tiled=True)]
    reshape x1 -> x0, local copies, waits for them, and re-layouts: 18.6 us -> none  [shards(): first = first.astype(jnp.bfloat16).reshape(slices, modes, modes)]
    ppermute x0 -> x8, waiting for transfers between devices: none -> 18.3 us  [the longest x6 15.2 us: halvings(): got = lax.ppermute(other, axis, [(i, i ^ distance) for i in range(size)])]
    all_to_all x1 -> x3, waiting for transfers between devices: 282 us -> 267 us  [shards(): lax.all_to_all(second, 'mode', split_axis=0, concat_axis=0, tiled=True)]
  transfers between devices with their start and end apart: 3 -> 11, of which waited for: 3 -> 10; matrix products, arithmetic and copies ran while one was open for 4% -> 1% of each run, Pallas kernels for 0% -> 11%
where the time goes in v1:
time: 391 us; the launch traced here: 390 us
  waiting for transfers between devices  285 us (73%)
  Pallas kernels  63.8 us (16%)
  starting transfers between devices  22.4 us (6%)
  local copies, waits for them, and re-layouts  11.7 us (3%)
  between operations  6.09 us (2%)
    all_to_all x3, waiting for transfers between devices, shards(): lax.all_to_all(second, 'mode', split_axis=0, concat_axis=0, tiled=True)  267 us
    pallas_call x3, Pallas kernels, rotate(): pl.pallas_call(rotate_kernel, grid=(slices // block,), in_specs=[pl.Block...  33 us
    pallas_call x3, Pallas kernels, gram(): pl.pallas_call(gram_kernel, grid=(span // group,), in_specs=[pl.BlockSpec...  30.9 us
    all_to_all x3, starting transfers between devices, shards(): lax.all_to_all(second, 'mode', split_axis=0, concat_axis=0, tiled=True)  15.8 us
    ppermute x6, waiting for transfers between devices, halvings(): got = lax.ppermute(other, axis, [(i, i ^ distance) for i in range(size)])  15.2 us
  transfers between devices with their start and end apart: 11, of which 10 were waited for; matrix products, arithmetic and copies ran while one was open for 1% of the time, Pallas kernels for 11%

profile of v1, /device:TPU:0, one launch (start us, length us, event | category | flops | bytes accessed | tf_op | source)
XLA Modules:
  0.0 389.9 jit_solution(5916644202381357822)
XLA Ops:
  0.0 1.4 fusion.6
  7.1 1.2 constant_dynamic-slice_fusion.12
  8.3 0.1 fusion.4
  8.4 0.2 copy.39
  8.6 11.0 %rotate.5 = bf16[384,48,128]{2,1,0:T(8,128)(2,1)S(1)} custom-call(bf16[48,384,384]{2,1,0:T(8,128)(2,1)} %bitcast.63, bf16[384,128]{1,0:T(8,128)(2,1)S(1)} %get-tuple-element.10.one_ref, bf16[384,384]{1,0:T(8,128)(2,1)S(1)} %bitcast.54), custom_call_target="tpu_custom_call" | custom-call | flops 3623878656 | bytes 18874368 | tf_op jit(solution)/shard_map/rotate/pallas_call | solution.py:45
  19.6 0.0 copy-start.2
  19.6 2.2 copy-done.2
  21.8 6.3 %all-to-all-start.2 = ((bf16[8,48,48,128]{3,2,1,0:T(8,128)(2,1)}), bf16[8,48,48,128]{3,2,1,0:T(8,128)(2,1)}, u32[]{:S(2)}, u32[]{:S(2)}) async-start(bf16[8,48,48,128]{3,2,1,0:T(8,128)(2,1)} %bitcast.53), calls=%async_computation.2 | async-start | bytes 9437184 | tf_op jit(solution)/shard_map/all_to_all | solution.py:167
  28.1 11.0 %rotate.4 = bf16[384,48,128]{2,1,0:T(8,128)(2,1)S(1)} custom-call(bf16[48,384,384]{2,1,0:T(8,128)(2,1)} %bitcast.64, bf16[384,128]{1,0:T(8,128)(2,1)S(1)} %get-tuple-element.11.one_ref, bf16[384,384]{1,0:T(8,128)(2,1)S(1)} %bitcast.55), custom_call_target="tpu_custom_call" | custom-call | flops 3623878656 | bytes 18874368 | tf_op jit(solution)/shard_map/rotate/pallas_call | solution.py:45
  39.1 0.0 copy-start.1
  39.1 2.1 copy-done.1
  41.3 92.2 %all-to-all-done.2.arr_ref = bf16[8,48,48,128]{3,2,1,0:T(8,128)(2,1)} async-done(((bf16[8,48,48,128]{3,2,1,0:T(8,128)(2,1)}), bf16[8,48,48,128]{3,2,1,0:T(8,128)(2,1)}, u32[]{:S(2)}, u32[]{:S(2)}) %all-to-all-start.2) | async-done | bytes 4718624 | tf_op jit(solution)/shard_map/all_to_all | solution.py:167
  133.5 4.6 %all-to-all-start.1 = ((bf16[8,48,48,128]{3,2,1,0:T(8,128)(2,1)}), bf16[8,48,48,128]{3,2,1,0:T(8,128)(2,1)}, u32[]{:S(2)}, u32[]{:S(2)}) async-start(bf16[8,48,48,128]{3,2,1,0:T(8,128)(2,1)} %bitcast.52), calls=%async_computation.1 | async-start | bytes 9437184 | tf_op jit(solution)/shard_map/all_to_all | solution.py:167
  138.1 11.0 %rotate.3 = bf16[384,48,128]{2,1,0:T(8,128)(2,1)S(1)} custom-call(bf16[48,384,384]{2,1,0:T(8,128)(2,1)} %bitcast.65, bf16[384,128]{1,0:T(8,128)(2,1)S(1)} %get-tuple-element.12.one_ref, bf16[384,384]{1,0:T(8,128)(2,1)S(1)} %bitcast.56), custom_call_target="tpu_custom_call" | custom-call | flops 3623878656 | bytes 18874368 | tf_op jit(solution)/shard_map/rotate/pallas_call | solution.py:45
  149.1 0.0 copy-start
  149.1 2.2 copy-done
  151.3 92.0 %all-to-all-done.1.arr_ref = bf16[8,48,48,128]{3,2,1,0:T(8,128)(2,1)} async-done(((bf16[8,48,48,128]{3,2,1,0:T(8,128)(2,1)}), bf16[8,48,48,128]{3,2,1,0:T(8,128)(2,1)}, u32[]{:S(2)}, u32[]{:S(2)}) %all-to-all-start.1) | async-done | bytes 4718624 | tf_op jit(solution)/shard_map/all_to_all | solution.py:167
  243.3 4.9 %all-to-all-start = ((bf16[8,48,48,128]{3,2,1,0:T(8,128)(2,1)}), bf16[8,48,48,128]{3,2,1,0:T(8,128)(2,1)}, u32[]{:S(2)}, u32[]{:S(2)}) async-start(bf16[8,48,48,128]{3,2,1,0:T(8,128)(2,1)} %bitcast.51), calls=%async_computation | async-start | bytes 9437184 | tf_op jit(solution)/shard_map/all_to_all | solution.py:167
  248.3 0.8 constant_dynamic-slice_fusion.8
  249.1 0.8 constant_dynamic-slice_fusion.6
  249.9 0.1 fusion.1
  250.0 0.1 copy.44
  250.1 0.2 copy.40
  250.3 0.1 broadcast_in_dim.2.old_ref
  250.4 10.3 %gram.3.old_ref = f32[2,384,384]{2,1,0:T(8,128)S(1)} custom-call(f32[1,2]{1,0:T(1,128)S(1)} %copy-done.3, bf16[8,48,48,128]{3,2,1,0:T(8,128)(2,1)} %all-to-all-done.2.arr_ref, bf16[384,384]{1,0:T(8,128)(2,1)S(1)} %bitcast.57, f32[3,128]{1,0:T(4,128)S(1)} %get-tuple-element.21.row_ref, f32[48,3]{1,0:T(8,128)S(1)} %bitcast.60, ...), custom_call_target="tpu_custom_call", output_to_operand_aliasing={{}: (5, {})} | custom-call | flops 5435817984 | bytes 7077888 | tf_op jit(solution)/shard_map/gram/pallas_call | solution.py:99
  260.7 10.3 %gram.4.old_ref = f32[2,384,384]{2,1,0:T(8,128)S(1)} custom-call(f32[1,2]{1,0:T(1,128)S(1)} %copy-done.3, bf16[8,48,48,128]{3,2,1,0:T(8,128)(2,1)} %all-to-all-done.1.arr_ref, bf16[384,384]{1,0:T(8,128)(2,1)S(1)} %bitcast.58, f32[3,128]{1,0:T(4,128)S(1)} %get-tuple-element.22.row_ref, f32[48,3]{1,0:T(8,128)S(1)} %bitcast.61, ...), custom_call_target="tpu_custom_call", output_to_operand_aliasing={{}: (5, {})} | custom-call | flops 5435817984 | bytes 7077888 | tf_op jit(solution)/shard_map/gram/pallas_call | solution.py:99
  271.0 82.3 %all-to-all-done.arr_ref = bf16[8,48,48,128]{3,2,1,0:T(8,128)(2,1)} async-done(((bf16[8,48,48,128]{3,2,1,0:T(8,128)(2,1)}), bf16[8,48,48,128]{3,2,1,0:T(8,128)(2,1)}, u32[]{:S(2)}, u32[]{:S(2)}) %all-to-all-start) | async-done | bytes 4718624 | tf_op jit(solution)/shard_map/all_to_all | solution.py:167
  353.3 10.3 %gram.5 = f32[2,384,384]{2,1,0:T(8,128)S(1)} custom-call(f32[1,2]{1,0:T(1,128)S(1)} %copy-done.3, bf16[8,48,48,128]{3,2,1,0:T(8,128)(2,1)} %all-to-all-done.arr_ref, bf16[384,384]{1,0:T(8,128)(2,1)S(1)} %bitcast.59, f32[3,128]{1,0:T(4,128)S(1)} %get-tuple-element.23.row_ref, f32[48,3]{1,0:T(8,128)S(1)} %bitcast.62, ...), custom_call_target="tpu_custom_call", output_to_operand_aliasing={{}: (5, {})} | custom-call | flops 5435817984 | bytes 7077888 | tf_op jit(solution)/shard_map/gram/pallas_call | solution.py:99
  363.7 0.1 collective-permute-start
  363.8 2.0 collective-permute-done
  365.8 0.1 bitcast_add_fusion
  365.9 1.6 collective-permute-start.1
  367.5 1.6 collective-permute-start.3
  369.1 2.8 collective-permute-done.1
  371.9 1.6 collective-permute-start.2
  373.5 0.0 collective-permute-done.3
  373.5 1.6 collective-permute-start.4
  375.1 1.2 collective-permute-done.2
  376.3 1.6 collective-permute-done.4
  378.0 0.1 copy.42
  378.1 0.1 collective-permute-start.5
  378.2 4.6 %collective-permute-done.5 = f32[2,1,2,48,96]{4,3,2,0,1:T(8,128)S(1)} collective-permute-done((f32[2,1,2,48,96]{4,3,2,0,1:T(8,128)S(1)}, f32[2,1,2,48,96]{4,3,2,0,1:T(8,128)S(1)}, u32[]{:S(2)}, u32[]{:S(2)}) %collective-permute-start.5) | collective-permute-done | bytes 73760 | tf_op jit(solution)/shard_map/ppermute | solution.py:211
  382.9 0.1 collective-permute-start.6
  383.0 5.0 %collective-permute-done.6 = f32[1,1,2,48,96]{4,3,2,0,1:T(8,128)S(1)} collective-permute-done((f32[1,1,2,48,96]{4,3,2,0,1:T(8,128)S(1)}, f32[1,1,2,48,96]{4,3,2,0,1:T(8,128)S(1)}, u32[]{:S(2)}, u32[]{:S(2)}) %collective-permute-start.6) | collective-permute-done | bytes 36896 | tf_op jit(solution)/shard_map/ppermute | solution.py:211
  387.9 0.1 collective-permute-start.7
  388.0 0.1 compare_convert_fusion
  388.1 1.1 collective-permute-done.7
  389.2 0.7 fusion
  (23 shorter events, 0.3 us)
Async XLA Ops:
  19.6 2.2 copy-start.2
  21.8 111.7 %all-to-all-start.2 = ((bf16[8,48,48,128]{3,2,1,0:T(8,128)(2,1)}), bf16[8,48,48,128]{3,2,1,0:T(8,128)(2,1)}, u32[]{:S(2)}, u32[]{:S(2)}) async-start(bf16[8,48,48,128]{3,2,1,0:T(8,128)(2,1)} %bitcast.53), calls=%async_computation.2 | async-start | bytes 9437184 | tf_op jit(solution)/shard_map/all_to_all | solution.py:167
  39.1 2.1 copy-start.1
  133.5 109.9 %all-to-all-start.1 = ((bf16[8,48,48,128]{3,2,1,0:T(8,128)(2,1)}), bf16[8,48,48,128]{3,2,1,0:T(8,128)(2,1)}, u32[]{:S(2)}, u32[]{:S(2)}) async-start(bf16[8,48,48,128]{3,2,1,0:T(8,128)(2,1)} %bitcast.52), calls=%async_computation.1 | async-start | bytes 9437184 | tf_op jit(solution)/shard_map/all_to_all | solution.py:167
  149.1 2.2 copy-start
  243.3 7.1 %copy-start.3 = (f32[1,2]{1,0:T(1,128)S(1)}, f32[1,2]{1,0:T(1,128)}, u32[]{:S(2)}) copy-start(f32[1,2]{1,0:T(1,128)} %omegas.5) | copy-start | bytes 28
  243.3 110.0 %all-to-all-start = ((bf16[8,48,48,128]{3,2,1,0:T(8,128)(2,1)}), bf16[8,48,48,128]{3,2,1,0:T(8,128)(2,1)}, u32[]{:S(2)}, u32[]{:S(2)}) async-start(bf16[8,48,48,128]{3,2,1,0:T(8,128)(2,1)} %bitcast.51), calls=%async_computation | async-start | bytes 9437184 | tf_op jit(solution)/shard_map/all_to_all | solution.py:167
  363.7 2.1 collective-permute-start
  365.9 6.0 %collective-permute-start.1 = (f32[2,1,48,384]{3,2,0,1:T(8,128)S(1)}, f32[2,1,48,384]{3,2,0,1:T(8,128)S(1)}, u32[]{:S(2)}, u32[]{:S(2)}) collective-permute-start(f32[2,1,48,384]{3,2,0,1:T(8,128)S(1)} %dynamic-slice_bitcast_fusion.3), channel_id=1, source_target_pairs={{0,8},{8,0},{16,24},{24,16},{1,9},{9,1},{17,25},{25,17},{2,10},{10... | collective-permute-start | bytes 442376 | tf_op jit(solution)/shard_map/ppermute | solution.py:211
  367.5 6.0 %collective-permute-start.3 = (f32[1,2,48,384]{3,2,1,0:T(8,128)S(1)}, f32[1,2,48,384]{3,2,1,0:T(8,128)S(1)}, u32[]{:S(2)}, u32[]{:S(2)}) collective-permute-start(f32[1,2,48,384]{3,2,1,0:T(8,128)S(1)} %dynamic-slice_bitcast_fusion.2), channel_id=1, source_target_pairs={{0,16},{8,24},{16,0},{24,8},{1,17},{9,25},{17,1},{25,9},{2,18},{10... | collective-permute-start | bytes 442376 | tf_op jit(solution)/shard_map/ppermute | solution.py:211
  371.9 4.4 %collective-permute-start.2 = (f32[1,1,48,384]{3,2,0,1:T(8,128)S(1)}, f32[1,1,48,384]{3,2,0,1:T(8,128)S(1)}, u32[]{:S(2)}, u32[]{:S(2)}) collective-permute-start(f32[1,1,48,384]{3,2,0,1:T(8,128)S(1)} %constant_dynamic-slice_fusion.4), channel_id=1, source_target_pairs={{0,16},{8,24},{16,0},{24,8},{1,17},{9,25},{17,1},{25,9},{2,18},{10... | collective-permute-start | bytes 221192 | tf_op jit(solution)/shard_map/ppermute | solution.py:211
  373.5 4.4 %collective-permute-start.4 = (f32[1,1,48,384]{3,2,1,0:T(8,128)S(1)}, f32[1,1,48,384]{3,2,1,0:T(8,128)S(1)}, u32[]{:S(2)}, u32[]{:S(2)}) collective-permute-start(f32[1,1,48,384]{3,2,1,0:T(8,128)S(1)} %constant_dynamic-slice_fusion.3), channel_id=1, source_target_pairs={{0,8},{8,0},{16,24},{24,16},{1,9},{9,1},{17,25},{25,17},{2,10},{10... | collective-permute-start | bytes 221192 | tf_op jit(solution)/shard_map/ppermute | solution.py:211
  378.1 4.7 %collective-permute-start.5 = (f32[2,1,2,48,96]{4,3,2,0,1:T(8,128)S(1)}, f32[2,1,2,48,96]{4,3,2,0,1:T(8,128)S(1)}, u32[]{:S(2)}, u32[]{:S(2)}) collective-permute-start(f32[2,1,2,48,96]{4,3,2,0,1:T(8,128)S(1)} %dynamic-slice_bitcast_fusion.4), channel_id=1, source_target_pairs={{0,2},{1,3},{2,0},{3,1},{4,6},{5,7},{6,4},{7,5},{8,10},{9,11},{10,... | collective-permute-start | bytes 221192 | tf_op jit(solution)/shard_map/ppermute | solution.py:211
  382.9 5.1 %collective-permute-start.6 = (f32[1,1,2,48,96]{4,3,2,0,1:T(8,128)S(1)}, f32[1,1,2,48,96]{4,3,2,0,1:T(8,128)S(1)}, u32[]{:S(2)}, u32[]{:S(2)}) collective-permute-start(f32[1,1,2,48,96]{4,3,2,0,1:T(8,128)S(1)} %constant_dynamic-slice_fusion.2), channel_id=1, source_target_pairs={{0,4},{1,5},{2,6},{3,7},{4,0},{5,1},{6,2},{7,3},{8,12},{9,13},{10,... | collective-permute-start | bytes 110600 | tf_op jit(solution)/shard_map/ppermute | solution.py:211
  387.9 1.3 collective-permute-start.7

commit v2 on v0

--- a/solution.py
+++ b/solution.py
@@ -1,9 +1,18 @@
+import functools
 import math
 
 import jax
 import jax.numpy as jnp
 from jax import lax
+from jax.experimental import pallas as pl
+from jax.experimental.pallas import tpu as pltpu
 from jax.sharding import PartitionSpec as P
+
+F32 = jnp.float32
+BF16 = jnp.bfloat16
+LANES = 128
+ROWS = 16
+VMEM = 48 * 2**20
 
 
 def lorentz(offset, eta):
@@ -25,7 +34,280 @@
     return jnp.stack(result)
 
 
+def weight_pair(f_one, n_one, h_one, f_two, n_two, h_two, omega):
+    total = f_two + f_one
+    differ = f_two - f_one
+    eta = 0.5 * (h_two + h_one)
+    value = (1.0 + n_one + n_two) * (lorentz(omega - total, eta) - lorentz(omega + total, eta))
+    return value + (n_one - n_two) * (lorentz(omega - differ, eta) - lorentz(omega + differ, eta))
+
+
+def rotate_kernel(parts, span, j_low, index, phi_ref, one_ref, two_ref, *rest):
+    outs, (turned_two, picked, held, turned) = rest[:parts], rest[parts:]
+    j_count = outs[0].shape[0]
+    _, block, rows, inner = phi_ref.shape
+    cols = one_ref.shape[2]
+    place = lax.axis_index("mode")
+
+    @pl.when(pl.program_id(0) == 0)
+    def _():
+        turned_two[...] = two_ref[0].T
+        for s in range(parts):
+            low = pl.multiple_of((place ^ s) * span + j_low, ROWS)
+            picked[s * j_count : (s + 1) * j_count] = turned_two[pl.ds(low, j_count)]
+
+    first = jnp.dot(phi_ref[0].reshape(block * rows, inner), one_ref[0], preferred_element_type=F32)
+    first = first.astype(BF16)
+    for c in range(block):
+        held[:, c * cols : (c + 1) * cols] = first[c * rows : (c + 1) * rows]
+    wide = jnp.dot(picked[...], held[...], preferred_element_type=F32)
+    for c in range(block):
+        turned[pl.ds(c, parts * j_count, stride=block), :] = wide[:, c * cols : (c + 1) * cols]
+    size = j_count * block
+    for s in range(parts):
+        outs[s][...] = turned[s * size : (s + 1) * size].reshape(j_count, block, cols).astype(BF16)
+
+
+def rotate(phi, eigvecs, pair_index, parts, tile, c_low, c_count, j_low, j_count):
+    _, slices, rows, inner = phi.shape
+    modes = eigvecs.shape[2]
+    first_block = c_low // ROWS
+    flops = 2 * c_count * rows * LANES * (inner + parts * j_count)
+    return pl.pallas_call(
+        functools.partial(rotate_kernel, parts, modes // parts, j_low),
+        grid_spec=pltpu.PrefetchScalarGridSpec(
+            num_scalar_prefetch=1,
+            grid=(c_count // ROWS,),
+            in_specs=[
+                pl.BlockSpec((1, ROWS, rows, inner), lambda g, index: (0, first_block + g, 0, 0)),
+                pl.BlockSpec((1, inner, LANES), lambda g, index: (index[0, 0], 0, tile)),
+                pl.BlockSpec((1, rows, modes), lambda g, index: (index[0, 1], 0, 0)),
+            ],
+            out_specs=[pl.BlockSpec((j_count, ROWS, LANES), lambda g, index: (0, g, 0))] * parts,
+            scratch_shapes=[
+                pltpu.VMEM((modes, rows), BF16),
+                pltpu.VMEM((parts * j_count, rows), BF16),
+                pltpu.VMEM((rows, ROWS * LANES), BF16),
+                pltpu.VMEM((parts * j_count * ROWS, LANES), F32),
+            ],
+        ),
+        out_shape=[jax.ShapeDtypeStruct((j_count, c_count, LANES), BF16)] * parts,
+        compiler_params=pltpu.CompilerParams(vmem_limit_bytes=VMEM),
+        cost_estimate=pl.CostEstimate(
+            flops=flops,
+            bytes_accessed=2 * c_count * (rows * inner + parts * j_count * LANES),
+            transcendentals=0,
+        ),
+        name="rotate",
+    )(pair_index, phi, eigvecs, eigvecs)
+
+
+def gram_kernel(parts, c_counts, fresh, omegas, three_ref, row_ref, col_ref, *rest):
+    pieces = len(c_counts)
+    arrived, rest = rest[: parts * pieces], rest[parts * pieces :]
+    old, (keep_ref, give_ref, side, rotated) = ((), rest) if fresh else (rest[:2], rest[2:])
+    modes = three_ref.shape[0]
+    slices = sum(c_counts)
+    group, _, cols = arrived[0].shape
+    half = modes // 2
+    span = modes // parts
+    core = lax.axis_index("mode") % 2
+
+    @pl.when(pl.program_id(0) == 0)
+    def _():
+        for at, ref in enumerate((keep_ref, give_ref)):
+            ref[...] = jnp.zeros_like(ref) if fresh else old[at][...]
+
+    for g in range(group):
+        for s in range(parts):
+            low = s * slices
+            for piece, count in enumerate(c_counts):
+                side[low : low + count, g * cols : (g + 1) * cols] = arrived[s * pieces + piece][g]
+                low += count
+    rotated[...] = jnp.dot(three_ref[...], side[...], preferred_element_type=F32).astype(BF16)
+    blocks = []
+    for order in (core, 1 - core):
+        for z in range(parts // 2):
+            low = pl.multiple_of((2 * z + order) * span, ROWS)
+            blocks.append(rotated[pl.ds(low, span)])
+    ordered = jnp.concatenate(blocks, axis=0).astype(F32)
+    for w in range(2):
+        weights = [
+            weight_pair(
+                row_ref[0:1, :], row_ref[1:2, :], row_ref[2:3, :],
+                col_ref[g : g + 1, 0:1], col_ref[g : g + 1, 1:2], col_ref[g : g + 1, 2:3],
+                omegas[0, w],
+            )
+            for g in range(group)
+        ]
+        scaled = (ordered * jnp.concatenate(weights, axis=1)).astype(BF16)
+        sums = lax.dot_general(
+            scaled, rotated[...], (((1,), (1,)), ((), ())), preferred_element_type=F32
+        )
+        keep_ref[w] += sums[:half]
+        give_ref[w] += sums[half:]
+
+
+def gram(arrived, c_counts, three, rows, cols, probes, old, tile, j_low, group):
+    parts = len(arrived)
+    pieces = [piece for one in arrived for piece in one]
+    j_count = pieces[0].shape[0]
+    modes = three.shape[0]
+    half = modes // 2
+    fresh = old is None
+    whole = pl.BlockSpec((2, half, modes), lambda g: (0, 0, 0))
+    return pl.pallas_call(
+        functools.partial(gram_kernel, parts, c_counts, fresh),
+        grid=(j_count // group,),
+        in_specs=[
+            pl.BlockSpec(memory_space=pltpu.SMEM),
+            pl.BlockSpec((modes, modes), lambda g: (0, 0)),
+            pl.BlockSpec((3, LANES), lambda g: (0, tile)),
+            pl.BlockSpec((group, 3), lambda g: (j_low // group + g, 0)),
+        ]
+        + [pl.BlockSpec((group, p.shape[1], LANES), lambda g: (g, 0, 0)) for p in pieces]
+        + ([] if fresh else [whole, whole]),
+        out_specs=[whole, whole],
+        out_shape=[jax.ShapeDtypeStruct((2, half, modes), F32)] * 2,
+        scratch_shapes=[
+            pltpu.VMEM((modes, group * LANES), BF16),
+            pltpu.VMEM((modes, group * LANES), BF16),
+        ],
+        input_output_aliases={} if fresh else {4 + len(pieces): 0, 5 + len(pieces): 1},
+        compiler_params=pltpu.CompilerParams(vmem_limit_bytes=VMEM),
+        cost_estimate=pl.CostEstimate(
+            flops=6 * modes * modes * j_count * LANES,
+            bytes_accessed=2 * modes * j_count * LANES + 16 * modes * modes,
+            transcendentals=0,
+        ),
+        name="gram",
+    )(probes, three, rows, cols, *pieces, *(() if fresh else old))
+
+
+def to_pairs_kernel(keep_ref, got_ref, *rest):
+    outs, turned = rest[:-1], rest[-1]
+    count = outs[0].shape[0]
+    modes = turned.shape[0]
+    turned[...] = (keep_ref[...] + got_ref[...]).reshape(modes, modes).T
+    place = lax.axis_index("pair")
+    for s, out in enumerate(outs):
+        out[...] = turned[pl.ds(pl.multiple_of((place ^ s) * count, 8), count)]
+
+
+def to_pairs(keep, got, pairs):
+    modes = keep.shape[2]
+    return pl.pallas_call(
+        to_pairs_kernel,
+        out_shape=[jax.ShapeDtypeStruct((modes // pairs, modes), F32)] * pairs,
+        scratch_shapes=[pltpu.VMEM((modes, modes), F32)],
+        compiler_params=pltpu.CompilerParams(vmem_limit_bytes=VMEM),
+        name="to_pairs",
+    )(keep, got)
+
+
+def to_modes_kernel(chips, *rest):
+    parts, outs, turned = rest[: -chips - 1], rest[-chips - 1 : -1], rest[-1]
+    _, span, count = outs[0].shape
+    turned[...] = sum(part[...] for part in parts).T
+    half = turned.shape[0] // 2
+    place = lax.axis_index("mode") // 2
+    for s, out in enumerate(outs):
+        low = pl.multiple_of((place ^ s) * span, 8)
+        out[0] = turned[pl.ds(low, span)]
+        out[1] = turned[pl.ds(half + low, span)]
+
+
+def to_modes(parts, chips):
+    count, modes = parts[0].shape
+    span = modes // 2 // chips
+    return pl.pallas_call(
+        functools.partial(to_modes_kernel, chips),
+        out_shape=[jax.ShapeDtypeStruct((2, span, count), F32)] * chips,
+        scratch_shapes=[pltpu.VMEM((modes, count), F32)],
+        compiler_params=pltpu.CompilerParams(vmem_limit_bytes=VMEM),
+        name="to_modes",
+    )(*parts)
+
+
+def swap(x, axis, size, distance):
+    return lax.ppermute(x, axis, [(i, i ^ distance) for i in range(size)])
+
+
+def plan(modes, slices, span):
+    whole = [(0, slices)]
+    cuts = [(0, ROWS), (ROWS, slices - ROWS)] if slices > ROWS else whole
+    blocks = [(0, cuts, 0, ROWS)]
+    if span > ROWS:
+        blocks.append((0, whole, ROWS, span - ROWS))
+    for tile in range(1, modes // LANES):
+        if tile == modes // LANES - 1 and span > ROWS:
+            blocks.append((tile, whole, 0, span - ROWS))
+            blocks.append((tile, whole, span - ROWS, ROWS))
+        else:
+            blocks.append((tile, whole, 0, span))
+    return blocks
+
+
 def shards(phi, eigvecs, freqs, occupations, smearing, probes, pair_index):
+    _, slices, modes, _ = phi.shape
+    pairs, parts = lax.axis_size("pair"), lax.axis_size("mode")
+    span = modes // parts
+    place = lax.axis_index("mode")
+    others = lax.iota(jnp.int32, parts) ^ place
+
+    def pick(table, at):
+        return lax.dynamic_index_in_dim(table, pair_index[0, at], 0, keepdims=False)
+
+    three = pick(eigvecs, 2).reshape(parts, slices, modes)[others].reshape(modes, modes).T
+    rows = jnp.stack([pick(freqs, 0), pick(occupations, 0), pick(smearing, 0)])
+    cols = jnp.stack([pick(freqs, 1), pick(occupations, 1), pick(smearing, 1)])
+    cols = lax.dynamic_slice_in_dim(cols, place * span, span, axis=1).T
+    blocks = plan(modes, slices, span)
+
+    def turn(step, after):
+        tile, cuts, j_low, j_count = blocks[step]
+        if after is None:
+            tensor = phi
+        else:
+            tensor, _ = lax.optimization_barrier((phi, after))
+        return [
+            rotate(tensor, eigvecs, pair_index, parts, tile, c_low, c_count, j_low, j_count)
+            for c_low, c_count in cuts
+        ]
+
+    far = list(range(parts // 2, parts))
+    near = list(range(1, parts // 2))
+    sums, before = None, None
+    ready = [turn(0, None), turn(1, None)]
+    for step, (tile, cuts, j_low, j_count) in enumerate(blocks):
+        arrived = [[] for _ in range(parts)]
+        arrived[0] = [piece[0] for piece in ready[step]]
+        for s in far + near:
+            for piece in ready[step]:
+                block = piece[s]
+                if before is not None:
+                    block, _ = lax.optimization_barrier((block, before[s][-1]))
+                arrived[s].append(swap(block, "mode", parts, s))
+        if step + 2 < len(blocks):
+            ready.append(turn(step + 2, [arrived[s][-1] for s in far]))
+        counts = [count for _, count in cuts]
+        sums = gram(arrived, counts, three, rows, cols, probes, sums, tile, j_low, 8)
+        before = arrived
+    keep, give = sums
+    blocks = to_pairs(keep, swap(give, "mode", parts, 1), pairs)
+    blocks = [b if s == 0 else swap(b, "pair", pairs, s) for s, b in enumerate(blocks)]
+    blocks = to_modes(blocks, parts // 2)
+    blocks = [b if s == 0 else swap(b, "mode", parts, 2 * s) for s, b in enumerate(blocks)]
+    local = jnp.transpose(sum(blocks), (1, 0, 2))
+    row_count, _, col_count = local.shape
+    row_ids = place * row_count + jnp.arange(row_count, dtype=jnp.int32)
+    col_ids = lax.axis_index("pair") * col_count + jnp.arange(col_count, dtype=jnp.int32)
+    offdiag = (row_ids[:, None] != col_ids[None, :]).astype(F32)
+    scale = 1.0 / (modes * math.sqrt(pairs))
+    return local * offdiag[:, None, :] * scale
+
+
+def shards_plain(phi, eigvecs, freqs, occupations, smearing, probes, pair_index):
     tensor = phi[0]
     slices = tensor.shape[0]
     modes = tensor.shape[1]
@@ -76,8 +358,17 @@
 
 
 def solution(mesh):
+    pairs, parts = mesh.shape["pair"], mesh.shape["mode"]
+
+    def either(phi, *rest):
+        _, slices, modes, _ = phi.shape
+        fits = slices % ROWS == 0 and modes % LANES == 0 and slices * parts == modes
+        fits = fits and parts > 1 and parts & (parts - 1) == 0 and pairs & (pairs - 1) == 0
+        fits = fits and modes % (8 * pairs) == 0
+        return (shards if fits else shards_plain)(phi, *rest)
+
     return jax.shard_map(
-        shards,
+        either,
         mesh=mesh,
         in_specs=(
             P("pair", "mode", None, None),

time: 564 us -> 366 us (0.65)
  waiting for transfers between devices: 364 us -> 149 us
  Pallas kernels: 0 us -> 93.1 us
  starting transfers between devices: 6.7 us -> 85.1 us
  matrix products: 76.5 us -> 0 us
  local copies, waits for them, and re-layouts: 88.2 us -> 29.8 us
  between operations: 19.9 us -> 6.1 us
    all_to_all x1 -> x0, waiting for transfers between devices: 282 us -> none  [shards(): lax.all_to_all(second, 'mode', split_axis=1, concat_axis=0, tiled=True)]
    ppermute x0 -> x49, waiting for transfers between devices: none -> 149 us  [swap(): return lax.ppermute(x, axis, [(i, i ^ distance) for i in range(size)])]
    pallas_call x0 -> x13, Pallas kernels: none -> 93.1 us  [the longest x6 56.8 us: rotate(): pl.pallas_call(functools.partial(rotate_kernel, parts, modes // parts, j_...]
    ppermute x0 -> x49, starting transfers between devices: none -> 85.1 us  [swap(): return lax.ppermute(x, axis, [(i, i ^ distance) for i in range(size)])]
    dot_general x4 -> x0, matrix products: 76.5 us -> none  [the longest x1 21.2 us: shards(): lax.dot_general(e_three, arrived.reshape(arrived.shape[0], span * count),...]
    unnamed x3 -> x0, waiting for transfers between devices: 55.4 us -> none
    convert_element_type x1 -> x0, local copies, waits for them, and re-layouts: 31.6 us -> none  [shards(): jnp.einsum('cbi,bj->cji', first, e_two, preferred_element_type=jnp.float32)]
    reduce_scatter x1 -> x0, waiting for transfers between devices: 26.8 us -> none  [shards(): reduced = lax.psum_scatter(whole, 'pair', scatter_dimension=2, tiled=True)]
  transfers between devices with their start and end apart: 3 -> 49, of which waited for: 3 -> 21; matrix products, arithmetic and copies ran while one was open for 4% -> 3% of each run, Pallas kernels for 0% -> 22%
where the time goes in v2:
time: 366 us; the launch traced here: 365 us
  waiting for transfers between devices  149 us (41%)
  Pallas kernels  93.1 us (25%)
  starting transfers between devices  85.1 us (23%)
  local copies, waits for them, and re-layouts  29.8 us (8%)
  between operations  6.1 us (2%)
    ppermute x49, waiting for transfers between devices, swap(): return lax.ppermute(x, axis, [(i, i ^ distance) for i in range(size)])  149 us
    ppermute x49, starting transfers between devices, swap(): return lax.ppermute(x, axis, [(i, i ^ distance) for i in range(size)])  85.1 us
    pallas_call x6, Pallas kernels, rotate(): pl.pallas_call(functools.partial(rotate_kernel, parts, modes // parts, j_...  56.8 us
    pallas_call x5, Pallas kernels, gram(): pl.pallas_call(functools.partial(gram_kernel, parts, c_counts, fresh), gr...  35.9 us
    unnamed x91, local copies, waits for them, and re-layouts  21.1 us
  transfers between devices with their start and end apart: 49, of which 21 were waited for; matrix products, arithmetic and copies ran while one was open for 3% of the time, Pallas kernels for 22%

profile of v2, /device:TPU:0, one launch (start us, length us, event | category | flops | bytes accessed | tf_op | source)
XLA Modules:
  0.0 364.8 jit_solution(18050144948363485955)
XLA Ops:
  0.0 2.0 copy-done
  2.7 7.9 %rotate.6 = (bf16[16,32,128]{2,1,0:T(8,128)(2,1)S(1)}, bf16[16,32,128]{2,1,0:T(8,128)(2,1)}, bf16[16,32,128]{2,1,0:T(8,128)(2,1)S(1)}, bf16[16,32,128]{2,1,0:T(8...) custom-call(s32[1,3]{1,0:T(1,128)S(1)} %copy-done.3, ...), custom_call_target="tpu_custom_call" | custom-call | flops 1610612736 | bytes 10485760 | tf_op jit(solution)/shard_map/rotate/pallas_call | solution.py:76
  11.2 4.5 %collective-permute-start.3 = (bf16[16,32,128]{2,1,0:T(8,128)(2,1)S(1)}, bf16[16,32,128]{2,1,0:T(8,128)(2,1)S(1)}, u32[]{:S(2)}, u32[]{:S(2)}) collective-permute-start(bf16[16,32,128]{2,1,0:T(8,128)(2,1)S(1)} %get-tuple-element.105), channel_id=1, source_target_pairs={{0,7},{1,6},{2,5},{3,4},{4,3},{5,2},{6,1},{7,0},{8,15},{9,14},{10,... | collective-permute-start | bytes 393224 | tf_op jit(solution)/shard_map/ppermute | solution.py:233
  15.7 11.2 %rotate.8 = (bf16[32,48,128]{2,1,0:T(8,128)(2,1)S(1)}, bf16[32,48,128]{2,1,0:T(8,128)(2,1)S(1)}, bf16[32,48,128]{2,1,0:T(8,128)(2,1)S(1)}, bf16[32,48,128]{2,1,0...) custom-call(s32[1,3]{1,0:T(1,128)S(1)} %copy-done.3, ...), custom_call_target="tpu_custom_call" | custom-call | flops 3019898880 | bytes 17301504 | tf_op jit(solution)/shard_map/rotate/pallas_call | solution.py:76
  29.7 1.9 collective-permute-start.1
  31.6 3.0 collective-permute-start.2
  34.6 4.9 %rotate.11 = (bf16[16,16,128]{2,1,0:T(8,128)(2,1)S(1)}, bf16[16,16,128]{2,1,0:T(8,128)(2,1)S(1)}, bf16[16,16,128]{2,1,0:T(8,128)(2,1)S(1)}, bf16[16,16,128]{2,1,...) custom-call(s32[1,3]{1,0:T(1,128)S(1)} %copy-done.3, ...), custom_call_target="tpu_custom_call" | custom-call | flops 805306368 | bytes 5242880 | tf_op jit(solution)/shard_map/rotate/pallas_call | solution.py:76
  41.8 17.6 %collective-permute-done.rest_9_ = bf16[16,32,128]{2,1,0:T(8,128)(2,1)S(1)} collective-permute-done((bf16[16,32,128]{2,1,0:T(8,128)(2,1)S(1)}, bf16[16,32,128]{2,1,0:T(8,128)(2,1)S(1)}, u32[]{:S(2)}, u32[]{:S(2)}) %collective-permute-start) | collective-permute-done | bytes 131104 | tf_op jit(solution)/shard_map/ppermute | solution.py:233
  61.7 2.6 collective-permute-start.39
  65.1 2.1 collective-permute-done.38.rest_8_
  67.2 3.0 collective-permute-done.39.rest_10_
  70.3 2.1 collective-permute-start.8
  72.4 12.6 %rotate.7 = (bf16[48,48,128]{2,1,0:T(8,128)(2,1)S(1)}, bf16[48,48,128]{2,1,0:T(8,128)(2,1)S(1)}, bf16[48,48,128]{2,1,0:T(8,128)(2,1)S(1)}, bf16[48,48,128]{2,1,0...) custom-call(s32[1,3]{1,0:T(1,128)S(1)} %copy-done.3, ...), custom_call_target="tpu_custom_call" | custom-call | flops 3623878656 | bytes 18874368 | tf_op jit(solution)/shard_map/rotate/pallas_call | solution.py:76
  87.4 2.2 collective-permute-start.11
  94.3 26.7 %collective-permute-done.4.rest_4_ = bf16[32,48,128]{2,1,0:T(8,128)(2,1)} collective-permute-done((bf16[32,48,128]{2,1,0:T(8,128)(2,1)}, bf16[32,48,128]{2,1,0:T(8,128)(2,1)}, u32[]{:S(2)}, u32[]{:S(2)}) %collective-permute-start.4) | collective-permute-done | bytes 393248 | tf_op jit(solution)/shard_map/ppermute | solution.py:233
  124.0 1.7 constant_dynamic-slice_fusion.6
  125.8 10.7 %collective-permute-done.6.rest_5_ = bf16[32,48,128]{2,1,0:T(8,128)(2,1)} collective-permute-done((bf16[32,48,128]{2,1,0:T(8,128)(2,1)}, bf16[32,48,128]{2,1,0:T(8,128)(2,1)}, u32[]{:S(2)}, u32[]{:S(2)}) %collective-permute-start.6) | collective-permute-done | bytes 393248 | tf_op jit(solution)/shard_map/ppermute | solution.py:233
  136.5 2.3 collective-permute-start.9
  141.3 3.0 collective-permute-start.41
  145.0 10.9 %collective-permute-done.40.rest_12_ = bf16[16,16,128]{2,1,0:T(8,128)(2,1)S(1)} collective-permute-done((bf16[16,16,128]{2,1,0:T(8,128)(2,1)}, bf16[16,16,128]{2,1,0:T(8,128)(2,1)S(1)}, u32[]{:S(2)}, u32[]{:S(2)}) %collective-permute-start.40) | collective-permute-done | bytes 65568 | tf_op jit(solution)/shard_map/ppermute | solution.py:233
  156.5 23.8 %collective-permute-start.7 = (bf16[48,48,128]{2,1,0:T(8,128)(2,1)}, bf16[48,48,128]{2,1,0:T(8,128)(2,1)}, u32[]{:S(2)}, u32[]{:S(2)}) collective-permute-start(bf16[48,48,128]{2,1,0:T(8,128)(2,1)} %get-tuple-element.114), channel_id=1, source_target_pairs={{0,5},{1,4},{2,7},{3,6},{4,1},{5,0},{6,3},{7,2},{8,13},{9,12},{10,... | collective-permute-start | bytes 1769480 | tf_op jit(solution)/shard_map/ppermute | solution.py:233
  180.9 1.6 collective-permute-start.5
  184.3 2.4 gather_fusion
  201.6 4.4 %gram.5 = (f32[2,192,384]{2,1,0:T(8,128)S(1)}, f32[2,192,384]{2,1,0:T(8,128)S(1)}) custom-call(f32[1,2]{1,0:T(1,128)S(1)} %copy-done.44, bf16[384,384]{1,0:T(8,128)(2,1)S(1)} %bitcast.11, f32[3,384]{1,0:T(4,128)S(1)} %pad_maximum_fusion.row_ref, f32[48,3]{1,0:T(8,128)S(1)} %bitcast.16, bf16[16,16,128]{2,1,0:T(8,128)(2,1)S(1)} %copy-done.27, ...), custom_call_target="tpu_custom_call" | custom-call | flops 1811939328 | bytes 3932160 | tf_op jit(solution)/shard_map/gram/pallas_call | solution.py:159
  206.6 10.5 %rotate.10 = (bf16[32,48,128]{2,1,0:T(8,128)(2,1)S(1)}, bf16[32,48,128]{2,1,0:T(8,128)(2,1)S(1)}, bf16[32,48,128]{2,1,0:T(8,128)(2,1)S(1)}, bf16[32,48,128]{2,1,...) custom-call(s32[1,3]{1,0:T(1,128)S(1)} %copy-done.4, ...), custom_call_target="tpu_custom_call" | custom-call | flops 3019898880 | bytes 17301504 | tf_op jit(solution)/shard_map/rotate/pallas_call | solution.py:76
  217.9 4.9 %collective-permute-start.33 = (bf16[32,48,128]{2,1,0:T(8,128)(2,1)S(1)}, bf16[32,48,128]{2,1,0:T(8,128)(2,1)S(1)}, u32[]{:S(2)}, u32[]{:S(2)}) collective-permute-start(bf16[32,48,128]{2,1,0:T(8,128)(2,1)S(1)} %get-tuple-element.167), channel_id=1, source_target_pairs={{0,7},{1,6},{2,5},{3,4},{4,3},{5,2},{6,1},{7,0},{8,15},{9,14},{10,... | collective-permute-start | bytes 1179656 | tf_op jit(solution)/shard_map/ppermute | solution.py:233
  222.8 28.5 %collective-permute-done.5.rest_4_ = bf16[48,48,128]{2,1,0:T(8,128)(2,1)} collective-permute-done((bf16[48,48,128]{2,1,0:T(8,128)(2,1)S(1)}, bf16[48,48,128]{2,1,0:T(8,128)(2,1)}, u32[]{:S(2)}, u32[]{:S(2)}) %collective-permute-start.5) | collective-permute-done | bytes 589856 | tf_op jit(solution)/shard_map/ppermute | solution.py:233
  251.4 8.3 %gram.6 = (f32[2,192,384]{2,1,0:T(8,128)S(1)}, f32[2,192,384]{2,1,0:T(8,128)S(1)}) custom-call(f32[1,2]{1,0:T(1,128)S(1)} %copy-done.44, bf16[384,384]{1,0:T(8,128)(2,1)S(1)} %bitcast.12, f32[3,384]{1,0:T(4,128)S(1)} %pad_maximum_fusion.row_ref, f32[48,3]{1,0:T(8,128)S(1)} %bitcast.17, ...), custom_call_target="tpu_custom_call", output_to_operand_aliasing={{0}: (12, {}), {1}: (13, {})} | custom-call | flops 3623878656 | bytes 5505024 | tf_op jit(solution)/shard_map/gram/pallas_call | solution.py:159
  259.8 4.1 %collective-permute-start.25 = (bf16[32,48,128]{2,1,0:T(8,128)(2,1)S(1)}, bf16[32,48,128]{2,1,0:T(8,128)(2,1)S(1)}, u32[]{:S(2)}, u32[]{:S(2)}) collective-permute-start(bf16[32,48,128]{2,1,0:T(8,128)(2,1)S(1)} %get-tuple-element.151), channel_id=1, source_target_pairs={{0,3},{1,2},{2,1},{3,0},{4,7},{5,6},{6,5},{7,4},{8,11},{9,10},{10,... | collective-permute-start | bytes 1179656 | tf_op jit(solution)/shard_map/ppermute | solution.py:233
  263.8 9.7 %rotate.9 = (bf16[16,48,128]{2,1,0:T(8,128)(2,1)S(1)}, bf16[16,48,128]{2,1,0:T(8,128)(2,1)S(1)}, bf16[16,48,128]{2,1,0:T(8,128)(2,1)S(1)}, bf16[16,48,128]{2,1,0...) custom-call(s32[1,3]{1,0:T(1,128)S(1)} %copy-done.4, ...), custom_call_target="tpu_custom_call" | custom-call | flops 2415919104 | bytes 15728640 | tf_op jit(solution)/shard_map/rotate/pallas_call | solution.py:76
  274.6 14.9 %collective-permute-done.29.rest_5_ = bf16[32,48,128]{2,1,0:T(8,128)(2,1)S(1)} collective-permute-done((bf16[32,48,128]{2,1,0:T(8,128)(2,1)S(1)}, bf16[32,48,128]{2,1,0:T(8,128)(2,1)S(1)}, u32[]{:S(2)}, u32[]{:S(2)}) %collective-permute-start.29) | collective-permute-done | bytes 393248 | tf_op jit(solution)/shard_map/ppermute | solution.py:233
  289.5 4.9 %collective-permute-start.34 = (bf16[16,48,128]{2,1,0:T(8,128)(2,1)S(1)}, bf16[16,48,128]{2,1,0:T(8,128)(2,1)S(1)}, u32[]{:S(2)}, u32[]{:S(2)}) collective-permute-start(bf16[16,48,128]{2,1,0:T(8,128)(2,1)S(1)} %get-tuple-element.168), channel_id=1, source_target_pairs={{0,7},{1,6},{2,5},{3,4},{4,3},{5,2},{6,1},{7,0},{8,15},{9,14},{10,... | collective-permute-start | bytes 589832 | tf_op jit(solution)/shard_map/ppermute | solution.py:233
  294.4 11.6 %collective-permute-done.27.rest_4_ = bf16[32,48,128]{2,1,0:T(8,128)(2,1)S(1)} collective-permute-done((bf16[32,48,128]{2,1,0:T(8,128)(2,1)S(1)}, bf16[32,48,128]{2,1,0:T(8,128)(2,1)S(1)}, u32[]{:S(2)}, u32[]{:S(2)}) %collective-permute-start.27) | collective-permute-done | bytes 393248 | tf_op jit(solution)/shard_map/ppermute | solution.py:233
  306.0 1.5 collective-permute-start.32
  307.5 11.6 %gram.7 = (f32[2,192,384]{2,1,0:T(8,128)S(1)}, f32[2,192,384]{2,1,0:T(8,128)S(1)}) custom-call(f32[1,2]{1,0:T(1,128)S(1)} %copy-done.44, bf16[384,384]{1,0:T(8,128)(2,1)S(1)} %bitcast.13, f32[3,384]{1,0:T(4,128)S(1)} %pad_maximum_fusion.row_ref, f32[48,3]{1,0:T(8,128)S(1)} %bitcast.18, ...), custom_call_target="tpu_custom_call", output_to_operand_aliasing={{0}: (12, {}), {1}: (13, {})} | custom-call | flops 5435817984 | bytes 7077888 | tf_op jit(solution)/shard_map/gram/pallas_call | solution.py:159
  319.4 2.5 collective-permute-start.26
  321.9 1.8 collective-permute-start.21
  323.7 7.5 %gram.8 = (f32[2,192,384]{2,1,0:T(8,128)S(1)}, f32[2,192,384]{2,1,0:T(8,128)S(1)}) custom-call(f32[1,2]{1,0:T(1,128)S(1)} %copy-done.44, bf16[384,384]{1,0:T(8,128)(2,1)S(1)} %bitcast.14, f32[3,384]{1,0:T(4,128)S(1)} %pad_maximum_fusion.row_ref, f32[48,3]{1,0:T(8,128)S(1)} %bitcast.19, ...), custom_call_target="tpu_custom_call", output_to_operand_aliasing={{0}: (12, {}), {1}: (13, {})} | custom-call | flops 3623878656 | bytes 5505024 | tf_op jit(solution)/shard_map/gram/pallas_call | solution.py:159
  331.2 2.9 collective-permute-done.30.rest_5_
  334.5 3.6 %collective-permute-done.21.rest_2_ = bf16[16,48,128]{2,1,0:T(8,128)(2,1)S(1)} collective-permute-done((bf16[16,48,128]{2,1,0:T(8,128)(2,1)S(1)}, bf16[16,48,128]{2,1,0:T(8,128)(2,1)S(1)}, u32[]{:S(2)}, u32[]{:S(2)}) %collective-permute-start.21) | collective-permute-done | bytes 196640 | tf_op jit(solution)/shard_map/ppermute | solution.py:233
  338.2 4.1 %gram.9 = (f32[2,192,384]{2,1,0:T(8,128)S(1)}, f32[2,192,384]{2,1,0:T(8,128)S(1)}) custom-call(f32[1,2]{1,0:T(1,128)S(1)} %copy-done.44, bf16[384,384]{1,0:T(8,128)(2,1)S(1)} %bitcast.15, f32[3,384]{1,0:T(4,128)S(1)} %pad_maximum_fusion.row_ref, f32[48,3]{1,0:T(8,128)S(1)} %bitcast.20, ...), custom_call_target="tpu_custom_call", output_to_operand_aliasing={{0}: (12, {}), {1}: (13, {})} | custom-call | flops 1811939328 | bytes 3932160 | tf_op jit(solution)/shard_map/gram/pallas_call | solution.py:159
  342.4 2.0 collective-permute-done.42.got_ref
  344.6 1.6 collective-permute-start.43
  346.2 1.5 collective-permute-start.44
  348.2 3.1 collective-permute-done.43.rest_1_
  351.3 3.7 %collective-permute-done.44.rest_2_ = f32[96,384]{1,0:T(8,128)S(1)} collective-permute-done((f32[96,384]{1,0:T(8,128)S(1)}, f32[96,384]{1,0:T(8,128)S(1)}, u32[]{:S(2)}, u32[]{:S(2)}) %collective-permute-start.44) | collective-permute-done | bytes 147488 | tf_op jit(solution)/shard_map/ppermute | solution.py:233
  355.2 3.0 collective-permute-start.47
  360.7 3.4 collective-permute-done.48
  (169 shorter events, 42.5 us)
Async XLA Ops:
  11.2 16.5 %collective-permute-start.3 = (bf16[16,32,128]{2,1,0:T(8,128)(2,1)S(1)}, bf16[16,32,128]{2,1,0:T(8,128)(2,1)S(1)}, u32[]{:S(2)}, u32[]{:S(2)}) collective-permute-start(bf16[16,32,128]{2,1,0:T(8,128)(2,1)S(1)} %get-tuple-element.105), channel_id=1, source_target_pairs={{0,7},{1,6},{2,5},{3,4},{4,3},{5,2},{6,1},{7,0},{8,15},{9,14},{10,... | collective-permute-start | bytes 393224 | tf_op jit(solution)/shard_map/ppermute | solution.py:233
  28.4 41.9 %collective-permute-start.10 = (bf16[32,48,128]{2,1,0:T(8,128)(2,1)S(1)}, bf16[32,48,128]{2,1,0:T(8,128)(2,1)S(1)}, u32[]{:S(2)}, u32[]{:S(2)}) collective-permute-start(bf16[32,48,128]{2,1,0:T(8,128)(2,1)S(1)} %get-tuple-element.121), channel_id=1, source_target_pairs={{0,7},{1,6},{2,5},{3,4},{4,3},{5,2},{6,1},{7,0},{8,15},{9,14},{10,... | collective-permute-start | bytes 1179656 | tf_op jit(solution)/shard_map/ppermute | solution.py:233
  28.7 30.6 %collective-permute-start = (bf16[16,32,128]{2,1,0:T(8,128)(2,1)S(1)}, bf16[16,32,128]{2,1,0:T(8,128)(2,1)S(1)}, u32[]{:S(2)}, u32[]{:S(2)}) collective-permute-start(bf16[16,32,128]{2,1,0:T(8,128)(2,1)S(1)} %get-tuple-element.102), channel_id=1, source_target_pairs={{0,4},{1,5},{2,6},{3,7},{4,0},{5,1},{6,2},{7,3},{8,12},{9,13},{10,... | collective-permute-start | bytes 393224 | tf_op jit(solution)/shard_map/ppermute | solution.py:233
  29.7 30.7 %collective-permute-start.1 = (bf16[16,32,128]{2,1,0:T(8,128)(2,1)S(1)}, bf16[16,32,128]{2,1,0:T(8,128)(2,1)S(1)}, u32[]{:S(2)}, u32[]{:S(2)}) collective-permute-start(bf16[16,32,128]{2,1,0:T(8,128)(2,1)S(1)} %get-tuple-element.103), channel_id=1, source_target_pairs={{0,5},{1,4},{2,7},{3,6},{4,1},{5,0},{6,3},{7,2},{8,13},{9,12},{10,... | collective-permute-start | bytes 393224 | tf_op jit(solution)/shard_map/ppermute | solution.py:233
  31.6 30.0 %collective-permute-start.2 = (bf16[16,32,128]{2,1,0:T(8,128)(2,1)S(1)}, bf16[16,32,128]{2,1,0:T(8,128)(2,1)S(1)}, u32[]{:S(2)}, u32[]{:S(2)}) collective-permute-start(bf16[16,32,128]{2,1,0:T(8,128)(2,1)S(1)} %get-tuple-element.104), channel_id=1, source_target_pairs={{0,6},{1,7},{2,4},{3,5},{4,2},{5,3},{6,0},{7,1},{8,14},{9,15},{10,... | collective-permute-start | bytes 393224 | tf_op jit(solution)/shard_map/ppermute | solution.py:233
  41.8 22.5 %collective-permute-start.36 = (bf16[16,16,128]{2,1,0:T(8,128)(2,1)S(1)}, bf16[16,16,128]{2,1,0:T(8,128)(2,1)S(1)}, u32[]{:S(2)}, u32[]{:S(2)}) collective-permute-start(bf16[16,16,128]{2,1,0:T(8,128)(2,1)S(1)} %get-tuple-element.175), channel_id=1, source_target_pairs={{0,2},{1,3},{2,0},{3,1},{4,6},{5,7},{6,4},{7,5},{8,10},{9,11},{10,... | collective-permute-start | bytes 196616 | tf_op jit(solution)/shard_map/ppermute | solution.py:233
  59.3 5.8 %collective-permute-start.37 = (bf16[16,16,128]{2,1,0:T(8,128)(2,1)S(1)}, bf16[16,16,128]{2,1,0:T(8,128)(2,1)S(1)}, u32[]{:S(2)}, u32[]{:S(2)}) collective-permute-start(bf16[16,16,128]{2,1,0:T(8,128)(2,1)S(1)} %get-tuple-element.176), channel_id=1, source_target_pairs={{0,3},{1,2},{2,1},{3,0},{4,7},{5,6},{6,5},{7,4},{8,11},{9,10},{10,... | collective-permute-start | bytes 196616 | tf_op jit(solution)/shard_map/ppermute | solution.py:233
  60.5 6.7 %collective-permute-start.38 = (bf16[16,16,128]{2,1,0:T(8,128)(2,1)S(1)}, bf16[16,16,128]{2,1,0:T(8,128)(2,1)S(1)}, u32[]{:S(2)}, u32[]{:S(2)}) collective-permute-start(bf16[16,16,128]{2,1,0:T(8,128)(2,1)S(1)} %get-tuple-element.177), channel_id=1, source_target_pairs={{0,4},{1,5},{2,6},{3,7},{4,0},{5,1},{6,2},{7,3},{8,12},{9,13},{10,... | collective-permute-start | bytes 196616 | tf_op jit(solution)/shard_map/ppermute | solution.py:233
  61.7 8.4 %collective-permute-start.39 = (bf16[16,16,128]{2,1,0:T(8,128)(2,1)S(1)}, bf16[16,16,128]{2,1,0:T(8,128)(2,1)S(1)}, u32[]{:S(2)}, u32[]{:S(2)}) collective-permute-start(bf16[16,16,128]{2,1,0:T(8,128)(2,1)S(1)} %get-tuple-element.178), channel_id=1, source_target_pairs={{0,5},{1,4},{2,7},{3,6},{4,1},{5,0},{6,3},{7,2},{8,13},{9,12},{10,... | collective-permute-start | bytes 196616 | tf_op jit(solution)/shard_map/ppermute | solution.py:233
  64.3 30.0 %collective-permute-start.12 = (bf16[16,32,128]{2,1,0:T(8,128)(2,1)}, bf16[16,32,128]{2,1,0:T(8,128)(2,1)}, u32[]{:S(2)}, u32[]{:S(2)}) collective-permute-start(bf16[16,32,128]{2,1,0:T(8,128)(2,1)} %get-tuple-element.130), channel_id=1, source_target_pairs={{0,1},{1,0},{2,3},{3,2},{4,5},{5,4},{6,7},{7,6},{8,9},{9,8},{10,11... | collective-permute-start | bytes 393224 | tf_op jit(solution)/shard_map/ppermute | solution.py:233
  65.1 20.0 %collective-permute-start.17 = (bf16[16,32,128]{2,1,0:T(8,128)(2,1)S(1)}, bf16[16,32,128]{2,1,0:T(8,128)(2,1)S(1)}, u32[]{:S(2)}, u32[]{:S(2)}) collective-permute-start(bf16[16,32,128]{2,1,0:T(8,128)(2,1)S(1)} %get-tuple-element.139), channel_id=1, source_target_pairs={{0,2},{1,3},{2,0},{3,1},{4,6},{5,7},{6,4},{7,5},{8,10},{9,11},{10,... | collective-permute-start | bytes 393224 | tf_op jit(solution)/shard_map/ppermute | solution.py:233
  67.2 19.6 %collective-permute-start.22 = (bf16[16,32,128]{2,1,0:T(8,128)(2,1)S(1)}, bf16[16,32,128]{2,1,0:T(8,128)(2,1)S(1)}, u32[]{:S(2)}, u32[]{:S(2)}) collective-permute-start(bf16[16,32,128]{2,1,0:T(8,128)(2,1)S(1)} %get-tuple-element.148), channel_id=1, source_target_pairs={{0,3},{1,2},{2,1},{3,0},{4,7},{5,6},{6,5},{7,4},{8,11},{9,10},{10,... | collective-permute-start | bytes 393224 | tf_op jit(solution)/shard_map/ppermute | solution.py:233
  70.1 50.9 %collective-permute-start.4 = (bf16[32,48,128]{2,1,0:T(8,128)(2,1)}, bf16[32,48,128]{2,1,0:T(8,128)(2,1)}, u32[]{:S(2)}, u32[]{:S(2)}) collective-permute-start(bf16[32,48,128]{2,1,0:T(8,128)(2,1)} %get-tuple-element.109), channel_id=1, source_target_pairs={{0,4},{1,5},{2,6},{3,7},{4,0},{5,1},{6,2},{7,3},{8,12},{9,13},{10,... | collective-permute-start | bytes 1179656 | tf_op jit(solution)/shard_map/ppermute | solution.py:233
  70.3 52.1 %collective-permute-start.8 = (bf16[32,48,128]{2,1,0:T(8,128)(2,1)}, bf16[32,48,128]{2,1,0:T(8,128)(2,1)}, u32[]{:S(2)}, u32[]{:S(2)}) collective-permute-start(bf16[32,48,128]{2,1,0:T(8,128)(2,1)} %get-tuple-element.117), channel_id=1, source_target_pairs={{0,6},{1,7},{2,4},{3,5},{4,2},{5,3},{6,0},{7,1},{8,14},{9,15},{10,... | collective-permute-start | bytes 1179656 | tf_op jit(solution)/shard_map/ppermute | solution.py:233
  85.7 50.7 %collective-permute-start.6 = (bf16[32,48,128]{2,1,0:T(8,128)(2,1)}, bf16[32,48,128]{2,1,0:T(8,128)(2,1)}, u32[]{:S(2)}, u32[]{:S(2)}) collective-permute-start(bf16[32,48,128]{2,1,0:T(8,128)(2,1)} %get-tuple-element.113), channel_id=1, source_target_pairs={{0,5},{1,4},{2,7},{3,6},{4,1},{5,0},{6,3},{7,2},{8,13},{9,12},{10,... | collective-permute-start | bytes 1179656 | tf_op jit(solution)/shard_map/ppermute | solution.py:233
  87.4 95.6 %collective-permute-start.11 = (bf16[48,48,128]{2,1,0:T(8,128)(2,1)S(1)}, bf16[48,48,128]{2,1,0:T(8,128)(2,1)}, u32[]{:S(2)}, u32[]{:S(2)}) collective-permute-start(bf16[48,48,128]{2,1,0:T(8,128)(2,1)S(1)} %get-tuple-element.122), channel_id=1, source_target_pairs={{0,7},{1,6},{2,5},{3,4},{4,3},{5,2},{6,1},{7,0},{8,15},{9,14},{10,... | collective-permute-start | bytes 1769480 | tf_op jit(solution)/shard_map/ppermute | solution.py:233
  94.3 45.1 %collective-permute-start.18 = (bf16[32,48,128]{2,1,0:T(8,128)(2,1)}, bf16[32,48,128]{2,1,0:T(8,128)(2,1)}, u32[]{:S(2)}, u32[]{:S(2)}) collective-permute-start(bf16[32,48,128]{2,1,0:T(8,128)(2,1)} %copy-done.11), channel_id=1, source_target_pairs={{0,2},{1,3},{2,0},{3,1},{4,6},{5,7},{6,4},{7,5},{8,10},{9,11},{10,... | collective-permute-start | bytes 1179656 | tf_op jit(solution)/shard_map/ppermute | solution.py:233
  121.0 20.2 %collective-permute-start.23 = (bf16[32,48,128]{2,1,0:T(8,128)(2,1)}, bf16[32,48,128]{2,1,0:T(8,128)(2,1)}, u32[]{:S(2)}, u32[]{:S(2)}) collective-permute-start(bf16[32,48,128]{2,1,0:T(8,128)(2,1)} %copy-done.10), channel_id=1, source_target_pairs={{0,3},{1,2},{2,1},{3,0},{4,7},{5,6},{6,5},{7,4},{8,11},{9,10},{10,... | collective-permute-start | bytes 1179656 | tf_op jit(solution)/shard_map/ppermute | solution.py:233
  122.4 60.2 %collective-permute-start.13 = (bf16[32,48,128]{2,1,0:T(8,128)(2,1)}, bf16[32,48,128]{2,1,0:T(8,128)(2,1)}, u32[]{:S(2)}, u32[]{:S(2)}) collective-permute-start(bf16[32,48,128]{2,1,0:T(8,128)(2,1)} %copy-done.9), channel_id=1, source_target_pairs={{0,1},{1,0},{2,3},{3,2},{4,5},{5,4},{6,7},{7,6},{8,9},{9,8},{10,11... | collective-permute-start | bytes 1179656 | tf_op jit(solution)/shard_map/ppermute | solution.py:233
  136.5 69.5 %collective-permute-start.9 = (bf16[48,48,128]{2,1,0:T(8,128)(2,1)}, bf16[48,48,128]{2,1,0:T(8,128)(2,1)}, u32[]{:S(2)}, u32[]{:S(2)}) collective-permute-start(bf16[48,48,128]{2,1,0:T(8,128)(2,1)} %get-tuple-element.118), channel_id=1, source_target_pairs={{0,6},{1,7},{2,4},{3,5},{4,2},{5,3},{6,0},{7,1},{8,14},{9,15},{10,... | collective-permute-start | bytes 1769480 | tf_op jit(solution)/shard_map/ppermute | solution.py:233
  139.4 16.5 %collective-permute-start.40 = (bf16[16,16,128]{2,1,0:T(8,128)(2,1)}, bf16[16,16,128]{2,1,0:T(8,128)(2,1)S(1)}, u32[]{:S(2)}, u32[]{:S(2)}) collective-permute-start(bf16[16,16,128]{2,1,0:T(8,128)(2,1)} %copy-done.39), channel_id=1, source_target_pairs={{0,6},{1,7},{2,4},{3,5},{4,2},{5,3},{6,0},{7,1},{8,14},{9,15},{10,... | collective-permute-start | bytes 196616 | tf_op jit(solution)/shard_map/ppermute | solution.py:233
  141.3 39.1 %collective-permute-start.41 = (bf16[16,16,128]{2,1,0:T(8,128)(2,1)}, bf16[16,16,128]{2,1,0:T(8,128)(2,1)S(1)}, u32[]{:S(2)}, u32[]{:S(2)}) collective-permute-start(bf16[16,16,128]{2,1,0:T(8,128)(2,1)} %copy-done.38), channel_id=1, source_target_pairs={{0,7},{1,6},{2,5},{3,4},{4,3},{5,2},{6,1},{7,0},{8,15},{9,14},{10,... | collective-permute-start | bytes 196616 | tf_op jit(solution)/shard_map/ppermute | solution.py:233
  156.5 61.4 %collective-permute-start.7 = (bf16[48,48,128]{2,1,0:T(8,128)(2,1)}, bf16[48,48,128]{2,1,0:T(8,128)(2,1)}, u32[]{:S(2)}, u32[]{:S(2)}) collective-permute-start(bf16[48,48,128]{2,1,0:T(8,128)(2,1)} %get-tuple-element.114), channel_id=1, source_target_pairs={{0,5},{1,4},{2,7},{3,6},{4,1},{5,0},{6,3},{7,2},{8,13},{9,12},{10,... | collective-permute-start | bytes 1769480 | tf_op jit(solution)/shard_map/ppermute | solution.py:233
  180.9 70.3 %collective-permute-start.5 = (bf16[48,48,128]{2,1,0:T(8,128)(2,1)S(1)}, bf16[48,48,128]{2,1,0:T(8,128)(2,1)}, u32[]{:S(2)}, u32[]{:S(2)}) collective-permute-start(bf16[48,48,128]{2,1,0:T(8,128)(2,1)S(1)} %get-tuple-element.110), channel_id=1, source_target_pairs={{0,4},{1,5},{2,6},{3,7},{4,0},{5,1},{6,2},{7,3},{8,12},{9,13},{10,... | collective-permute-start | bytes 1769480 | tf_op jit(solution)/shard_map/ppermute | solution.py:233
  182.5 68.7 %collective-permute-start.19 = (bf16[48,48,128]{2,1,0:T(8,128)(2,1)S(1)}, bf16[48,48,128]{2,1,0:T(8,128)(2,1)}, u32[]{:S(2)}, u32[]{:S(2)}) collective-permute-start(bf16[48,48,128]{2,1,0:T(8,128)(2,1)S(1)} %get-tuple-element.141), channel_id=1, source_target_pairs={{0,2},{1,3},{2,0},{3,1},{4,6},{5,7},{6,4},{7,5},{8,10},{9,11},{10,... | collective-permute-start | bytes 1769480 | tf_op jit(solution)/shard_map/ppermute | solution.py:233
  183.0 68.3 %collective-permute-start.24 = (bf16[48,48,128]{2,1,0:T(8,128)(2,1)S(1)}, bf16[48,48,128]{2,1,0:T(8,128)(2,1)}, u32[]{:S(2)}, u32[]{:S(2)}) collective-permute-start(bf16[48,48,128]{2,1,0:T(8,128)(2,1)S(1)} %get-tuple-element.150), channel_id=1, source_target_pairs={{0,3},{1,2},{2,1},{3,0},{4,7},{5,6},{6,5},{7,4},{8,11},{9,10},{10,... | collective-permute-start | bytes 1769480 | tf_op jit(solution)/shard_map/ppermute | solution.py:233
  206.0 53.7 %collective-permute-start.14 = (bf16[48,48,128]{2,1,0:T(8,128)(2,1)S(1)}, bf16[48,48,128]{2,1,0:T(8,128)(2,1)S(1)}, u32[]{:S(2)}, u32[]{:S(2)}) collective-permute-start(bf16[48,48,128]{2,1,0:T(8,128)(2,1)S(1)} %get-tuple-element.132), channel_id=1, source_target_pairs={{0,1},{1,0},{2,3},{3,2},{4,5},{5,4},{6,7},{7,6},{8,9},{9,8},{10,11... | collective-permute-start | bytes 1769480 | tf_op jit(solution)/shard_map/ppermute | solution.py:233
  217.9 55.6 %collective-permute-start.33 = (bf16[32,48,128]{2,1,0:T(8,128)(2,1)S(1)}, bf16[32,48,128]{2,1,0:T(8,128)(2,1)S(1)}, u32[]{:S(2)}, u32[]{:S(2)}) collective-permute-start(bf16[32,48,128]{2,1,0:T(8,128)(2,1)S(1)} %get-tuple-element.167), channel_id=1, source_target_pairs={{0,7},{1,6},{2,5},{3,4},{4,3},{5,2},{6,1},{7,0},{8,15},{9,14},{10,... | collective-permute-start | bytes 1179656 | tf_op jit(solution)/shard_map/ppermute | solution.py:233
  251.3 23.3 %collective-permute-start.31 = (bf16[32,48,128]{2,1,0:T(8,128)(2,1)S(1)}, bf16[32,48,128]{2,1,0:T(8,128)(2,1)S(1)}, u32[]{:S(2)}, u32[]{:S(2)}) collective-permute-start(bf16[32,48,128]{2,1,0:T(8,128)(2,1)S(1)} %get-tuple-element.163), channel_id=1, source_target_pairs={{0,6},{1,7},{2,4},{3,5},{4,2},{5,3},{6,0},{7,1},{8,14},{9,15},{10,... | collective-permute-start | bytes 1179656 | tf_op jit(solution)/shard_map/ppermute | solution.py:233
  251.3 38.2 %collective-permute-start.29 = (bf16[32,48,128]{2,1,0:T(8,128)(2,1)S(1)}, bf16[32,48,128]{2,1,0:T(8,128)(2,1)S(1)}, u32[]{:S(2)}, u32[]{:S(2)}) collective-permute-start(bf16[32,48,128]{2,1,0:T(8,128)(2,1)S(1)} %get-tuple-element.159), channel_id=1, source_target_pairs={{0,5},{1,4},{2,7},{3,6},{4,1},{5,0},{6,3},{7,2},{8,13},{9,12},{10,... | collective-permute-start | bytes 1179656 | tf_op jit(solution)/shard_map/ppermute | solution.py:233
  251.3 54.7 %collective-permute-start.27 = (bf16[32,48,128]{2,1,0:T(8,128)(2,1)S(1)}, bf16[32,48,128]{2,1,0:T(8,128)(2,1)S(1)}, u32[]{:S(2)}, u32[]{:S(2)}) collective-permute-start(bf16[32,48,128]{2,1,0:T(8,128)(2,1)S(1)} %get-tuple-element.155), channel_id=1, source_target_pairs={{0,4},{1,5},{2,6},{3,7},{4,0},{5,1},{6,2},{7,3},{8,12},{9,13},{10,... | collective-permute-start | bytes 1179656 | tf_op jit(solution)/shard_map/ppermute | solution.py:233
  259.8 59.4 %collective-permute-start.25 = (bf16[32,48,128]{2,1,0:T(8,128)(2,1)S(1)}, bf16[32,48,128]{2,1,0:T(8,128)(2,1)S(1)}, u32[]{:S(2)}, u32[]{:S(2)}) collective-permute-start(bf16[32,48,128]{2,1,0:T(8,128)(2,1)S(1)} %get-tuple-element.151), channel_id=1, source_target_pairs={{0,3},{1,2},{2,1},{3,0},{4,7},{5,6},{6,5},{7,4},{8,11},{9,10},{10,... | collective-permute-start | bytes 1179656 | tf_op jit(solution)/shard_map/ppermute | solution.py:233
  273.5 45.7 %collective-permute-start.20 = (bf16[32,48,128]{2,1,0:T(8,128)(2,1)S(1)}, bf16[32,48,128]{2,1,0:T(8,128)(2,1)S(1)}, u32[]{:S(2)}, u32[]{:S(2)}) collective-permute-start(bf16[32,48,128]{2,1,0:T(8,128)(2,1)S(1)} %get-tuple-element.142), channel_id=1, source_target_pairs={{0,2},{1,3},{2,0},{3,1},{4,6},{5,7},{6,4},{7,5},{8,10},{9,11},{10,... | collective-permute-start | bytes 1179656 | tf_op jit(solution)/shard_map/ppermute | solution.py:233
  274.6 44.8 %collective-permute-start.15 = (bf16[32,48,128]{2,1,0:T(8,128)(2,1)S(1)}, bf16[32,48,128]{2,1,0:T(8,128)(2,1)S(1)}, u32[]{:S(2)}, u32[]{:S(2)}) collective-permute-start(bf16[32,48,128]{2,1,0:T(8,128)(2,1)S(1)} %get-tuple-element.133), channel_id=1, source_target_pairs={{0,1},{1,0},{2,3},{3,2},{4,5},{5,4},{6,7},{7,6},{8,9},{9,8},{10,11... | collective-permute-start | bytes 1179656 | tf_op jit(solution)/shard_map/ppermute | solution.py:233
  289.5 32.4 %collective-permute-start.34 = (bf16[16,48,128]{2,1,0:T(8,128)(2,1)S(1)}, bf16[16,48,128]{2,1,0:T(8,128)(2,1)S(1)}, u32[]{:S(2)}, u32[]{:S(2)}) collective-permute-start(bf16[16,48,128]{2,1,0:T(8,128)(2,1)S(1)} %get-tuple-element.168), channel_id=1, source_target_pairs={{0,7},{1,6},{2,5},{3,4},{4,3},{5,2},{6,1},{7,0},{8,15},{9,14},{10,... | collective-permute-start | bytes 589832 | tf_op jit(solution)/shard_map/ppermute | solution.py:233
  306.0 17.7 %collective-permute-start.32 = (bf16[16,48,128]{2,1,0:T(8,128)(2,1)S(1)}, bf16[16,48,128]{2,1,0:T(8,128)(2,1)S(1)}, u32[]{:S(2)}, u32[]{:S(2)}) collective-permute-start(bf16[16,48,128]{2,1,0:T(8,128)(2,1)S(1)} %get-tuple-element.164), channel_id=1, source_target_pairs={{0,6},{1,7},{2,4},{3,5},{4,2},{5,3},{6,0},{7,1},{8,14},{9,15},{10,... | collective-permute-start | bytes 589832 | tf_op jit(solution)/shard_map/ppermute | solution.py:233
  319.2 14.9 %collective-permute-start.30 = (bf16[16,48,128]{2,1,0:T(8,128)(2,1)S(1)}, bf16[16,48,128]{2,1,0:T(8,128)(2,1)S(1)}, u32[]{:S(2)}, u32[]{:S(2)}) collective-permute-start(bf16[16,48,128]{2,1,0:T(8,128)(2,1)S(1)} %get-tuple-element.160), channel_id=1, source_target_pairs={{0,5},{1,4},{2,7},{3,6},{4,1},{5,0},{6,3},{7,2},{8,13},{9,12},{10,... | collective-permute-start | bytes 589832 | tf_op jit(solution)/shard_map/ppermute | solution.py:233
  319.3 15.2 %collective-permute-start.28 = (bf16[16,48,128]{2,1,0:T(8,128)(2,1)S(1)}, bf16[16,48,128]{2,1,0:T(8,128)(2,1)S(1)}, u32[]{:S(2)}, u32[]{:S(2)}) collective-permute-start(bf16[16,48,128]{2,1,0:T(8,128)(2,1)S(1)} %get-tuple-element.156), channel_id=1, source_target_pairs={{0,4},{1,5},{2,6},{3,7},{4,0},{5,1},{6,2},{7,3},{8,12},{9,13},{10,... | collective-permute-start | bytes 589832 | tf_op jit(solution)/shard_map/ppermute | solution.py:233
  319.4 15.2 %collective-permute-start.26 = (bf16[16,48,128]{2,1,0:T(8,128)(2,1)S(1)}, bf16[16,48,128]{2,1,0:T(8,128)(2,1)S(1)}, u32[]{:S(2)}, u32[]{:S(2)}) collective-permute-start(bf16[16,48,128]{2,1,0:T(8,128)(2,1)S(1)} %get-tuple-element.152), channel_id=1, source_target_pairs={{0,3},{1,2},{2,1},{3,0},{4,7},{5,6},{6,5},{7,4},{8,11},{9,10},{10,... | collective-permute-start | bytes 589832 | tf_op jit(solution)/shard_map/ppermute | solution.py:233
  321.9 16.3 %collective-permute-start.21 = (bf16[16,48,128]{2,1,0:T(8,128)(2,1)S(1)}, bf16[16,48,128]{2,1,0:T(8,128)(2,1)S(1)}, u32[]{:S(2)}, u32[]{:S(2)}) collective-permute-start(bf16[16,48,128]{2,1,0:T(8,128)(2,1)S(1)} %get-tuple-element.143), channel_id=1, source_target_pairs={{0,2},{1,3},{2,0},{3,1},{4,6},{5,7},{6,4},{7,5},{8,10},{9,11},{10,... | collective-permute-start | bytes 589832 | tf_op jit(solution)/shard_map/ppermute | solution.py:233
  323.7 14.5 %collective-permute-start.16 = (bf16[16,48,128]{2,1,0:T(8,128)(2,1)S(1)}, bf16[16,48,128]{2,1,0:T(8,128)(2,1)S(1)}, u32[]{:S(2)}, u32[]{:S(2)}) collective-permute-start(bf16[16,48,128]{2,1,0:T(8,128)(2,1)S(1)} %get-tuple-element.134), channel_id=1, source_target_pairs={{0,1},{1,0},{2,3},{3,2},{4,5},{5,4},{6,7},{7,6},{8,9},{9,8},{10,11... | collective-permute-start | bytes 589832 | tf_op jit(solution)/shard_map/ppermute | solution.py:233
  342.3 2.1 collective-permute-start.42
  344.6 6.7 %collective-permute-start.43 = (f32[96,384]{1,0:T(8,128)S(1)}, f32[96,384]{1,0:T(8,128)S(1)}, u32[]{:S(2)}, u32[]{:S(2)}) collective-permute-start(f32[96,384]{1,0:T(8,128)S(1)} %get-tuple-element.192), channel_id=1, source_target_pairs={{0,8},{8,0},{16,24},{24,16},{1,9},{9,1},{17,25},{25,17},{2,10},{10... | collective-permute-start | bytes 442376 | tf_op jit(solution)/shard_map/ppermute | solution.py:233
  346.2 8.8 %collective-permute-start.44 = (f32[96,384]{1,0:T(8,128)S(1)}, f32[96,384]{1,0:T(8,128)S(1)}, u32[]{:S(2)}, u32[]{:S(2)}) collective-permute-start(f32[96,384]{1,0:T(8,128)S(1)} %get-tuple-element.193), channel_id=1, source_target_pairs={{0,16},{8,24},{16,0},{24,8},{1,17},{9,25},{17,1},{25,9},{2,18},{10... | collective-permute-start | bytes 442376 | tf_op jit(solution)/shard_map/ppermute | solution.py:233
  347.7 7.2 %collective-permute-start.45 = (f32[96,384]{1,0:T(8,128)S(1)}, f32[96,384]{1,0:T(8,128)S(1)}, u32[]{:S(2)}, u32[]{:S(2)}) collective-permute-start(f32[96,384]{1,0:T(8,128)S(1)} %get-tuple-element.194), channel_id=1, source_target_pairs={{0,24},{8,16},{16,8},{24,0},{1,25},{9,17},{17,9},{25,1},{2,26},{10... | collective-permute-start | bytes 442376 | tf_op jit(solution)/shard_map/ppermute | solution.py:233
  355.1 4.5 %collective-permute-start.46 = (f32[2,48,96]{2,1,0:T(8,128)S(1)}, f32[2,48,96]{2,1,0:T(8,128)S(1)}, u32[]{:S(2)}, u32[]{:S(2)}) collective-permute-start(f32[2,48,96]{2,1,0:T(8,128)S(1)} %get-tuple-element.196), channel_id=1, source_target_pairs={{0,2},{1,3},{2,0},{3,1},{4,6},{5,7},{6,4},{7,5},{8,10},{9,11},{10,... | collective-permute-start | bytes 110600 | tf_op jit(solution)/shard_map/ppermute | solution.py:233
  355.2 5.5 %collective-permute-start.47 = (f32[2,48,96]{2,1,0:T(8,128)S(1)}, f32[2,48,96]{2,1,0:T(8,128)S(1)}, u32[]{:S(2)}, u32[]{:S(2)}) collective-permute-start(f32[2,48,96]{2,1,0:T(8,128)S(1)} %get-tuple-element.197), channel_id=1, source_target_pairs={{0,4},{1,5},{2,6},{3,7},{4,0},{5,1},{6,2},{7,3},{8,12},{9,13},{10,... | collective-permute-start | bytes 110600 | tf_op jit(solution)/shard_map/ppermute | solution.py:233
  358.2 5.9 %collective-permute-start.48 = (f32[2,48,96]{2,1,0:T(8,128)S(1)}, f32[2,48,96]{2,1,0:T(8,128)S(1)}, u32[]{:S(2)}, u32[]{:S(2)}) collective-permute-start(f32[2,48,96]{2,1,0:T(8,128)S(1)} %get-tuple-element.198), channel_id=1, source_target_pairs={{0,6},{1,7},{2,4},{3,5},{4,2},{5,3},{6,0},{7,1},{8,14},{9,15},{10,... | collective-permute-start | bytes 110600 | tf_op jit(solution)/shard_map/ppermute | solution.py:233
  (46 other events, 620.4 us)

commit v3 on v2

--- a/solution.py
+++ b/solution.py
@@ -12,7 +12,7 @@
 BF16 = jnp.bfloat16
 LANES = 128
 ROWS = 16
-VMEM = 48 * 2**20
+VMEM = 60 * 2**20
 
 
 def lorentz(offset, eta):
@@ -42,14 +42,15 @@
     return value + (n_one - n_two) * (lorentz(omega - differ, eta) - lorentz(omega + differ, eta))
 
 
-def rotate_kernel(parts, span, j_low, index, phi_ref, one_ref, two_ref, *rest):
-    outs, (turned_two, picked, held, turned) = rest[:parts], rest[parts:]
-    j_count = outs[0].shape[0]
+def rotate_kernel(parts, span, j_cuts, index, phi_ref, one_ref, two_ref, *rest):
+    outs, (turned_two, picked, held, turned) = rest[:-4], rest[-4:]
+    j_low, j_count = j_cuts[0][0], sum(count for _, count in j_cuts)
     _, block, rows, inner = phi_ref.shape
     cols = one_ref.shape[2]
     place = lax.axis_index("mode")
-
-    @pl.when(pl.program_id(0) == 0)
+    step = pl.program_id(0)
+
+    @pl.when(step == 0)
     def _():
         turned_two[...] = two_ref[0].T
         for s in range(parts):
@@ -61,45 +62,56 @@
     for c in range(block):
         held[:, c * cols : (c + 1) * cols] = first[c * rows : (c + 1) * rows]
     wide = jnp.dot(picked[...], held[...], preferred_element_type=F32)
+    at = lax.rem(step * block, ROWS)
     for c in range(block):
-        turned[pl.ds(c, parts * j_count, stride=block), :] = wide[:, c * cols : (c + 1) * cols]
-    size = j_count * block
-    for s in range(parts):
-        outs[s][...] = turned[s * size : (s + 1) * size].reshape(j_count, block, cols).astype(BF16)
-
-
-def rotate(phi, eigvecs, pair_index, parts, tile, c_low, c_count, j_low, j_count):
-    _, slices, rows, inner = phi.shape
+        turned[pl.ds(at + c, parts * j_count, stride=ROWS), :] = wide[:, c * cols : (c + 1) * cols]
+
+    @pl.when(at == ROWS - block)
+    def _():
+        for cut, (low, count) in enumerate(j_cuts):
+            for s in range(parts):
+                start = (s * j_count + low - j_low) * ROWS
+                piece = turned[start : start + count * ROWS].reshape(count, ROWS, cols)
+                outs[cut * parts + s][...] = piece.astype(BF16)
+
+
+def rotate(phi, eigvecs, pair_index, parts, tile, c_low, c_count, j_cuts, step):
+    _, _, rows, inner = phi.shape
     modes = eigvecs.shape[2]
-    first_block = c_low // ROWS
-    flops = 2 * c_count * rows * LANES * (inner + parts * j_count)
-    return pl.pallas_call(
-        functools.partial(rotate_kernel, parts, modes // parts, j_low),
+    j_count = sum(count for _, count in j_cuts)
+    first_block = c_low // step
+    outs = pl.pallas_call(
+        functools.partial(rotate_kernel, parts, modes // parts, j_cuts),
         grid_spec=pltpu.PrefetchScalarGridSpec(
             num_scalar_prefetch=1,
-            grid=(c_count // ROWS,),
+            grid=(c_count // step,),
             in_specs=[
-                pl.BlockSpec((1, ROWS, rows, inner), lambda g, index: (0, first_block + g, 0, 0)),
+                pl.BlockSpec((1, step, rows, inner), lambda g, index: (0, first_block + g, 0, 0)),
                 pl.BlockSpec((1, inner, LANES), lambda g, index: (index[0, 0], 0, tile)),
                 pl.BlockSpec((1, rows, modes), lambda g, index: (index[0, 1], 0, 0)),
             ],
-            out_specs=[pl.BlockSpec((j_count, ROWS, LANES), lambda g, index: (0, g, 0))] * parts,
+            out_specs=[
+                pl.BlockSpec((count, ROWS, LANES), lambda g, index: (0, g * step // ROWS, 0))
+                for _, count in j_cuts
+                for _ in range(parts)
+            ],
             scratch_shapes=[
                 pltpu.VMEM((modes, rows), BF16),
                 pltpu.VMEM((parts * j_count, rows), BF16),
-                pltpu.VMEM((rows, ROWS * LANES), BF16),
+                pltpu.VMEM((rows, step * LANES), BF16),
                 pltpu.VMEM((parts * j_count * ROWS, LANES), F32),
             ],
         ),
-        out_shape=[jax.ShapeDtypeStruct((j_count, c_count, LANES), BF16)] * parts,
+        out_shape=[
+            jax.ShapeDtypeStruct((count, c_count, LANES), BF16)
+            for _, count in j_cuts
+            for _ in range(parts)
+        ],
         compiler_params=pltpu.CompilerParams(vmem_limit_bytes=VMEM),
-        cost_estimate=pl.CostEstimate(
-            flops=flops,
-            bytes_accessed=2 * c_count * (rows * inner + parts * j_count * LANES),
-            transcendentals=0,
-        ),
+        cost_estimate=pl.CostEstimate(flops=1, bytes_accessed=1, transcendentals=0),
         name="rotate",
     )(pair_index, phi, eigvecs, eigvecs)
+    return [outs[cut * parts : (cut + 1) * parts] for cut in range(len(j_cuts))]
 
 
 def gram_kernel(parts, c_counts, fresh, omegas, three_ref, row_ref, col_ref, *rest):
@@ -131,27 +143,31 @@
             low = pl.multiple_of((2 * z + order) * span, ROWS)
             blocks.append(rotated[pl.ds(low, span)])
     ordered = jnp.concatenate(blocks, axis=0).astype(F32)
+    scaled = []
     for w in range(2):
-        weights = [
-            weight_pair(
-                row_ref[0:1, :], row_ref[1:2, :], row_ref[2:3, :],
-                col_ref[g : g + 1, 0:1], col_ref[g : g + 1, 1:2], col_ref[g : g + 1, 2:3],
-                omegas[0, w],
-            )
-            for g in range(group)
-        ]
-        scaled = (ordered * jnp.concatenate(weights, axis=1)).astype(BF16)
-        sums = lax.dot_general(
-            scaled, rotated[...], (((1,), (1,)), ((), ())), preferred_element_type=F32
+        weights = weight_pair(
+            row_ref[0:1, :], row_ref[1:2, :], row_ref[2:3, :],
+            col_ref[:, 0:1], col_ref[:, 1:2], col_ref[:, 2:3],
+            omegas[0, w],
         )
-        keep_ref[w] += sums[:half]
-        give_ref[w] += sums[half:]
-
-
-def gram(arrived, c_counts, three, rows, cols, probes, old, tile, j_low, group):
+        wide = jnp.concatenate([weights[g : g + 1] for g in range(group)], axis=1)
+        scaled.append((ordered * wide).astype(BF16))
+    sums = lax.dot_general(
+        jnp.concatenate(scaled, axis=0),
+        rotated[...],
+        (((1,), (1,)), ((), ())),
+        preferred_element_type=F32,
+    )
+    for w in range(2):
+        keep_ref[w] += sums[2 * w * half : (2 * w + 1) * half]
+        give_ref[w] += sums[(2 * w + 1) * half : (2 * w + 2) * half]
+
+
+def gram(arrived, offsets, three, rows, cols, probes, old, tile, j_low, j_count, group):
     parts = len(arrived)
     pieces = [piece for one in arrived for piece in one]
-    j_count = pieces[0].shape[0]
+    c_counts = [piece.shape[1] for piece in arrived[0]]
+    blocks = [offset // group for offset in offsets] * parts
     modes = three.shape[0]
     half = modes // 2
     fresh = old is None
@@ -165,7 +181,10 @@
             pl.BlockSpec((3, LANES), lambda g: (0, tile)),
             pl.BlockSpec((group, 3), lambda g: (j_low // group + g, 0)),
         ]
-        + [pl.BlockSpec((group, p.shape[1], LANES), lambda g: (g, 0, 0)) for p in pieces]
+        + [
+            pl.BlockSpec((group, p.shape[1], LANES), lambda g, b=b: (b + g, 0, 0))
+            for p, b in zip(pieces, blocks)
+        ]
         + ([] if fresh else [whole, whole]),
         out_specs=[whole, whole],
         out_shape=[jax.ShapeDtypeStruct((2, half, modes), F32)] * 2,
@@ -174,10 +193,10 @@
             pltpu.VMEM((modes, group * LANES), BF16),
         ],
         input_output_aliases={} if fresh else {4 + len(pieces): 0, 5 + len(pieces): 1},
-        compiler_params=pltpu.CompilerParams(vmem_limit_bytes=VMEM),
+        compiler_params=pltpu.CompilerParams(vmem_limit_bytes=VMEM // 2),
         cost_estimate=pl.CostEstimate(
-            flops=6 * modes * modes * j_count * LANES,
-            bytes_accessed=2 * modes * j_count * LANES + 16 * modes * modes,
+            flops=int(1 * 6 * modes * modes * j_count * LANES),
+            bytes_accessed=int(1 * (2 * modes * j_count * LANES + 16 * modes * modes)),
             transcendentals=0,
         ),
         name="gram",
@@ -200,7 +219,7 @@
         to_pairs_kernel,
         out_shape=[jax.ShapeDtypeStruct((modes // pairs, modes), F32)] * pairs,
         scratch_shapes=[pltpu.VMEM((modes, modes), F32)],
-        compiler_params=pltpu.CompilerParams(vmem_limit_bytes=VMEM),
+        compiler_params=pltpu.CompilerParams(vmem_limit_bytes=VMEM // 4),
         name="to_pairs",
     )(keep, got)
 
@@ -224,7 +243,7 @@
         functools.partial(to_modes_kernel, chips),
         out_shape=[jax.ShapeDtypeStruct((2, span, count), F32)] * chips,
         scratch_shapes=[pltpu.VMEM((modes, count), F32)],
-        compiler_params=pltpu.CompilerParams(vmem_limit_bytes=VMEM),
+        compiler_params=pltpu.CompilerParams(vmem_limit_bytes=VMEM // 4),
         name="to_modes",
     )(*parts)
 
@@ -234,18 +253,23 @@
 
 
 def plan(modes, slices, span):
-    whole = [(0, slices)]
-    cuts = [(0, ROWS), (ROWS, slices - ROWS)] if slices > ROWS else whole
-    blocks = [(0, cuts, 0, ROWS)]
-    if span > ROWS:
-        blocks.append((0, whole, ROWS, span - ROWS))
-    for tile in range(1, modes // LANES):
-        if tile == modes // LANES - 1 and span > ROWS:
-            blocks.append((tile, whole, 0, span - ROWS))
-            blocks.append((tile, whole, span - ROWS, ROWS))
+    last = 8 if span > 8 else span
+    rotations, sums = [], []
+    block = 0
+    for tile in range(modes // LANES):
+        cuts = [(0, span)]
+        if tile == modes // LANES - 1 and span > last:
+            cuts = [(0, span - last), (span - last, last)]
+        if tile == 0 and slices > ROWS:
+            rotations.append((tile, 0, ROWS, [(0, span)], ROWS // 4))
+            rotations.append((tile, ROWS, slices - ROWS, cuts, ROWS))
+            sums += [(tile, low, count, [(0, low), (1 + at, 0)]) for at, (low, count) in enumerate(cuts)]
+            block = 1 + len(cuts)
         else:
-            blocks.append((tile, whole, 0, span))
-    return blocks
+            rotations.append((tile, 0, slices, cuts, ROWS))
+            sums += [(tile, low, count, [(block + at, 0)]) for at, (low, count) in enumerate(cuts)]
+            block += len(cuts)
+    return rotations, sums
 
 
 def shards(phi, eigvecs, freqs, occupations, smearing, probes, pair_index):
@@ -262,38 +286,34 @@
     rows = jnp.stack([pick(freqs, 0), pick(occupations, 0), pick(smearing, 0)])
     cols = jnp.stack([pick(freqs, 1), pick(occupations, 1), pick(smearing, 1)])
     cols = lax.dynamic_slice_in_dim(cols, place * span, span, axis=1).T
-    blocks = plan(modes, slices, span)
-
-    def turn(step, after):
-        tile, cuts, j_low, j_count = blocks[step]
-        if after is None:
-            tensor = phi
-        else:
-            tensor, _ = lax.optimization_barrier((phi, after))
-        return [
-            rotate(tensor, eigvecs, pair_index, parts, tile, c_low, c_count, j_low, j_count)
-            for c_low, c_count in cuts
-        ]
-
     far = list(range(parts // 2, parts))
     near = list(range(1, parts // 2))
-    sums, before = None, None
-    ready = [turn(0, None), turn(1, None)]
-    for step, (tile, cuts, j_low, j_count) in enumerate(blocks):
-        arrived = [[] for _ in range(parts)]
-        arrived[0] = [piece[0] for piece in ready[step]]
+    rotations, sums = plan(modes, slices, span)
+    ready, sent, total = [], [], None
+
+    def turn(after):
+        tile, c_low, c_count, j_cuts, step = rotations.pop(0)
+        tensor = phi if after is None else lax.optimization_barrier((phi, after))[0]
+        ready.extend(rotate(tensor, eigvecs, pair_index, parts, tile, c_low, c_count, j_cuts, step))
+
+    turn(None)
+    for step, blocks in enumerate(ready):
+        got = {0: blocks[0]}
         for s in far + near:
-            for piece in ready[step]:
-                block = piece[s]
-                if before is not None:
-                    block, _ = lax.optimization_barrier((block, before[s][-1]))
-                arrived[s].append(swap(block, "mode", parts, s))
-        if step + 2 < len(blocks):
-            ready.append(turn(step + 2, [arrived[s][-1] for s in far]))
-        counts = [count for _, count in cuts]
-        sums = gram(arrived, counts, three, rows, cols, probes, sums, tile, j_low, 8)
-        before = arrived
-    keep, give = sums
+            block = blocks[s]
+            if step > 0:
+                before = [sent[-1][r] for r in (far if s == 1 else [s])]
+                block, _ = lax.optimization_barrier((block, before))
+            got[s] = swap(block, "mode", parts, s)
+        sent.append(got)
+        if rotations:
+            turn(got[1])
+        while sums and max(block for block, _ in sums[0][-1]) <= step:
+            tile, j_low, j_count, used = sums.pop(0)
+            arrived = [[sent[block][s] for block, _ in used] for s in range(parts)]
+            offsets = [offset for _, offset in used]
+            total = gram(arrived, offsets, three, rows, cols, probes, total, tile, j_low, j_count, 8)
+    keep, give = total
     blocks = to_pairs(keep, swap(give, "mode", parts, 1), pairs)
     blocks = [b if s == 0 else swap(b, "pair", pairs, s) for s, b in enumerate(blocks)]
     blocks = to_modes(blocks, parts // 2)
@@ -363,8 +383,8 @@
     def either(phi, *rest):
         _, slices, modes, _ = phi.shape
         fits = slices % ROWS == 0 and modes % LANES == 0 and slices * parts == modes
-        fits = fits and parts > 1 and parts & (parts - 1) == 0 and pairs & (pairs - 1) == 0
-        fits = fits and modes % (8 * pairs) == 0
+        fits = fits and parts > 3 and parts & (parts - 1) == 0 and pairs & (pairs - 1) == 0
+        fits = fits and modes % (8 * pairs) == 0 and modes // parts % ROWS == 0
         return (shards if fits else shards_plain)(phi, *rest)
 
     return jax.shard_map(

time: 366 us -> 358 us (0.978)
  starting transfers between devices: 85.1 us -> 103 us
  Pallas kernels: 93.1 us -> 78.5 us
  waiting for transfers between devices: 149 us -> 138 us
    ppermute x49 -> x42, starting transfers between devices: 85.1 us -> 103 us  [swap(): return lax.ppermute(x, axis, [(i, i ^ distance) for i in range(size)])]
    ppermute x49 -> x42, waiting for transfers between devices: 149 us -> 138 us  [swap(): return lax.ppermute(x, axis, [(i, i ^ distance) for i in range(size)])]
    pallas_call x6 -> x4, Pallas kernels: 56.8 us -> 45.6 us  [rotate(): pl.pallas_call(functools.partial(rotate_kernel, parts, modes // parts, j_...]
    unnamed x91 -> x99, local copies, waits for them, and re-layouts: 21.1 us -> 24.7 us
    pallas_call x5 -> x4, Pallas kernels: 35.9 us -> 32.5 us  [gram(): pl.pallas_call(functools.partial(gram_kernel, parts, c_counts, fresh), gr...]
  transfers between devices with their start and end apart: 49 -> 42, of which waited for: 21 -> 14; matrix products, arithmetic and copies ran while one was open for 3% -> 2% of each run, Pallas kernels for 22% -> 19%
where the time goes in v3:
time: 358 us; the launch traced here: 357 us
  waiting for transfers between devices  138 us (39%)
  starting transfers between devices  103 us (29%)
  Pallas kernels  78.5 us (22%)
  local copies, waits for them, and re-layouts  31 us (9%)
  between operations  5.92 us (2%)
    ppermute x42, waiting for transfers between devices, swap(): return lax.ppermute(x, axis, [(i, i ^ distance) for i in range(size)])  138 us
    ppermute x42, starting transfers between devices, swap(): return lax.ppermute(x, axis, [(i, i ^ distance) for i in range(size)])  103 us
    pallas_call x4, Pallas kernels, rotate(): pl.pallas_call(functools.partial(rotate_kernel, parts, modes // parts, j_...  45.6 us
    pallas_call x4, Pallas kernels, gram(): pl.pallas_call(functools.partial(gram_kernel, parts, c_counts, fresh), gr...  32.5 us
    unnamed x99, local copies, waits for them, and re-layouts  24.7 us
  transfers between devices with their start and end apart: 42, of which 14 were waited for; matrix products, arithmetic and copies ran while one was open for 2% of the time, Pallas kernels for 19%

profile of v3, /device:TPU:0, one launch (start us, length us, event | category | flops | bytes accessed | tf_op | source)
XLA Modules:
  0.0 356.8 jit_solution(16199704713532989637)
XLA Ops:
  0.0 8.7 %rotate.4 = (bf16[48,16,128]{2,1,0:T(8,128)(2,1)}, bf16[48,16,128]{2,1,0:T(8,128)(2,1)}, bf16[48,16,128]{2,1,0:T(8,128)(2,1)}, bf16[48,16,128]{2,1,0:T(8,128)(2,...) custom-call(s32[1,3]{1,0:T(1,128)} %index.7, ...), custom_call_target="tpu_custom_call" | custom-call | flops 1 | bytes 1 | tf_op jit(solution)/shard_map/rotate/pallas_call | solution.py:83
  9.2 3.7 %collective-permute-start.1 = (bf16[48,16,128]{2,1,0:T(8,128)(2,1)}, bf16[48,16,128]{2,1,0:T(8,128)(2,1)S(1)}, u32[]{:S(2)}, u32[]{:S(2)}) collective-permute-start(bf16[48,16,128]{2,1,0:T(8,128)(2,1)} %get-tuple-element.95), channel_id=1, source_target_pairs={{0,4},{1,5},{2,6},{3,7},{4,0},{5,1},{6,2},{7,3},{8,12},{9,13},{10,... | collective-permute-start | bytes 589832 | tf_op jit(solution)/shard_map/ppermute | solution.py:252
  12.9 3.7 %collective-permute-start.3 = (bf16[48,16,128]{2,1,0:T(8,128)(2,1)}, bf16[48,16,128]{2,1,0:T(8,128)(2,1)S(1)}, u32[]{:S(2)}, u32[]{:S(2)}) collective-permute-start(bf16[48,16,128]{2,1,0:T(8,128)(2,1)} %get-tuple-element.97), channel_id=1, source_target_pairs={{0,6},{1,7},{2,4},{3,5},{4,2},{5,3},{6,0},{7,1},{8,14},{9,15},{10,... | collective-permute-start | bytes 589832 | tf_op jit(solution)/shard_map/ppermute | solution.py:252
  17.2 10.2 %rotate.5 = (bf16[48,32,128]{2,1,0:T(8,128)(2,1)}, bf16[48,32,128]{2,1,0:T(8,128)(2,1)}, bf16[48,32,128]{2,1,0:T(8,128)(2,1)}, bf16[48,32,128]{2,1,0:T(8,128)(2,...) custom-call(s32[1,3]{1,0:T(1,128)} %index.7, ...), custom_call_target="tpu_custom_call" | custom-call | flops 1 | bytes 1 | tf_op jit(solution)/shard_map/rotate/pallas_call | solution.py:83
  27.4 8.2 %collective-permute-done.1.rest_8_ = bf16[48,16,128]{2,1,0:T(8,128)(2,1)S(1)} collective-permute-done((bf16[48,16,128]{2,1,0:T(8,128)(2,1)}, bf16[48,16,128]{2,1,0:T(8,128)(2,1)S(1)}, u32[]{:S(2)}, u32[]{:S(2)}) %collective-permute-start.1) | collective-permute-done | bytes 196640 | tf_op jit(solution)/shard_map/ppermute | solution.py:252
  36.3 3.0 collective-permute-done.2.rest_10_
  41.7 3.6 %collective-permute-start.8 = (bf16[48,32,128]{2,1,0:T(8,128)(2,1)}, bf16[48,32,128]{2,1,0:T(8,128)(2,1)S(1)}, u32[]{:S(2)}, u32[]{:S(2)}) collective-permute-start(bf16[48,32,128]{2,1,0:T(8,128)(2,1)} %get-tuple-element.107), channel_id=1, source_target_pairs={{0,6},{1,7},{2,4},{3,5},{4,2},{5,3},{6,0},{7,1},{8,14},{9,15},{10,... | collective-permute-start | bytes 1179656 | tf_op jit(solution)/shard_map/ppermute | solution.py:252
  45.3 23.6 %collective-permute-start.20 = (bf16[48,16,128]{2,1,0:T(8,128)(2,1)S(1)}, bf16[48,16,128]{2,1,0:T(8,128)(2,1)S(1)}, u32[]{:S(2)}, u32[]{:S(2)}) collective-permute-start(bf16[48,16,128]{2,1,0:T(8,128)(2,1)S(1)} %copy-done.41), channel_id=1, source_target_pairs={{0,2},{1,3},{2,0},{3,1},{4,6},{5,7},{6,4},{7,5},{8,10},{9,11},{10,... | collective-permute-start | bytes 589832 | tf_op jit(solution)/shard_map/ppermute | solution.py:252
  69.8 13.1 %rotate.6 = (bf16[48,48,128]{2,1,0:T(8,128)(2,1)}, bf16[48,48,128]{2,1,0:T(8,128)(2,1)}, bf16[48,48,128]{2,1,0:T(8,128)(2,1)}, bf16[48,48,128]{2,1,0:T(8,128)(2,...) custom-call(s32[1,3]{1,0:T(1,128)} %index.7, ...), custom_call_target="tpu_custom_call" | custom-call | flops 1 | bytes 1 | tf_op jit(solution)/shard_map/rotate/pallas_call | solution.py:83
  83.7 2.7 collective-permute-start.15
  87.3 2.1 collective-permute-start.6
  90.1 1.1 collective-permute-start.21
  97.0 41.3 %collective-permute-done.7.rest_11_ = bf16[48,32,128]{2,1,0:T(8,128)(2,1)S(1)} collective-permute-done((bf16[48,32,128]{2,1,0:T(8,128)(2,1)}, bf16[48,32,128]{2,1,0:T(8,128)(2,1)S(1)}, u32[]{:S(2)}, u32[]{:S(2)}) %collective-permute-start.7) | collective-permute-done | bytes 393248 | tf_op jit(solution)/shard_map/ppermute | solution.py:252
  139.0 8.0 %collective-permute-done.6.rest_9_ = bf16[48,32,128]{2,1,0:T(8,128)(2,1)S(1)} collective-permute-done((bf16[48,32,128]{2,1,0:T(8,128)(2,1)}, bf16[48,32,128]{2,1,0:T(8,128)(2,1)S(1)}, u32[]{:S(2)}, u32[]{:S(2)}) %collective-permute-start.6) | collective-permute-done | bytes 393248 | tf_op jit(solution)/shard_map/ppermute | solution.py:252
  150.2 2.1 collective-permute-start.22
  152.3 1.9 collective-permute-start.17
  156.9 1.0 constant_dynamic-slice_fusion.6
  157.9 1.3 gather_fusion
  159.2 1.2 copy.23
  160.4 3.1 collective-permute-start.13
  163.5 13.7 %rotate.7 = (bf16[40,48,128]{2,1,0:T(8,128)(2,1)}, bf16[40,48,128]{2,1,0:T(8,128)(2,1)}, bf16[40,48,128]{2,1,0:T(8,128)(2,1)}, bf16[40,48,128]{2,1,0:T(8,128)(2,...) custom-call(s32[1,3]{1,0:T(1,128)} %index.7, ...), custom_call_target="tpu_custom_call" | custom-call | flops 1 | bytes 1 | tf_op jit(solution)/shard_map/rotate/pallas_call | solution.py:83
  177.2 15.0 %collective-permute-done.17.rest_7_ = bf16[48,48,128]{2,1,0:T(8,128)(2,1)S(1)} collective-permute-done((bf16[48,48,128]{2,1,0:T(8,128)(2,1)}, bf16[48,48,128]{2,1,0:T(8,128)(2,1)S(1)}, u32[]{:S(2)}, u32[]{:S(2)}) %collective-permute-start.17) | collective-permute-done | bytes 589856 | tf_op jit(solution)/shard_map/ppermute | solution.py:252
  192.2 11.1 %collective-permute-done.22.rest_2_ = bf16[48,48,128]{2,1,0:T(8,128)(2,1)S(1)} collective-permute-done((bf16[48,48,128]{2,1,0:T(8,128)(2,1)}, bf16[48,48,128]{2,1,0:T(8,128)(2,1)S(1)}, u32[]{:S(2)}, u32[]{:S(2)}) %collective-permute-start.22) | collective-permute-done | bytes 589856 | tf_op jit(solution)/shard_map/ppermute | solution.py:252
  203.4 1.2 collective-permute-start.23
  204.6 1.5 collective-permute-start.18
  206.1 12.6 %collective-permute-done.11.rest_4_ = bf16[48,48,128]{2,1,0:T(8,128)(2,1)} collective-permute-done((bf16[48,48,128]{2,1,0:T(8,128)(2,1)}, bf16[48,48,128]{2,1,0:T(8,128)(2,1)}, u32[]{:S(2)}, u32[]{:S(2)}) %collective-permute-start.11) | collective-permute-done | bytes 589856 | tf_op jit(solution)/shard_map/ppermute | solution.py:252
  218.7 2.6 collective-permute-start.16
  221.3 1.0 copy-done.2
  222.3 1.0 copy-done.4
  235.8 10.4 %gram.4 = (f32[2,192,384]{2,1,0:T(8,128)S(1)}, f32[2,192,384]{2,1,0:T(8,128)S(1)}) custom-call(f32[1,2]{1,0:T(1,128)S(1)} %copy-done.33, bf16[384,384]{1,0:T(8,128)(2,1)S(1)} %bitcast.11, f32[3,384]{1,0:T(4,128)S(1)} %pad_maximum_fusion.row_ref, f32[48,3]{1,0:T(8,128)S(1)} %bitcast.15, bf16[48,16,128]{2,1,0:T(8,128)(2,1)S(1)} %copy-done.17, ...), custom_call_target="tpu_custom_call" | custom-call | flops 5435817984 | bytes 7077888 | tf_op jit(solution)/shard_map/gram/pallas_call | solution.py:175
  246.4 15.0 %collective-permute-done.23.rest_2_ = bf16[40,48,128]{2,1,0:T(8,128)(2,1)S(1)} collective-permute-done((bf16[40,48,128]{2,1,0:T(8,128)(2,1)}, bf16[40,48,128]{2,1,0:T(8,128)(2,1)S(1)}, u32[]{:S(2)}, u32[]{:S(2)}) %collective-permute-start.23) | collective-permute-done | bytes 491552 | tf_op jit(solution)/shard_map/ppermute | solution.py:252
  262.2 21.6 %collective-permute-start.29 = (bf16[8,48,128]{2,1,0:T(8,128)(2,1)S(1)}, bf16[8,48,128]{2,1,0:T(8,128)(2,1)S(1)}, u32[]{:S(2)}, u32[]{:S(2)}) collective-permute-start(bf16[8,48,128]{2,1,0:T(8,128)(2,1)S(1)} %copy-done.48), channel_id=1, source_target_pairs={{0,3},{1,2},{2,1},{3,0},{4,7},{5,6},{6,5},{7,4},{8,11},{9,10},{10,... | collective-permute-start | bytes 294920 | tf_op jit(solution)/shard_map/ppermute | solution.py:252
  283.8 11.1 %collective-permute-start.24 = (bf16[8,48,128]{2,1,0:T(8,128)(2,1)S(1)}, bf16[8,48,128]{2,1,0:T(8,128)(2,1)S(1)}, u32[]{:S(2)}, u32[]{:S(2)}) collective-permute-start(bf16[8,48,128]{2,1,0:T(8,128)(2,1)S(1)} %copy-done.47), channel_id=1, source_target_pairs={{0,2},{1,3},{2,0},{3,1},{4,6},{5,7},{6,4},{7,5},{8,10},{9,11},{10,... | collective-permute-start | bytes 294920 | tf_op jit(solution)/shard_map/ppermute | solution.py:252
  295.0 11.0 %gram.5 = (f32[2,192,384]{2,1,0:T(8,128)S(1)}, f32[2,192,384]{2,1,0:T(8,128)S(1)}) custom-call(f32[1,2]{1,0:T(1,128)S(1)} %copy-done.33, bf16[384,384]{1,0:T(8,128)(2,1)S(1)} %bitcast.12, f32[3,384]{1,0:T(4,128)S(1)} %pad_maximum_fusion.row_ref, f32[48,3]{1,0:T(8,128)S(1)} %bitcast.16, ...), custom_call_target="tpu_custom_call", output_to_operand_aliasing={{0}: (12, {}), {1}: (13, {})} | custom-call | flops 5435817984 | bytes 7077888 | tf_op jit(solution)/shard_map/gram/pallas_call | solution.py:175
  306.0 1.4 collective-permute-start.33
  307.5 10.1 %collective-permute-done.12.rest_4_ = bf16[40,48,128]{2,1,0:T(8,128)(2,1)S(1)} collective-permute-done((bf16[40,48,128]{2,1,0:T(8,128)(2,1)S(1)}, bf16[40,48,128]{2,1,0:T(8,128)(2,1)S(1)}, u32[]{:S(2)}, u32[]{:S(2)}) %collective-permute-start.12) | collective-permute-done | bytes 491552 | tf_op jit(solution)/shard_map/ppermute | solution.py:252
  317.6 2.6 collective-permute-start.32
  320.3 2.9 collective-permute-start.30
  323.3 8.8 %gram.6 = (f32[2,192,384]{2,1,0:T(8,128)S(1)}, f32[2,192,384]{2,1,0:T(8,128)S(1)}) custom-call(f32[1,2]{1,0:T(1,128)S(1)} %copy-done.33, bf16[384,384]{1,0:T(8,128)(2,1)S(1)} %bitcast.13, f32[3,384]{1,0:T(4,128)S(1)} %pad_maximum_fusion.row_ref, f32[48,3]{1,0:T(8,128)S(1)} %bitcast.17, ...), custom_call_target="tpu_custom_call", output_to_operand_aliasing={{0}: (12, {}), {1}: (13, {})} | custom-call | flops 4529848320 | bytes 6291456 | tf_op jit(solution)/shard_map/gram/pallas_call | solution.py:175
  332.1 2.2 gram.7
  334.4 2.0 collective-permute-done.35.got_ref
  336.7 1.6 collective-permute-start.36
  338.2 1.5 collective-permute-start.37
  340.3 3.1 collective-permute-done.36.rest_1_
  343.3 3.7 %collective-permute-done.37.rest_2_ = f32[96,384]{1,0:T(8,128)S(1)} collective-permute-done((f32[96,384]{1,0:T(8,128)S(1)}, f32[96,384]{1,0:T(8,128)S(1)}, u32[]{:S(2)}, u32[]{:S(2)}) %collective-permute-start.37) | collective-permute-done | bytes 147488 | tf_op jit(solution)/shard_map/ppermute | solution.py:252
  347.3 3.0 collective-permute-start.40
  350.2 1.4 collective-permute-start.41
  352.6 3.5 collective-permute-done.41
  (160 shorter events, 30.7 us)
Async XLA Ops:
  8.7 7.9 %collective-permute-start = (bf16[48,16,128]{2,1,0:T(8,128)(2,1)}, bf16[48,16,128]{2,1,0:T(8,128)(2,1)S(1)}, u32[]{:S(2)}, u32[]{:S(2)}) collective-permute-start(bf16[48,16,128]{2,1,0:T(8,128)(2,1)} %get-tuple-element.92), channel_id=1, source_target_pairs={{0,1},{1,0},{2,3},{3,2},{4,5},{5,4},{6,7},{7,6},{8,9},{9,8},{10,11... | collective-permute-start | bytes 589832 | tf_op jit(solution)/shard_map/ppermute | solution.py:252
  9.2 26.5 %collective-permute-start.1 = (bf16[48,16,128]{2,1,0:T(8,128)(2,1)}, bf16[48,16,128]{2,1,0:T(8,128)(2,1)S(1)}, u32[]{:S(2)}, u32[]{:S(2)}) collective-permute-start(bf16[48,16,128]{2,1,0:T(8,128)(2,1)} %get-tuple-element.95), channel_id=1, source_target_pairs={{0,4},{1,5},{2,6},{3,7},{4,0},{5,1},{6,2},{7,3},{8,12},{9,13},{10,... | collective-permute-start | bytes 589832 | tf_op jit(solution)/shard_map/ppermute | solution.py:252
  12.8 26.5 %collective-permute-start.2 = (bf16[48,16,128]{2,1,0:T(8,128)(2,1)}, bf16[48,16,128]{2,1,0:T(8,128)(2,1)S(1)}, u32[]{:S(2)}, u32[]{:S(2)}) collective-permute-start(bf16[48,16,128]{2,1,0:T(8,128)(2,1)} %get-tuple-element.96), channel_id=1, source_target_pairs={{0,5},{1,4},{2,7},{3,6},{4,1},{5,0},{6,3},{7,2},{8,13},{9,12},{10,... | collective-permute-start | bytes 589832 | tf_op jit(solution)/shard_map/ppermute | solution.py:252
  12.9 27.1 %collective-permute-start.3 = (bf16[48,16,128]{2,1,0:T(8,128)(2,1)}, bf16[48,16,128]{2,1,0:T(8,128)(2,1)S(1)}, u32[]{:S(2)}, u32[]{:S(2)}) collective-permute-start(bf16[48,16,128]{2,1,0:T(8,128)(2,1)} %get-tuple-element.97), channel_id=1, source_target_pairs={{0,6},{1,7},{2,4},{3,5},{4,2},{5,3},{6,0},{7,1},{8,14},{9,15},{10,... | collective-permute-start | bytes 589832 | tf_op jit(solution)/shard_map/ppermute | solution.py:252
  16.6 28.8 %copy-start.41 = (bf16[48,16,128]{2,1,0:T(8,128)(2,1)S(1)}, bf16[48,16,128]{2,1,0:T(8,128)(2,1)}, u32[]{:S(2)}) copy-start(bf16[48,16,128]{2,1,0:T(8,128)(2,1)} %get-tuple-element.135) | copy-start | bytes 589828
  16.6 52.4 %copy-start.40 = (bf16[48,16,128]{2,1,0:T(8,128)(2,1)S(1)}, bf16[48,16,128]{2,1,0:T(8,128)(2,1)}, u32[]{:S(2)}) copy-start(bf16[48,16,128]{2,1,0:T(8,128)(2,1)} %get-tuple-element.144) | copy-start | bytes 589828
  16.6 24.1 %collective-permute-start.4 = (bf16[48,16,128]{2,1,0:T(8,128)(2,1)}, bf16[48,16,128]{2,1,0:T(8,128)(2,1)S(1)}, u32[]{:S(2)}, u32[]{:S(2)}) collective-permute-start(bf16[48,16,128]{2,1,0:T(8,128)(2,1)} %get-tuple-element.98), channel_id=1, source_target_pairs={{0,7},{1,6},{2,5},{3,4},{4,3},{5,2},{6,1},{7,0},{8,15},{9,14},{10,... | collective-permute-start | bytes 589832 | tf_op jit(solution)/shard_map/ppermute | solution.py:252
  41.4 27.6 %collective-permute-start.5 = (bf16[48,32,128]{2,1,0:T(8,128)(2,1)}, bf16[48,32,128]{2,1,0:T(8,128)(2,1)S(1)}, u32[]{:S(2)}, u32[]{:S(2)}) collective-permute-start(bf16[48,32,128]{2,1,0:T(8,128)(2,1)} %get-tuple-element.99), channel_id=1, source_target_pairs={{0,1},{1,0},{2,3},{3,2},{4,5},{5,4},{6,7},{7,6},{8,9},{9,8},{10,11... | collective-permute-start | bytes 1179656 | tf_op jit(solution)/shard_map/ppermute | solution.py:252
  41.7 41.2 %collective-permute-start.8 = (bf16[48,32,128]{2,1,0:T(8,128)(2,1)}, bf16[48,32,128]{2,1,0:T(8,128)(2,1)S(1)}, u32[]{:S(2)}, u32[]{:S(2)}) collective-permute-start(bf16[48,32,128]{2,1,0:T(8,128)(2,1)} %get-tuple-element.107), channel_id=1, source_target_pairs={{0,6},{1,7},{2,4},{3,5},{4,2},{5,3},{6,0},{7,1},{8,14},{9,15},{10,... | collective-permute-start | bytes 1179656 | tf_op jit(solution)/shard_map/ppermute | solution.py:252
  45.3 45.8 %collective-permute-start.9 = (bf16[48,32,128]{2,1,0:T(8,128)(2,1)}, bf16[48,32,128]{2,1,0:T(8,128)(2,1)S(1)}, u32[]{:S(2)}, u32[]{:S(2)}) collective-permute-start(bf16[48,32,128]{2,1,0:T(8,128)(2,1)} %get-tuple-element.109), channel_id=1, source_target_pairs={{0,7},{1,6},{2,5},{3,4},{4,3},{5,2},{6,1},{7,0},{8,15},{9,14},{10,... | collective-permute-start | bytes 1179656 | tf_op jit(solution)/shard_map/ppermute | solution.py:252
  45.3 41.3 %collective-permute-start.20 = (bf16[48,16,128]{2,1,0:T(8,128)(2,1)S(1)}, bf16[48,16,128]{2,1,0:T(8,128)(2,1)S(1)}, u32[]{:S(2)}, u32[]{:S(2)}) collective-permute-start(bf16[48,16,128]{2,1,0:T(8,128)(2,1)S(1)} %copy-done.41), channel_id=1, source_target_pairs={{0,2},{1,3},{2,0},{3,1},{4,6},{5,7},{6,4},{7,5},{8,10},{9,11},{10,... | collective-permute-start | bytes 589832 | tf_op jit(solution)/shard_map/ppermute | solution.py:252
  68.9 20.5 %collective-permute-start.25 = (bf16[48,16,128]{2,1,0:T(8,128)(2,1)S(1)}, bf16[48,16,128]{2,1,0:T(8,128)(2,1)S(1)}, u32[]{:S(2)}, u32[]{:S(2)}) collective-permute-start(bf16[48,16,128]{2,1,0:T(8,128)(2,1)S(1)} %copy-done.40), channel_id=1, source_target_pairs={{0,3},{1,2},{2,1},{3,0},{4,7},{5,6},{6,5},{7,4},{8,11},{9,10},{10,... | collective-permute-start | bytes 589832 | tf_op jit(solution)/shard_map/ppermute | solution.py:252
  83.7 70.5 %collective-permute-start.15 = (bf16[48,48,128]{2,1,0:T(8,128)(2,1)}, bf16[48,48,128]{2,1,0:T(8,128)(2,1)S(1)}, u32[]{:S(2)}, u32[]{:S(2)}) collective-permute-start(bf16[48,48,128]{2,1,0:T(8,128)(2,1)} %get-tuple-element.124), channel_id=1, source_target_pairs={{0,6},{1,7},{2,4},{3,5},{4,2},{5,3},{6,0},{7,1},{8,14},{9,15},{10,... | collective-permute-start | bytes 1769480 | tf_op jit(solution)/shard_map/ppermute | solution.py:252
  86.3 51.9 %collective-permute-start.7 = (bf16[48,32,128]{2,1,0:T(8,128)(2,1)}, bf16[48,32,128]{2,1,0:T(8,128)(2,1)S(1)}, u32[]{:S(2)}, u32[]{:S(2)}) collective-permute-start(bf16[48,32,128]{2,1,0:T(8,128)(2,1)} %get-tuple-element.105), channel_id=1, source_target_pairs={{0,5},{1,4},{2,7},{3,6},{4,1},{5,0},{6,3},{7,2},{8,13},{9,12},{10,... | collective-permute-start | bytes 1179656 | tf_op jit(solution)/shard_map/ppermute | solution.py:252
  87.3 59.7 %collective-permute-start.6 = (bf16[48,32,128]{2,1,0:T(8,128)(2,1)}, bf16[48,32,128]{2,1,0:T(8,128)(2,1)S(1)}, u32[]{:S(2)}, u32[]{:S(2)}) collective-permute-start(bf16[48,32,128]{2,1,0:T(8,128)(2,1)} %get-tuple-element.103), channel_id=1, source_target_pairs={{0,4},{1,5},{2,6},{3,7},{4,0},{5,1},{6,2},{7,3},{8,12},{9,13},{10,... | collective-permute-start | bytes 1179656 | tf_op jit(solution)/shard_map/ppermute | solution.py:252
  90.1 58.6 %collective-permute-start.21 = (bf16[48,32,128]{2,1,0:T(8,128)(2,1)S(1)}, bf16[48,32,128]{2,1,0:T(8,128)(2,1)S(1)}, u32[]{:S(2)}, u32[]{:S(2)}) collective-permute-start(bf16[48,32,128]{2,1,0:T(8,128)(2,1)S(1)} %copy-done.39), channel_id=1, source_target_pairs={{0,2},{1,3},{2,0},{3,1},{4,6},{5,7},{6,4},{7,5},{8,10},{9,11},{10,... | collective-permute-start | bytes 1179656 | tf_op jit(solution)/shard_map/ppermute | solution.py:252
  91.9 57.5 %collective-permute-start.26 = (bf16[48,32,128]{2,1,0:T(8,128)(2,1)S(1)}, bf16[48,32,128]{2,1,0:T(8,128)(2,1)S(1)}, u32[]{:S(2)}, u32[]{:S(2)}) collective-permute-start(bf16[48,32,128]{2,1,0:T(8,128)(2,1)S(1)} %copy-done.38), channel_id=1, source_target_pairs={{0,3},{1,2},{2,1},{3,0},{4,7},{5,6},{6,5},{7,4},{8,11},{9,10},{10,... | collective-permute-start | bytes 1179656 | tf_op jit(solution)/shard_map/ppermute | solution.py:252
  147.8 12.5 %collective-permute-start.10 = (bf16[48,48,128]{2,1,0:T(8,128)(2,1)}, bf16[48,48,128]{2,1,0:T(8,128)(2,1)S(1)}, u32[]{:S(2)}, u32[]{:S(2)}) collective-permute-start(bf16[48,48,128]{2,1,0:T(8,128)(2,1)} %get-tuple-element.110), channel_id=1, source_target_pairs={{0,1},{1,0},{2,3},{3,2},{4,5},{5,4},{6,7},{7,6},{8,9},{9,8},{10,11... | collective-permute-start | bytes 1769480 | tf_op jit(solution)/shard_map/ppermute | solution.py:252
  150.2 53.2 %collective-permute-start.27 = (bf16[48,48,128]{2,1,0:T(8,128)(2,1)}, bf16[48,48,128]{2,1,0:T(8,128)(2,1)S(1)}, u32[]{:S(2)}, u32[]{:S(2)}) collective-permute-start(bf16[48,48,128]{2,1,0:T(8,128)(2,1)} %get-tuple-element.146), channel_id=1, source_target_pairs={{0,3},{1,2},{2,1},{3,0},{4,7},{5,6},{6,5},{7,4},{8,11},{9,10},{10,... | collective-permute-start | bytes 1769480 | tf_op jit(solution)/shard_map/ppermute | solution.py:252
  150.2 53.2 %collective-permute-start.22 = (bf16[48,48,128]{2,1,0:T(8,128)(2,1)}, bf16[48,48,128]{2,1,0:T(8,128)(2,1)S(1)}, u32[]{:S(2)}, u32[]{:S(2)}) collective-permute-start(bf16[48,48,128]{2,1,0:T(8,128)(2,1)} %get-tuple-element.137), channel_id=1, source_target_pairs={{0,2},{1,3},{2,0},{3,1},{4,6},{5,7},{6,4},{7,5},{8,10},{9,11},{10,... | collective-permute-start | bytes 1769480 | tf_op jit(solution)/shard_map/ppermute | solution.py:252
  152.3 39.9 %collective-permute-start.17 = (bf16[48,48,128]{2,1,0:T(8,128)(2,1)}, bf16[48,48,128]{2,1,0:T(8,128)(2,1)S(1)}, u32[]{:S(2)}, u32[]{:S(2)}) collective-permute-start(bf16[48,48,128]{2,1,0:T(8,128)(2,1)} %get-tuple-element.128), channel_id=1, source_target_pairs={{0,7},{1,6},{2,5},{3,4},{4,3},{5,2},{6,1},{7,0},{8,15},{9,14},{10,... | collective-permute-start | bytes 1769480 | tf_op jit(solution)/shard_map/ppermute | solution.py:252
  154.2 64.5 %collective-permute-start.11 = (bf16[48,48,128]{2,1,0:T(8,128)(2,1)}, bf16[48,48,128]{2,1,0:T(8,128)(2,1)}, u32[]{:S(2)}, u32[]{:S(2)}) collective-permute-start(bf16[48,48,128]{2,1,0:T(8,128)(2,1)} %get-tuple-element.116), channel_id=1, source_target_pairs={{0,4},{1,5},{2,6},{3,7},{4,0},{5,1},{6,2},{7,3},{8,12},{9,13},{10,... | collective-permute-start | bytes 1769480 | tf_op jit(solution)/shard_map/ppermute | solution.py:252
  160.4 85.9 %collective-permute-start.13 = (bf16[48,48,128]{2,1,0:T(8,128)(2,1)}, bf16[48,48,128]{2,1,0:T(8,128)(2,1)}, u32[]{:S(2)}, u32[]{:S(2)}) collective-permute-start(bf16[48,48,128]{2,1,0:T(8,128)(2,1)} %get-tuple-element.120), channel_id=1, source_target_pairs={{0,5},{1,4},{2,7},{3,6},{4,1},{5,0},{6,3},{7,2},{8,13},{9,12},{10,... | collective-permute-start | bytes 1769480 | tf_op jit(solution)/shard_map/ppermute | solution.py:252
  163.5 57.8 %copy-start.17 = (bf16[48,16,128]{2,1,0:T(8,128)(2,1)S(1)}, bf16[48,16,128]{2,1,0:T(8,128)(2,1)}, u32[]{:S(2)}) copy-start(bf16[48,16,128]{2,1,0:T(8,128)(2,1)} %get-tuple-element.161.rest_0_) | copy-start | bytes 589828
  163.5 57.8 %copy-start.33 = (f32[1,2]{1,0:T(1,128)S(1)}, f32[1,2]{1,0:T(1,128)}, u32[]{:S(2)}) copy-start(f32[1,2]{1,0:T(1,128)} %omegas.7) | copy-start | bytes 28
  203.4 43.0 %collective-permute-start.28 = (bf16[40,48,128]{2,1,0:T(8,128)(2,1)}, bf16[40,48,128]{2,1,0:T(8,128)(2,1)S(1)}, u32[]{:S(2)}, u32[]{:S(2)}) collective-permute-start(bf16[40,48,128]{2,1,0:T(8,128)(2,1)} %get-tuple-element.147), channel_id=1, source_target_pairs={{0,3},{1,2},{2,1},{3,0},{4,7},{5,6},{6,5},{7,4},{8,11},{9,10},{10,... | collective-permute-start | bytes 1474568 | tf_op jit(solution)/shard_map/ppermute | solution.py:252
  203.4 58.0 %collective-permute-start.23 = (bf16[40,48,128]{2,1,0:T(8,128)(2,1)}, bf16[40,48,128]{2,1,0:T(8,128)(2,1)S(1)}, u32[]{:S(2)}, u32[]{:S(2)}) collective-permute-start(bf16[40,48,128]{2,1,0:T(8,128)(2,1)} %get-tuple-element.138), channel_id=1, source_target_pairs={{0,2},{1,3},{2,0},{3,1},{4,6},{5,7},{6,4},{7,5},{8,10},{9,11},{10,... | collective-permute-start | bytes 1474568 | tf_op jit(solution)/shard_map/ppermute | solution.py:252
  204.6 57.6 %collective-permute-start.18 = (bf16[40,48,128]{2,1,0:T(8,128)(2,1)}, bf16[40,48,128]{2,1,0:T(8,128)(2,1)S(1)}, u32[]{:S(2)}, u32[]{:S(2)}) collective-permute-start(bf16[40,48,128]{2,1,0:T(8,128)(2,1)} %get-tuple-element.129), channel_id=1, source_target_pairs={{0,7},{1,6},{2,5},{3,4},{4,3},{5,2},{6,1},{7,0},{8,15},{9,14},{10,... | collective-permute-start | bytes 1474568 | tf_op jit(solution)/shard_map/ppermute | solution.py:252
  218.7 65.1 %collective-permute-start.16 = (bf16[40,48,128]{2,1,0:T(8,128)(2,1)}, bf16[40,48,128]{2,1,0:T(8,128)(2,1)S(1)}, u32[]{:S(2)}, u32[]{:S(2)}) collective-permute-start(bf16[40,48,128]{2,1,0:T(8,128)(2,1)} %get-tuple-element.125), channel_id=1, source_target_pairs={{0,6},{1,7},{2,4},{3,5},{4,2},{5,3},{6,0},{7,1},{8,14},{9,15},{10,... | collective-permute-start | bytes 1474568 | tf_op jit(solution)/shard_map/ppermute | solution.py:252
  235.8 48.1 %copy-start.47 = (bf16[8,48,128]{2,1,0:T(8,128)(2,1)S(1)}, bf16[8,48,128]{2,1,0:T(8,128)(2,1)}, u32[]{:S(2)}) copy-start(bf16[8,48,128]{2,1,0:T(8,128)(2,1)} %get-tuple-element.139) | copy-start | bytes 294916
  235.8 59.2 %copy-start = (bf16[48,48,128]{2,1,0:T(8,128)(2,1)S(1)}, bf16[48,48,128]{2,1,0:T(8,128)(2,1)}, u32[]{:S(2)}) copy-start(bf16[48,48,128]{2,1,0:T(8,128)(2,1)} %get-tuple-element.160.rest_0_) | copy-start | bytes 1769476
  246.3 73.9 %collective-permute-start.34 = (bf16[40,48,128]{2,1,0:T(8,128)(2,1)S(1)}, bf16[40,48,128]{2,1,0:T(8,128)(2,1)S(1)}, u32[]{:S(2)}, u32[]{:S(2)}) collective-permute-start(bf16[40,48,128]{2,1,0:T(8,128)(2,1)S(1)} %copy-done.35), channel_id=1, source_target_pairs={{0,1},{1,0},{2,3},{3,2},{4,5},{5,4},{6,7},{7,6},{8,9},{9,8},{10,11... | collective-permute-start | bytes 1474568 | tf_op jit(solution)/shard_map/ppermute | solution.py:252
  246.4 59.7 %collective-permute-start.14 = (bf16[40,48,128]{2,1,0:T(8,128)(2,1)S(1)}, bf16[40,48,128]{2,1,0:T(8,128)(2,1)S(1)}, u32[]{:S(2)}, u32[]{:S(2)}) collective-permute-start(bf16[40,48,128]{2,1,0:T(8,128)(2,1)S(1)} %copy-done.37), channel_id=1, source_target_pairs={{0,5},{1,4},{2,7},{3,6},{4,1},{5,0},{6,3},{7,2},{8,13},{9,12},{10,... | collective-permute-start | bytes 1474568 | tf_op jit(solution)/shard_map/ppermute | solution.py:252
  261.4 56.2 %collective-permute-start.12 = (bf16[40,48,128]{2,1,0:T(8,128)(2,1)S(1)}, bf16[40,48,128]{2,1,0:T(8,128)(2,1)S(1)}, u32[]{:S(2)}, u32[]{:S(2)}) collective-permute-start(bf16[40,48,128]{2,1,0:T(8,128)(2,1)S(1)} %copy-done.36), channel_id=1, source_target_pairs={{0,4},{1,5},{2,6},{3,7},{4,0},{5,1},{6,2},{7,3},{8,12},{9,13},{10,... | collective-permute-start | bytes 1474568 | tf_op jit(solution)/shard_map/ppermute | solution.py:252
  262.2 58.0 %collective-permute-start.29 = (bf16[8,48,128]{2,1,0:T(8,128)(2,1)S(1)}, bf16[8,48,128]{2,1,0:T(8,128)(2,1)S(1)}, u32[]{:S(2)}, u32[]{:S(2)}) collective-permute-start(bf16[8,48,128]{2,1,0:T(8,128)(2,1)S(1)} %copy-done.48), channel_id=1, source_target_pairs={{0,3},{1,2},{2,1},{3,0},{4,7},{5,6},{6,5},{7,4},{8,11},{9,10},{10,... | collective-permute-start | bytes 294920 | tf_op jit(solution)/shard_map/ppermute | solution.py:252
  283.8 36.5 %collective-permute-start.24 = (bf16[8,48,128]{2,1,0:T(8,128)(2,1)S(1)}, bf16[8,48,128]{2,1,0:T(8,128)(2,1)S(1)}, u32[]{:S(2)}, u32[]{:S(2)}) collective-permute-start(bf16[8,48,128]{2,1,0:T(8,128)(2,1)S(1)} %copy-done.47), channel_id=1, source_target_pairs={{0,2},{1,3},{2,0},{3,1},{4,6},{5,7},{6,4},{7,5},{8,10},{9,11},{10,... | collective-permute-start | bytes 294920 | tf_op jit(solution)/shard_map/ppermute | solution.py:252
  306.0 26.0 %collective-permute-start.33 = (bf16[8,48,128]{2,1,0:T(8,128)(2,1)S(1)}, bf16[8,48,128]{2,1,0:T(8,128)(2,1)S(1)}, u32[]{:S(2)}, u32[]{:S(2)}) collective-permute-start(bf16[8,48,128]{2,1,0:T(8,128)(2,1)S(1)} %copy-done.46), channel_id=1, source_target_pairs={{0,7},{1,6},{2,5},{3,4},{4,3},{5,2},{6,1},{7,0},{8,15},{9,14},{10,... | collective-permute-start | bytes 294920 | tf_op jit(solution)/shard_map/ppermute | solution.py:252
  317.6 14.5 %collective-permute-start.32 = (bf16[8,48,128]{2,1,0:T(8,128)(2,1)S(1)}, bf16[8,48,128]{2,1,0:T(8,128)(2,1)S(1)}, u32[]{:S(2)}, u32[]{:S(2)}) collective-permute-start(bf16[8,48,128]{2,1,0:T(8,128)(2,1)S(1)} %copy-done.45), channel_id=1, source_target_pairs={{0,6},{1,7},{2,4},{3,5},{4,2},{5,3},{6,0},{7,1},{8,14},{9,15},{10,... | collective-permute-start | bytes 294920 | tf_op jit(solution)/shard_map/ppermute | solution.py:252
  320.2 11.9 %collective-permute-start.31 = (bf16[8,48,128]{2,1,0:T(8,128)(2,1)S(1)}, bf16[8,48,128]{2,1,0:T(8,128)(2,1)S(1)}, u32[]{:S(2)}, u32[]{:S(2)}) collective-permute-start(bf16[8,48,128]{2,1,0:T(8,128)(2,1)S(1)} %copy-done.44), channel_id=1, source_target_pairs={{0,5},{1,4},{2,7},{3,6},{4,1},{5,0},{6,3},{7,2},{8,13},{9,12},{10,... | collective-permute-start | bytes 294920 | tf_op jit(solution)/shard_map/ppermute | solution.py:252
  320.2 11.9 %collective-permute-start.19 = (bf16[8,48,128]{2,1,0:T(8,128)(2,1)S(1)}, bf16[8,48,128]{2,1,0:T(8,128)(2,1)S(1)}, u32[]{:S(2)}, u32[]{:S(2)}) collective-permute-start(bf16[8,48,128]{2,1,0:T(8,128)(2,1)S(1)} %copy-done.43), channel_id=1, source_target_pairs={{0,1},{1,0},{2,3},{3,2},{4,5},{5,4},{6,7},{7,6},{8,9},{9,8},{10,11... | collective-permute-start | bytes 294920 | tf_op jit(solution)/shard_map/ppermute | solution.py:252
  320.3 11.8 %collective-permute-start.30 = (bf16[8,48,128]{2,1,0:T(8,128)(2,1)S(1)}, bf16[8,48,128]{2,1,0:T(8,128)(2,1)S(1)}, u32[]{:S(2)}, u32[]{:S(2)}) collective-permute-start(bf16[8,48,128]{2,1,0:T(8,128)(2,1)S(1)} %copy-done.42), channel_id=1, source_target_pairs={{0,4},{1,5},{2,6},{3,7},{4,0},{5,1},{6,2},{7,3},{8,12},{9,13},{10,... | collective-permute-start | bytes 294920 | tf_op jit(solution)/shard_map/ppermute | solution.py:252
  334.3 2.1 collective-permute-start.35
  336.7 6.7 %collective-permute-start.36 = (f32[96,384]{1,0:T(8,128)S(1)}, f32[96,384]{1,0:T(8,128)S(1)}, u32[]{:S(2)}, u32[]{:S(2)}) collective-permute-start(f32[96,384]{1,0:T(8,128)S(1)} %get-tuple-element.172), channel_id=1, source_target_pairs={{0,8},{8,0},{16,24},{24,16},{1,9},{9,1},{17,25},{25,17},{2,10},{10... | collective-permute-start | bytes 442376 | tf_op jit(solution)/shard_map/ppermute | solution.py:252
  338.2 8.8 %collective-permute-start.37 = (f32[96,384]{1,0:T(8,128)S(1)}, f32[96,384]{1,0:T(8,128)S(1)}, u32[]{:S(2)}, u32[]{:S(2)}) collective-permute-start(f32[96,384]{1,0:T(8,128)S(1)} %get-tuple-element.173), channel_id=1, source_target_pairs={{0,16},{8,24},{16,0},{24,8},{1,17},{9,25},{17,1},{25,9},{2,18},{10... | collective-permute-start | bytes 442376 | tf_op jit(solution)/shard_map/ppermute | solution.py:252
  339.8 7.2 %collective-permute-start.38 = (f32[96,384]{1,0:T(8,128)S(1)}, f32[96,384]{1,0:T(8,128)S(1)}, u32[]{:S(2)}, u32[]{:S(2)}) collective-permute-start(f32[96,384]{1,0:T(8,128)S(1)} %get-tuple-element.174), channel_id=1, source_target_pairs={{0,24},{8,16},{16,8},{24,0},{1,25},{9,17},{17,9},{25,1},{2,26},{10... | collective-permute-start | bytes 442376 | tf_op jit(solution)/shard_map/ppermute | solution.py:252
  347.2 4.5 %collective-permute-start.39 = (f32[2,48,96]{2,1,0:T(8,128)S(1)}, f32[2,48,96]{2,1,0:T(8,128)S(1)}, u32[]{:S(2)}, u32[]{:S(2)}) collective-permute-start(f32[2,48,96]{2,1,0:T(8,128)S(1)} %get-tuple-element.176), channel_id=1, source_target_pairs={{0,2},{1,3},{2,0},{3,1},{4,6},{5,7},{6,4},{7,5},{8,10},{9,11},{10,... | collective-permute-start | bytes 110600 | tf_op jit(solution)/shard_map/ppermute | solution.py:252
  347.3 5.4 %collective-permute-start.40 = (f32[2,48,96]{2,1,0:T(8,128)S(1)}, f32[2,48,96]{2,1,0:T(8,128)S(1)}, u32[]{:S(2)}, u32[]{:S(2)}) collective-permute-start(f32[2,48,96]{2,1,0:T(8,128)S(1)} %get-tuple-element.177), channel_id=1, source_target_pairs={{0,4},{1,5},{2,6},{3,7},{4,0},{5,1},{6,2},{7,3},{8,12},{9,13},{10,... | collective-permute-start | bytes 110600 | tf_op jit(solution)/shard_map/ppermute | solution.py:252
  350.2 5.9 %collective-permute-start.41 = (f32[2,48,96]{2,1,0:T(8,128)S(1)}, f32[2,48,96]{2,1,0:T(8,128)S(1)}, u32[]{:S(2)}, u32[]{:S(2)}) collective-permute-start(f32[2,48,96]{2,1,0:T(8,128)S(1)} %get-tuple-element.178), channel_id=1, source_target_pairs={{0,6},{1,7},{2,4},{3,5},{4,2},{5,3},{6,0},{7,1},{8,14},{9,15},{10,... | collective-permute-start | bytes 110600 | tf_op jit(solution)/shard_map/ppermute | solution.py:252
  (43 other events, 312.2 us)

commit v4 on v3

--- a/solution.py
+++ b/solution.py
@@ -258,10 +258,12 @@
     block = 0
     for tile in range(modes // LANES):
         cuts = [(0, span)]
+        if 0 < tile < modes // LANES - 1:
+            cuts = [(0, span // 2), (span // 2, span - span // 2)]
         if tile == modes // LANES - 1 and span > last:
             cuts = [(0, span - last), (span - last, last)]
         if tile == 0 and slices > ROWS:
-            rotations.append((tile, 0, ROWS, [(0, span)], ROWS // 4))
+            rotations.append((tile, 0, ROWS, [(0, span)], ROWS // 2))
             rotations.append((tile, ROWS, slices - ROWS, cuts, ROWS))
             sums += [(tile, low, count, [(0, low), (1 + at, 0)]) for at, (low, count) in enumerate(cuts)]
             block = 1 + len(cuts)
@@ -286,7 +288,7 @@
     rows = jnp.stack([pick(freqs, 0), pick(occupations, 0), pick(smearing, 0)])
     cols = jnp.stack([pick(freqs, 1), pick(occupations, 1), pick(smearing, 1)])
     cols = lax.dynamic_slice_in_dim(cols, place * span, span, axis=1).T
-    far = list(range(parts // 2, parts))
+    far = list(range(parts // 2, parts))[::-1]
     near = list(range(1, parts // 2))
     rotations, sums = plan(modes, slices, span)
     ready, sent, total = [], [], None

time: 358 us -> 346 us (0.966)
  local copies, waits for them, and re-layouts: 31 us -> 17.6 us
  waiting for transfers between devices: 138 us -> 144 us
  starting transfers between devices: 103 us -> 98.7 us
    unnamed x99 -> x69, local copies, waits for them, and re-layouts: 24.7 us -> 9.65 us
    ppermute x42 -> x49, waiting for transfers between devices: 138 us -> 144 us  [swap(): return lax.ppermute(x, axis, [(i, i ^ distance) for i in range(size)])]
    ppermute x42 -> x49, starting transfers between devices: 103 us -> 98.7 us  [swap(): return lax.ppermute(x, axis, [(i, i ^ distance) for i in range(size)])]
    pallas_call x4 -> x5, Pallas kernels: 32.5 us -> 34.3 us  [gram(): pl.pallas_call(functools.partial(gram_kernel, parts, c_counts, fresh), gr...]
  transfers between devices with their start and end apart: 42 -> 49, of which waited for: 14 -> 15; matrix products, arithmetic and copies ran while one was open for 2% -> 2% of each run, Pallas kernels for 19% -> 20%
where the time goes in v4:
time: 346 us; the launch traced here: 345 us
  waiting for transfers between devices  144 us (42%)
  starting transfers between devices  98.7 us (29%)
  Pallas kernels  78.9 us (23%)
  local copies, waits for them, and re-layouts  17.6 us (5%)
  between operations  5.96 us (2%)
    ppermute x49, waiting for transfers between devices, swap(): return lax.ppermute(x, axis, [(i, i ^ distance) for i in range(size)])  144 us
    ppermute x49, starting transfers between devices, swap(): return lax.ppermute(x, axis, [(i, i ^ distance) for i in range(size)])  98.7 us
    pallas_call x4, Pallas kernels, rotate(): pl.pallas_call(functools.partial(rotate_kernel, parts, modes // parts, j_...  44.1 us
    pallas_call x5, Pallas kernels, gram(): pl.pallas_call(functools.partial(gram_kernel, parts, c_counts, fresh), gr...  34.3 us
    unnamed x69, local copies, waits for them, and re-layouts  9.65 us
  transfers between devices with their start and end apart: 49, of which 15 were waited for; matrix products, arithmetic and copies ran while one was open for 2% of the time, Pallas kernels for 20%

profile of v4, /device:TPU:0, one launch (start us, length us, event | category | flops | bytes accessed | tf_op | source)
XLA Modules:
  0.0 345.2 jit_solution(14448906435151746525)
XLA Ops:
  0.0 6.9 %rotate.4 = (bf16[48,16,128]{2,1,0:T(8,128)(2,1)}, bf16[48,16,128]{2,1,0:T(8,128)(2,1)}, bf16[48,16,128]{2,1,0:T(8,128)(2,1)}, bf16[48,16,128]{2,1,0:T(8,128)(2,...) custom-call(s32[1,3]{1,0:T(1,128)} %index.7, ...), custom_call_target="tpu_custom_call" | custom-call | flops 1 | bytes 1 | tf_op jit(solution)/shard_map/rotate/pallas_call | solution.py:83
  7.4 3.7 %collective-permute-start.3 = (bf16[48,16,128]{2,1,0:T(8,128)(2,1)}, bf16[48,16,128]{2,1,0:T(8,128)(2,1)S(1)}, u32[]{:S(2)}, u32[]{:S(2)}) collective-permute-start(bf16[48,16,128]{2,1,0:T(8,128)(2,1)} %get-tuple-element.114), channel_id=1, source_target_pairs={{0,5},{1,4},{2,7},{3,6},{4,1},{5,0},{6,3},{7,2},{8,13},{9,12},{10,... | collective-permute-start | bytes 589832 | tf_op jit(solution)/shard_map/ppermute | solution.py:252
  12.2 2.5 collective-permute-start.2
  15.3 1.9 collective-permute-start.24
  17.2 16.2 %collective-permute-done.3.rest_10_ = bf16[48,16,128]{2,1,0:T(8,128)(2,1)S(1)} collective-permute-done((bf16[48,16,128]{2,1,0:T(8,128)(2,1)}, bf16[48,16,128]{2,1,0:T(8,128)(2,1)S(1)}, u32[]{:S(2)}, u32[]{:S(2)}) %collective-permute-start.3) | collective-permute-done | bytes 196640 | tf_op jit(solution)/shard_map/ppermute | solution.py:252
  34.8 10.2 %rotate.5 = (bf16[48,32,128]{2,1,0:T(8,128)(2,1)}, bf16[48,32,128]{2,1,0:T(8,128)(2,1)}, bf16[48,32,128]{2,1,0:T(8,128)(2,1)}, bf16[48,32,128]{2,1,0:T(8,128)(2,...) custom-call(s32[1,3]{1,0:T(1,128)} %index.7, ...), custom_call_target="tpu_custom_call" | custom-call | flops 1 | bytes 1 | tf_op jit(solution)/shard_map/rotate/pallas_call | solution.py:83
  45.1 3.4 collective-permute-start.8
  51.3 15.4 %collective-permute-done.8.rest_11_ = bf16[48,32,128]{2,1,0:T(8,128)(2,1)S(1)} collective-permute-done((bf16[48,32,128]{2,1,0:T(8,128)(2,1)}, bf16[48,32,128]{2,1,0:T(8,128)(2,1)S(1)}, u32[]{:S(2)}, u32[]{:S(2)}) %collective-permute-start.8) | collective-permute-done | bytes 393248 | tf_op jit(solution)/shard_map/ppermute | solution.py:252
  66.7 2.2 collective-permute-start.7
  69.9 13.4 %rotate.6 = (bf16[24,48,128]{2,1,0:T(8,128)(2,1)}, bf16[24,48,128]{2,1,0:T(8,128)(2,1)}, bf16[24,48,128]{2,1,0:T(8,128)(2,1)}, bf16[24,48,128]{2,1,0:T(8,128)(2,...) custom-call(s32[1,3]{1,0:T(1,128)} %index.7, ...), custom_call_target="tpu_custom_call" | custom-call | flops 1 | bytes 1 | tf_op jit(solution)/shard_map/rotate/pallas_call | solution.py:83
  83.5 18.4 %collective-permute-done.31.rest_7_ = bf16[48,32,128]{2,1,0:T(8,128)(2,1)S(1)} collective-permute-done((bf16[48,32,128]{2,1,0:T(8,128)(2,1)}, bf16[48,32,128]{2,1,0:T(8,128)(2,1)S(1)}, u32[]{:S(2)}, u32[]{:S(2)}) %collective-permute-start.31) | collective-permute-done | bytes 393248 | tf_op jit(solution)/shard_map/ppermute | solution.py:252
  101.8 1.9 collective-permute-start.26
  110.0 14.8 %collective-permute-start.20 = (bf16[24,48,128]{2,1,0:T(8,128)(2,1)}, bf16[24,48,128]{2,1,0:T(8,128)(2,1)}, u32[]{:S(2)}, u32[]{:S(2)}) collective-permute-start(bf16[24,48,128]{2,1,0:T(8,128)(2,1)} %get-tuple-element.152), channel_id=1, source_target_pairs={{0,4},{1,5},{2,6},{3,7},{4,0},{5,1},{6,2},{7,3},{8,12},{9,13},{10,... | collective-permute-start | bytes 884744 | tf_op jit(solution)/shard_map/ppermute | solution.py:252
  124.8 1.6 collective-permute-start.14
  126.5 16.0 %collective-permute-done.17.rest_5_ = bf16[24,48,128]{2,1,0:T(8,128)(2,1)S(1)} collective-permute-done((bf16[24,48,128]{2,1,0:T(8,128)(2,1)}, bf16[24,48,128]{2,1,0:T(8,128)(2,1)S(1)}, u32[]{:S(2)}, u32[]{:S(2)}) %collective-permute-start.17) | collective-permute-done | bytes 294944 | tf_op jit(solution)/shard_map/ppermute | solution.py:252
  142.5 2.2 collective-permute-start.11
  146.4 15.4 %collective-permute-done.20.rest_4_ = bf16[24,48,128]{2,1,0:T(8,128)(2,1)} collective-permute-done((bf16[24,48,128]{2,1,0:T(8,128)(2,1)}, bf16[24,48,128]{2,1,0:T(8,128)(2,1)}, u32[]{:S(2)}, u32[]{:S(2)}) %collective-permute-start.20) | collective-permute-done | bytes 294944 | tf_op jit(solution)/shard_map/ppermute | solution.py:252
  161.8 6.9 %collective-permute-start.27 = (bf16[24,48,128]{2,1,0:T(8,128)(2,1)}, bf16[24,48,128]{2,1,0:T(8,128)(2,1)}, u32[]{:S(2)}, u32[]{:S(2)}) collective-permute-start(bf16[24,48,128]{2,1,0:T(8,128)(2,1)} %get-tuple-element.164), channel_id=1, source_target_pairs={{0,2},{1,3},{2,0},{3,1},{4,6},{5,7},{6,4},{7,5},{8,10},{9,11},{10,... | collective-permute-start | bytes 884744 | tf_op jit(solution)/shard_map/ppermute | solution.py:252
  168.7 6.8 %collective-permute-start.21 = (bf16[24,48,128]{2,1,0:T(8,128)(2,1)}, bf16[24,48,128]{2,1,0:T(8,128)(2,1)}, u32[]{:S(2)}, u32[]{:S(2)}) collective-permute-start(bf16[24,48,128]{2,1,0:T(8,128)(2,1)} %get-tuple-element.153), channel_id=1, source_target_pairs={{0,4},{1,5},{2,6},{3,7},{4,0},{5,1},{6,2},{7,3},{8,12},{9,13},{10,... | collective-permute-start | bytes 884744 | tf_op jit(solution)/shard_map/ppermute | solution.py:252
  175.5 1.7 collective-permute-start.15
  177.1 16.1 %collective-permute-done.18.rest_5_ = bf16[24,48,128]{2,1,0:T(8,128)(2,1)} collective-permute-done((bf16[24,48,128]{2,1,0:T(8,128)(2,1)}, bf16[24,48,128]{2,1,0:T(8,128)(2,1)}, u32[]{:S(2)}, u32[]{:S(2)}) %collective-permute-start.18) | collective-permute-done | bytes 294944 | tf_op jit(solution)/shard_map/ppermute | solution.py:252
  193.2 2.2 collective-permute-start.12
  195.4 1.7 constant_dynamic-slice_fusion.6
  197.1 2.3 gather_fusion
  200.6 13.6 %rotate.7 = (bf16[40,48,128]{2,1,0:T(8,128)(2,1)}, bf16[40,48,128]{2,1,0:T(8,128)(2,1)}, bf16[40,48,128]{2,1,0:T(8,128)(2,1)}, bf16[40,48,128]{2,1,0:T(8,128)(2,...) custom-call(s32[1,3]{1,0:T(1,128)} %index.7, ...), custom_call_target="tpu_custom_call" | custom-call | flops 1 | bytes 1 | tf_op jit(solution)/shard_map/rotate/pallas_call | solution.py:83
  214.4 2.0 collective-permute-start.28
  216.6 3.1 collective-permute-start.19
  227.1 10.5 %gram.5 = (f32[2,192,384]{2,1,0:T(8,128)S(1)}, f32[2,192,384]{2,1,0:T(8,128)S(1)}) custom-call(f32[1,2]{1,0:T(1,128)S(1)} %copy-done.22, bf16[384,384]{1,0:T(8,128)(2,1)S(1)} %bitcast.11, f32[3,384]{1,0:T(4,128)S(1)} %pad_maximum_fusion.row_ref, f32[48,3]{1,0:T(8,128)S(1)} %bitcast.16, bf16[48,16,128]{2,1,0:T(8,128)(2,1)S(1)} %copy-done.6, ...), custom_call_target="tpu_custom_call" | custom-call | flops 5435817984 | bytes 7077888 | tf_op jit(solution)/shard_map/gram/pallas_call | solution.py:175
  237.9 8.0 %collective-permute-done.34.rest_3_ = bf16[40,48,128]{2,1,0:T(8,128)(2,1)S(1)} collective-permute-done((bf16[40,48,128]{2,1,0:T(8,128)(2,1)}, bf16[40,48,128]{2,1,0:T(8,128)(2,1)S(1)}, u32[]{:S(2)}, u32[]{:S(2)}) %collective-permute-start.34) | collective-permute-done | bytes 491552 | tf_op jit(solution)/shard_map/ppermute | solution.py:252
  245.9 2.7 collective-permute-start.16
  248.6 8.3 %collective-permute-done.28.rest_2_ = bf16[40,48,128]{2,1,0:T(8,128)(2,1)S(1)} collective-permute-done((bf16[40,48,128]{2,1,0:T(8,128)(2,1)}, bf16[40,48,128]{2,1,0:T(8,128)(2,1)S(1)}, u32[]{:S(2)}, u32[]{:S(2)}) %collective-permute-start.28) | collective-permute-done | bytes 491552 | tf_op jit(solution)/shard_map/ppermute | solution.py:252
  257.0 1.9 collective-permute-start.13
  258.9 6.2 %gram.6 = (f32[2,192,384]{2,1,0:T(8,128)S(1)}, f32[2,192,384]{2,1,0:T(8,128)S(1)}) custom-call(f32[1,2]{1,0:T(1,128)S(1)} %copy-done.22, bf16[384,384]{1,0:T(8,128)(2,1)S(1)} %bitcast.12, f32[3,384]{1,0:T(4,128)S(1)} %pad_maximum_fusion.row_ref, f32[48,3]{1,0:T(8,128)S(1)} %bitcast.17, ...), custom_call_target="tpu_custom_call", output_to_operand_aliasing={{0}: (12, {}), {1}: (13, {})} | custom-call | flops 2717908992 | bytes 4718592 | tf_op jit(solution)/shard_map/gram/pallas_call | solution.py:175
  265.3 16.9 %collective-permute-done.19.rest_5_ = bf16[40,48,128]{2,1,0:T(8,128)(2,1)S(1)} collective-permute-done((bf16[40,48,128]{2,1,0:T(8,128)(2,1)}, bf16[40,48,128]{2,1,0:T(8,128)(2,1)S(1)}, u32[]{:S(2)}, u32[]{:S(2)}) %collective-permute-start.19) | collective-permute-done | bytes 491552 | tf_op jit(solution)/shard_map/ppermute | solution.py:252
  283.0 6.3 %gram.7 = (f32[2,192,384]{2,1,0:T(8,128)S(1)}, f32[2,192,384]{2,1,0:T(8,128)S(1)}) custom-call(f32[1,2]{1,0:T(1,128)S(1)} %copy-done.22, bf16[384,384]{1,0:T(8,128)(2,1)S(1)} %bitcast.13, f32[3,384]{1,0:T(4,128)S(1)} %pad_maximum_fusion.row_ref, f32[48,3]{1,0:T(8,128)S(1)} %bitcast.18, ...), custom_call_target="tpu_custom_call", output_to_operand_aliasing={{0}: (12, {}), {1}: (13, {})} | custom-call | flops 2717908992 | bytes 4718592 | tf_op jit(solution)/shard_map/gram/pallas_call | solution.py:175
  289.4 6.0 %collective-permute-start.36 = (bf16[8,48,128]{2,1,0:T(8,128)(2,1)S(1)}, bf16[8,48,128]{2,1,0:T(8,128)(2,1)S(1)}, u32[]{:S(2)}, u32[]{:S(2)}) collective-permute-start(bf16[8,48,128]{2,1,0:T(8,128)(2,1)S(1)} %copy-done.31), channel_id=1, source_target_pairs={{0,4},{1,5},{2,6},{3,7},{4,0},{5,1},{6,2},{7,3},{8,12},{9,13},{10,... | collective-permute-start | bytes 294920 | tf_op jit(solution)/shard_map/ppermute | solution.py:252
  295.3 12.1 %collective-permute-start.37 = (bf16[8,48,128]{2,1,0:T(8,128)(2,1)S(1)}, bf16[8,48,128]{2,1,0:T(8,128)(2,1)S(1)}, u32[]{:S(2)}, u32[]{:S(2)}) collective-permute-start(bf16[8,48,128]{2,1,0:T(8,128)(2,1)S(1)} %copy-done.30), channel_id=1, source_target_pairs={{0,5},{1,4},{2,7},{3,6},{4,1},{5,0},{6,3},{7,2},{8,13},{9,12},{10,... | collective-permute-start | bytes 294920 | tf_op jit(solution)/shard_map/ppermute | solution.py:252
  307.4 2.4 collective-permute-start.38
  311.4 9.1 %gram.8 = (f32[2,192,384]{2,1,0:T(8,128)S(1)}, f32[2,192,384]{2,1,0:T(8,128)S(1)}) custom-call(f32[1,2]{1,0:T(1,128)S(1)} %copy-done.22, bf16[384,384]{1,0:T(8,128)(2,1)S(1)} %bitcast.14, f32[3,384]{1,0:T(4,128)S(1)} %pad_maximum_fusion.row_ref, f32[48,3]{1,0:T(8,128)S(1)} %bitcast.19, ...), custom_call_target="tpu_custom_call", output_to_operand_aliasing={{0}: (12, {}), {1}: (13, {})} | custom-call | flops 4529848320 | bytes 6291456 | tf_op jit(solution)/shard_map/gram/pallas_call | solution.py:175
  320.5 2.2 gram.9
  322.9 1.9 collective-permute-done.42.got_ref
  325.1 1.6 collective-permute-start.43
  326.6 1.5 collective-permute-start.44
  328.7 3.1 collective-permute-done.43.rest_1_
  331.7 3.7 %collective-permute-done.44.rest_2_ = f32[96,384]{1,0:T(8,128)S(1)} collective-permute-done((f32[96,384]{1,0:T(8,128)S(1)}, f32[96,384]{1,0:T(8,128)S(1)}, u32[]{:S(2)}, u32[]{:S(2)}) %collective-permute-start.44) | collective-permute-done | bytes 147488 | tf_op jit(solution)/shard_map/ppermute | solution.py:252
  336.9 1.8 collective-permute-start.47
  340.3 2.7 collective-permute-done.47
  342.9 1.6 collective-permute-done.48
  (145 shorter events, 26.5 us)
Async XLA Ops:
  6.9 7.7 %collective-permute-start = (bf16[48,16,128]{2,1,0:T(8,128)(2,1)}, bf16[48,16,128]{2,1,0:T(8,128)(2,1)S(1)}, u32[]{:S(2)}, u32[]{:S(2)}) collective-permute-start(bf16[48,16,128]{2,1,0:T(8,128)(2,1)} %get-tuple-element.109), channel_id=1, source_target_pairs={{0,1},{1,0},{2,3},{3,2},{4,5},{5,4},{6,7},{7,6},{8,9},{9,8},{10,11... | collective-permute-start | bytes 589832 | tf_op jit(solution)/shard_map/ppermute | solution.py:252
  7.4 26.0 %collective-permute-start.3 = (bf16[48,16,128]{2,1,0:T(8,128)(2,1)}, bf16[48,16,128]{2,1,0:T(8,128)(2,1)S(1)}, u32[]{:S(2)}, u32[]{:S(2)}) collective-permute-start(bf16[48,16,128]{2,1,0:T(8,128)(2,1)} %get-tuple-element.114), channel_id=1, source_target_pairs={{0,5},{1,4},{2,7},{3,6},{4,1},{5,0},{6,3},{7,2},{8,13},{9,12},{10,... | collective-permute-start | bytes 589832 | tf_op jit(solution)/shard_map/ppermute | solution.py:252
  11.1 33.9 %collective-permute-start.1 = (bf16[48,16,128]{2,1,0:T(8,128)(2,1)}, bf16[48,16,128]{2,1,0:T(8,128)(2,1)S(1)}, u32[]{:S(2)}, u32[]{:S(2)}) collective-permute-start(bf16[48,16,128]{2,1,0:T(8,128)(2,1)} %get-tuple-element.112), channel_id=1, source_target_pairs={{0,7},{1,6},{2,5},{3,4},{4,3},{5,2},{6,1},{7,0},{8,15},{9,14},{10,... | collective-permute-start | bytes 589832 | tf_op jit(solution)/shard_map/ppermute | solution.py:252
  12.2 36.3 %collective-permute-start.2 = (bf16[48,16,128]{2,1,0:T(8,128)(2,1)}, bf16[48,16,128]{2,1,0:T(8,128)(2,1)S(1)}, u32[]{:S(2)}, u32[]{:S(2)}) collective-permute-start(bf16[48,16,128]{2,1,0:T(8,128)(2,1)} %get-tuple-element.113), channel_id=1, source_target_pairs={{0,6},{1,7},{2,4},{3,5},{4,2},{5,3},{6,0},{7,1},{8,14},{9,15},{10,... | collective-permute-start | bytes 589832 | tf_op jit(solution)/shard_map/ppermute | solution.py:252
  14.6 33.8 %collective-permute-start.4 = (bf16[48,16,128]{2,1,0:T(8,128)(2,1)}, bf16[48,16,128]{2,1,0:T(8,128)(2,1)S(1)}, u32[]{:S(2)}, u32[]{:S(2)}) collective-permute-start(bf16[48,16,128]{2,1,0:T(8,128)(2,1)} %get-tuple-element.115), channel_id=1, source_target_pairs={{0,4},{1,5},{2,6},{3,7},{4,0},{5,1},{6,2},{7,3},{8,12},{9,13},{10,... | collective-permute-start | bytes 589832 | tf_op jit(solution)/shard_map/ppermute | solution.py:252
  15.3 33.3 %collective-permute-start.24 = (bf16[48,16,128]{2,1,0:T(8,128)(2,1)}, bf16[48,16,128]{2,1,0:T(8,128)(2,1)S(1)}, u32[]{:S(2)}, u32[]{:S(2)}) collective-permute-start(bf16[48,16,128]{2,1,0:T(8,128)(2,1)} %get-tuple-element.161), channel_id=1, source_target_pairs={{0,2},{1,3},{2,0},{3,1},{4,6},{5,7},{6,4},{7,5},{8,10},{9,11},{10,... | collective-permute-start | bytes 589832 | tf_op jit(solution)/shard_map/ppermute | solution.py:252
  34.1 14.8 %collective-permute-start.30 = (bf16[48,16,128]{2,1,0:T(8,128)(2,1)}, bf16[48,16,128]{2,1,0:T(8,128)(2,1)S(1)}, u32[]{:S(2)}, u32[]{:S(2)}) collective-permute-start(bf16[48,16,128]{2,1,0:T(8,128)(2,1)} %get-tuple-element.172), channel_id=1, source_target_pairs={{0,3},{1,2},{2,1},{3,0},{4,7},{5,6},{6,5},{7,4},{8,11},{9,10},{10,... | collective-permute-start | bytes 589832 | tf_op jit(solution)/shard_map/ppermute | solution.py:252
  45.1 21.6 %collective-permute-start.8 = (bf16[48,32,128]{2,1,0:T(8,128)(2,1)}, bf16[48,32,128]{2,1,0:T(8,128)(2,1)S(1)}, u32[]{:S(2)}, u32[]{:S(2)}) collective-permute-start(bf16[48,32,128]{2,1,0:T(8,128)(2,1)} %get-tuple-element.124), channel_id=1, source_target_pairs={{0,5},{1,4},{2,7},{3,6},{4,1},{5,0},{6,3},{7,2},{8,13},{9,12},{10,... | collective-permute-start | bytes 1179656 | tf_op jit(solution)/shard_map/ppermute | solution.py:252
  48.5 20.4 %collective-permute-start.5 = (bf16[48,32,128]{2,1,0:T(8,128)(2,1)}, bf16[48,32,128]{2,1,0:T(8,128)(2,1)S(1)}, u32[]{:S(2)}, u32[]{:S(2)}) collective-permute-start(bf16[48,32,128]{2,1,0:T(8,128)(2,1)} %get-tuple-element.116), channel_id=1, source_target_pairs={{0,1},{1,0},{2,3},{3,2},{4,5},{5,4},{6,7},{7,6},{8,9},{9,8},{10,11... | collective-permute-start | bytes 1179656 | tf_op jit(solution)/shard_map/ppermute | solution.py:252
  48.6 34.8 %collective-permute-start.25 = (bf16[48,32,128]{2,1,0:T(8,128)(2,1)}, bf16[48,32,128]{2,1,0:T(8,128)(2,1)S(1)}, u32[]{:S(2)}, u32[]{:S(2)}) collective-permute-start(bf16[48,32,128]{2,1,0:T(8,128)(2,1)} %get-tuple-element.162), channel_id=1, source_target_pairs={{0,2},{1,3},{2,0},{3,1},{4,6},{5,7},{6,4},{7,5},{8,10},{9,11},{10,... | collective-permute-start | bytes 1179656 | tf_op jit(solution)/shard_map/ppermute | solution.py:252
  49.6 52.2 %collective-permute-start.31 = (bf16[48,32,128]{2,1,0:T(8,128)(2,1)}, bf16[48,32,128]{2,1,0:T(8,128)(2,1)S(1)}, u32[]{:S(2)}, u32[]{:S(2)}) collective-permute-start(bf16[48,32,128]{2,1,0:T(8,128)(2,1)} %get-tuple-element.173), channel_id=1, source_target_pairs={{0,3},{1,2},{2,1},{3,0},{4,7},{5,6},{6,5},{7,4},{8,11},{9,10},{10,... | collective-permute-start | bytes 1179656 | tf_op jit(solution)/shard_map/ppermute | solution.py:252
  51.1 50.7 %collective-permute-start.9 = (bf16[48,32,128]{2,1,0:T(8,128)(2,1)}, bf16[48,32,128]{2,1,0:T(8,128)(2,1)S(1)}, u32[]{:S(2)}, u32[]{:S(2)}) collective-permute-start(bf16[48,32,128]{2,1,0:T(8,128)(2,1)} %get-tuple-element.126), channel_id=1, source_target_pairs={{0,4},{1,5},{2,6},{3,7},{4,0},{5,1},{6,2},{7,3},{8,12},{9,13},{10,... | collective-permute-start | bytes 1179656 | tf_op jit(solution)/shard_map/ppermute | solution.py:252
  66.7 43.3 %collective-permute-start.7 = (bf16[48,32,128]{2,1,0:T(8,128)(2,1)}, bf16[48,32,128]{2,1,0:T(8,128)(2,1)S(1)}, u32[]{:S(2)}, u32[]{:S(2)}) collective-permute-start(bf16[48,32,128]{2,1,0:T(8,128)(2,1)} %get-tuple-element.122), channel_id=1, source_target_pairs={{0,6},{1,7},{2,4},{3,5},{4,2},{5,3},{6,0},{7,1},{8,14},{9,15},{10,... | collective-permute-start | bytes 1179656 | tf_op jit(solution)/shard_map/ppermute | solution.py:252
  68.9 41.1 %collective-permute-start.6 = (bf16[48,32,128]{2,1,0:T(8,128)(2,1)}, bf16[48,32,128]{2,1,0:T(8,128)(2,1)S(1)}, u32[]{:S(2)}, u32[]{:S(2)}) collective-permute-start(bf16[48,32,128]{2,1,0:T(8,128)(2,1)} %get-tuple-element.120), channel_id=1, source_target_pairs={{0,7},{1,6},{2,5},{3,4},{4,3},{5,2},{6,1},{7,0},{8,15},{9,14},{10,... | collective-permute-start | bytes 1179656 | tf_op jit(solution)/shard_map/ppermute | solution.py:252
  83.4 59.1 %collective-permute-start.17 = (bf16[24,48,128]{2,1,0:T(8,128)(2,1)}, bf16[24,48,128]{2,1,0:T(8,128)(2,1)S(1)}, u32[]{:S(2)}, u32[]{:S(2)}) collective-permute-start(bf16[24,48,128]{2,1,0:T(8,128)(2,1)} %get-tuple-element.146), channel_id=1, source_target_pairs={{0,5},{1,4},{2,7},{3,6},{4,1},{5,0},{6,3},{7,2},{8,13},{9,12},{10,... | collective-permute-start | bytes 884744 | tf_op jit(solution)/shard_map/ppermute | solution.py:252
  101.8 42.9 %collective-permute-start.32 = (bf16[24,48,128]{2,1,0:T(8,128)(2,1)}, bf16[24,48,128]{2,1,0:T(8,128)(2,1)S(1)}, u32[]{:S(2)}, u32[]{:S(2)}) collective-permute-start(bf16[24,48,128]{2,1,0:T(8,128)(2,1)} %get-tuple-element.174), channel_id=1, source_target_pairs={{0,3},{1,2},{2,1},{3,0},{4,7},{5,6},{6,5},{7,4},{8,11},{9,10},{10,... | collective-permute-start | bytes 884744 | tf_op jit(solution)/shard_map/ppermute | solution.py:252
  101.8 43.0 %collective-permute-start.26 = (bf16[24,48,128]{2,1,0:T(8,128)(2,1)}, bf16[24,48,128]{2,1,0:T(8,128)(2,1)}, u32[]{:S(2)}, u32[]{:S(2)}) collective-permute-start(bf16[24,48,128]{2,1,0:T(8,128)(2,1)} %get-tuple-element.163), channel_id=1, source_target_pairs={{0,2},{1,3},{2,0},{3,1},{4,6},{5,7},{6,4},{7,5},{8,10},{9,11},{10,... | collective-permute-start | bytes 884744 | tf_op jit(solution)/shard_map/ppermute | solution.py:252
  110.0 51.8 %collective-permute-start.20 = (bf16[24,48,128]{2,1,0:T(8,128)(2,1)}, bf16[24,48,128]{2,1,0:T(8,128)(2,1)}, u32[]{:S(2)}, u32[]{:S(2)}) collective-permute-start(bf16[24,48,128]{2,1,0:T(8,128)(2,1)} %get-tuple-element.152), channel_id=1, source_target_pairs={{0,4},{1,5},{2,6},{3,7},{4,0},{5,1},{6,2},{7,3},{8,12},{9,13},{10,... | collective-permute-start | bytes 884744 | tf_op jit(solution)/shard_map/ppermute | solution.py:252
  124.8 37.0 %collective-permute-start.14 = (bf16[24,48,128]{2,1,0:T(8,128)(2,1)}, bf16[24,48,128]{2,1,0:T(8,128)(2,1)}, u32[]{:S(2)}, u32[]{:S(2)}) collective-permute-start(bf16[24,48,128]{2,1,0:T(8,128)(2,1)} %get-tuple-element.140), channel_id=1, source_target_pairs={{0,6},{1,7},{2,4},{3,5},{4,2},{5,3},{6,0},{7,1},{8,14},{9,15},{10,... | collective-permute-start | bytes 884744 | tf_op jit(solution)/shard_map/ppermute | solution.py:252
  142.5 26.2 %collective-permute-start.11 = (bf16[24,48,128]{2,1,0:T(8,128)(2,1)}, bf16[24,48,128]{2,1,0:T(8,128)(2,1)}, u32[]{:S(2)}, u32[]{:S(2)}) collective-permute-start(bf16[24,48,128]{2,1,0:T(8,128)(2,1)} %get-tuple-element.134), channel_id=1, source_target_pairs={{0,7},{1,6},{2,5},{3,4},{4,3},{5,2},{6,1},{7,0},{8,15},{9,14},{10,... | collective-permute-start | bytes 884744 | tf_op jit(solution)/shard_map/ppermute | solution.py:252
  144.7 30.8 %collective-permute-start.10 = (bf16[24,48,128]{2,1,0:T(8,128)(2,1)}, bf16[24,48,128]{2,1,0:T(8,128)(2,1)}, u32[]{:S(2)}, u32[]{:S(2)}) collective-permute-start(bf16[24,48,128]{2,1,0:T(8,128)(2,1)} %get-tuple-element.127), channel_id=1, source_target_pairs={{0,1},{1,0},{2,3},{3,2},{4,5},{5,4},{6,7},{7,6},{8,9},{9,8},{10,11... | collective-permute-start | bytes 884744 | tf_op jit(solution)/shard_map/ppermute | solution.py:252
  144.8 48.4 %collective-permute-start.18 = (bf16[24,48,128]{2,1,0:T(8,128)(2,1)}, bf16[24,48,128]{2,1,0:T(8,128)(2,1)}, u32[]{:S(2)}, u32[]{:S(2)}) collective-permute-start(bf16[24,48,128]{2,1,0:T(8,128)(2,1)} %get-tuple-element.147), channel_id=1, source_target_pairs={{0,5},{1,4},{2,7},{3,6},{4,1},{5,0},{6,3},{7,2},{8,13},{9,12},{10,... | collective-permute-start | bytes 884744 | tf_op jit(solution)/shard_map/ppermute | solution.py:252
  161.8 52.5 %collective-permute-start.33 = (bf16[24,48,128]{2,1,0:T(8,128)(2,1)}, bf16[24,48,128]{2,1,0:T(8,128)(2,1)}, u32[]{:S(2)}, u32[]{:S(2)}) collective-permute-start(bf16[24,48,128]{2,1,0:T(8,128)(2,1)} %get-tuple-element.175), channel_id=1, source_target_pairs={{0,3},{1,2},{2,1},{3,0},{4,7},{5,6},{6,5},{7,4},{8,11},{9,10},{10,... | collective-permute-start | bytes 884744 | tf_op jit(solution)/shard_map/ppermute | solution.py:252
  161.8 52.5 %collective-permute-start.27 = (bf16[24,48,128]{2,1,0:T(8,128)(2,1)}, bf16[24,48,128]{2,1,0:T(8,128)(2,1)}, u32[]{:S(2)}, u32[]{:S(2)}) collective-permute-start(bf16[24,48,128]{2,1,0:T(8,128)(2,1)} %get-tuple-element.164), channel_id=1, source_target_pairs={{0,2},{1,3},{2,0},{3,1},{4,6},{5,7},{6,4},{7,5},{8,10},{9,11},{10,... | collective-permute-start | bytes 884744 | tf_op jit(solution)/shard_map/ppermute | solution.py:252
  168.7 45.5 %collective-permute-start.21 = (bf16[24,48,128]{2,1,0:T(8,128)(2,1)}, bf16[24,48,128]{2,1,0:T(8,128)(2,1)}, u32[]{:S(2)}, u32[]{:S(2)}) collective-permute-start(bf16[24,48,128]{2,1,0:T(8,128)(2,1)} %get-tuple-element.153), channel_id=1, source_target_pairs={{0,4},{1,5},{2,6},{3,7},{4,0},{5,1},{6,2},{7,3},{8,12},{9,13},{10,... | collective-permute-start | bytes 884744 | tf_op jit(solution)/shard_map/ppermute | solution.py:252
  175.5 40.9 %collective-permute-start.15 = (bf16[24,48,128]{2,1,0:T(8,128)(2,1)}, bf16[24,48,128]{2,1,0:T(8,128)(2,1)}, u32[]{:S(2)}, u32[]{:S(2)}) collective-permute-start(bf16[24,48,128]{2,1,0:T(8,128)(2,1)} %get-tuple-element.141), channel_id=1, source_target_pairs={{0,6},{1,7},{2,4},{3,5},{4,2},{5,3},{6,0},{7,1},{8,14},{9,15},{10,... | collective-permute-start | bytes 884744 | tf_op jit(solution)/shard_map/ppermute | solution.py:252
  193.2 23.4 %collective-permute-start.12 = (bf16[24,48,128]{2,1,0:T(8,128)(2,1)}, bf16[24,48,128]{2,1,0:T(8,128)(2,1)}, u32[]{:S(2)}, u32[]{:S(2)}) collective-permute-start(bf16[24,48,128]{2,1,0:T(8,128)(2,1)} %get-tuple-element.135), channel_id=1, source_target_pairs={{0,7},{1,6},{2,5},{3,4},{4,3},{5,2},{6,1},{7,0},{8,15},{9,14},{10,... | collective-permute-start | bytes 884744 | tf_op jit(solution)/shard_map/ppermute | solution.py:252
  214.2 23.5 %collective-permute-start.41 = (bf16[24,48,128]{2,1,0:T(8,128)(2,1)}, bf16[24,48,128]{2,1,0:T(8,128)(2,1)S(1)}, u32[]{:S(2)}, u32[]{:S(2)}) collective-permute-start(bf16[24,48,128]{2,1,0:T(8,128)(2,1)} %get-tuple-element.191), channel_id=1, source_target_pairs={{0,1},{1,0},{2,3},{3,2},{4,5},{5,4},{6,7},{7,6},{8,9},{9,8},{10,11... | collective-permute-start | bytes 884744 | tf_op jit(solution)/shard_map/ppermute | solution.py:252
  214.3 31.6 %collective-permute-start.34 = (bf16[40,48,128]{2,1,0:T(8,128)(2,1)}, bf16[40,48,128]{2,1,0:T(8,128)(2,1)S(1)}, u32[]{:S(2)}, u32[]{:S(2)}) collective-permute-start(bf16[40,48,128]{2,1,0:T(8,128)(2,1)} %get-tuple-element.176), channel_id=1, source_target_pairs={{0,3},{1,2},{2,1},{3,0},{4,7},{5,6},{6,5},{7,4},{8,11},{9,10},{10,... | collective-permute-start | bytes 1474568 | tf_op jit(solution)/shard_map/ppermute | solution.py:252
  214.4 42.6 %collective-permute-start.28 = (bf16[40,48,128]{2,1,0:T(8,128)(2,1)}, bf16[40,48,128]{2,1,0:T(8,128)(2,1)S(1)}, u32[]{:S(2)}, u32[]{:S(2)}) collective-permute-start(bf16[40,48,128]{2,1,0:T(8,128)(2,1)} %get-tuple-element.165), channel_id=1, source_target_pairs={{0,2},{1,3},{2,0},{3,1},{4,6},{5,7},{6,4},{7,5},{8,10},{9,11},{10,... | collective-permute-start | bytes 1474568 | tf_op jit(solution)/shard_map/ppermute | solution.py:252
  216.4 48.7 %collective-permute-start.22 = (bf16[40,48,128]{2,1,0:T(8,128)(2,1)}, bf16[40,48,128]{2,1,0:T(8,128)(2,1)S(1)}, u32[]{:S(2)}, u32[]{:S(2)}) collective-permute-start(bf16[40,48,128]{2,1,0:T(8,128)(2,1)} %get-tuple-element.154), channel_id=1, source_target_pairs={{0,4},{1,5},{2,6},{3,7},{4,0},{5,1},{6,2},{7,3},{8,12},{9,13},{10,... | collective-permute-start | bytes 1474568 | tf_op jit(solution)/shard_map/ppermute | solution.py:252
  216.6 65.5 %collective-permute-start.19 = (bf16[40,48,128]{2,1,0:T(8,128)(2,1)}, bf16[40,48,128]{2,1,0:T(8,128)(2,1)S(1)}, u32[]{:S(2)}, u32[]{:S(2)}) collective-permute-start(bf16[40,48,128]{2,1,0:T(8,128)(2,1)} %get-tuple-element.148), channel_id=1, source_target_pairs={{0,5},{1,4},{2,7},{3,6},{4,1},{5,0},{6,3},{7,2},{8,13},{9,12},{10,... | collective-permute-start | bytes 1474568 | tf_op jit(solution)/shard_map/ppermute | solution.py:252
  237.7 69.7 %collective-permute-start.40 = (bf16[40,48,128]{2,1,0:T(8,128)(2,1)S(1)}, bf16[40,48,128]{2,1,0:T(8,128)(2,1)S(1)}, u32[]{:S(2)}, u32[]{:S(2)}) collective-permute-start(bf16[40,48,128]{2,1,0:T(8,128)(2,1)S(1)} %copy-done.24), channel_id=1, source_target_pairs={{0,1},{1,0},{2,3},{3,2},{4,5},{5,4},{6,7},{7,6},{8,9},{9,8},{10,11... | collective-permute-start | bytes 1474568 | tf_op jit(solution)/shard_map/ppermute | solution.py:252
  245.9 43.5 %collective-permute-start.16 = (bf16[40,48,128]{2,1,0:T(8,128)(2,1)S(1)}, bf16[40,48,128]{2,1,0:T(8,128)(2,1)S(1)}, u32[]{:S(2)}, u32[]{:S(2)}) collective-permute-start(bf16[40,48,128]{2,1,0:T(8,128)(2,1)S(1)} %copy-done.26), channel_id=1, source_target_pairs={{0,6},{1,7},{2,4},{3,5},{4,2},{5,3},{6,0},{7,1},{8,14},{9,15},{10,... | collective-permute-start | bytes 1474568 | tf_op jit(solution)/shard_map/ppermute | solution.py:252
  257.0 38.4 %collective-permute-start.13 = (bf16[40,48,128]{2,1,0:T(8,128)(2,1)S(1)}, bf16[40,48,128]{2,1,0:T(8,128)(2,1)S(1)}, u32[]{:S(2)}, u32[]{:S(2)}) collective-permute-start(bf16[40,48,128]{2,1,0:T(8,128)(2,1)S(1)} %copy-done.25), channel_id=1, source_target_pairs={{0,7},{1,6},{2,5},{3,4},{4,3},{5,2},{6,1},{7,0},{8,15},{9,14},{10,... | collective-permute-start | bytes 1474568 | tf_op jit(solution)/shard_map/ppermute | solution.py:252
  265.2 44.6 %collective-permute-start.35 = (bf16[8,48,128]{2,1,0:T(8,128)(2,1)S(1)}, bf16[8,48,128]{2,1,0:T(8,128)(2,1)S(1)}, u32[]{:S(2)}, u32[]{:S(2)}) collective-permute-start(bf16[8,48,128]{2,1,0:T(8,128)(2,1)S(1)} %copy-done.33), channel_id=1, source_target_pairs={{0,3},{1,2},{2,1},{3,0},{4,7},{5,6},{6,5},{7,4},{8,11},{9,10},{10,... | collective-permute-start | bytes 294920 | tf_op jit(solution)/shard_map/ppermute | solution.py:252
  282.1 27.7 %collective-permute-start.29 = (bf16[8,48,128]{2,1,0:T(8,128)(2,1)S(1)}, bf16[8,48,128]{2,1,0:T(8,128)(2,1)S(1)}, u32[]{:S(2)}, u32[]{:S(2)}) collective-permute-start(bf16[8,48,128]{2,1,0:T(8,128)(2,1)S(1)} %copy-done.32), channel_id=1, source_target_pairs={{0,2},{1,3},{2,0},{3,1},{4,6},{5,7},{6,4},{7,5},{8,10},{9,11},{10,... | collective-permute-start | bytes 294920 | tf_op jit(solution)/shard_map/ppermute | solution.py:252
  289.4 31.1 %collective-permute-start.36 = (bf16[8,48,128]{2,1,0:T(8,128)(2,1)S(1)}, bf16[8,48,128]{2,1,0:T(8,128)(2,1)S(1)}, u32[]{:S(2)}, u32[]{:S(2)}) collective-permute-start(bf16[8,48,128]{2,1,0:T(8,128)(2,1)S(1)} %copy-done.31), channel_id=1, source_target_pairs={{0,4},{1,5},{2,6},{3,7},{4,0},{5,1},{6,2},{7,3},{8,12},{9,13},{10,... | collective-permute-start | bytes 294920 | tf_op jit(solution)/shard_map/ppermute | solution.py:252
  295.3 25.1 %collective-permute-start.37 = (bf16[8,48,128]{2,1,0:T(8,128)(2,1)S(1)}, bf16[8,48,128]{2,1,0:T(8,128)(2,1)S(1)}, u32[]{:S(2)}, u32[]{:S(2)}) collective-permute-start(bf16[8,48,128]{2,1,0:T(8,128)(2,1)S(1)} %copy-done.30), channel_id=1, source_target_pairs={{0,5},{1,4},{2,7},{3,6},{4,1},{5,0},{6,3},{7,2},{8,13},{9,12},{10,... | collective-permute-start | bytes 294920 | tf_op jit(solution)/shard_map/ppermute | solution.py:252
  307.4 13.1 %collective-permute-start.38 = (bf16[8,48,128]{2,1,0:T(8,128)(2,1)S(1)}, bf16[8,48,128]{2,1,0:T(8,128)(2,1)S(1)}, u32[]{:S(2)}, u32[]{:S(2)}) collective-permute-start(bf16[8,48,128]{2,1,0:T(8,128)(2,1)S(1)} %copy-done.29), channel_id=1, source_target_pairs={{0,6},{1,7},{2,4},{3,5},{4,2},{5,3},{6,0},{7,1},{8,14},{9,15},{10,... | collective-permute-start | bytes 294920 | tf_op jit(solution)/shard_map/ppermute | solution.py:252
  309.8 10.7 %collective-permute-start.23 = (bf16[8,48,128]{2,1,0:T(8,128)(2,1)S(1)}, bf16[8,48,128]{2,1,0:T(8,128)(2,1)S(1)}, u32[]{:S(2)}, u32[]{:S(2)}) collective-permute-start(bf16[8,48,128]{2,1,0:T(8,128)(2,1)S(1)} %copy-done.28), channel_id=1, source_target_pairs={{0,1},{1,0},{2,3},{3,2},{4,5},{5,4},{6,7},{7,6},{8,9},{9,8},{10,11... | collective-permute-start | bytes 294920 | tf_op jit(solution)/shard_map/ppermute | solution.py:252
  309.8 10.7 %collective-permute-start.39 = (bf16[8,48,128]{2,1,0:T(8,128)(2,1)S(1)}, bf16[8,48,128]{2,1,0:T(8,128)(2,1)S(1)}, u32[]{:S(2)}, u32[]{:S(2)}) collective-permute-start(bf16[8,48,128]{2,1,0:T(8,128)(2,1)S(1)} %copy-done.27), channel_id=1, source_target_pairs={{0,7},{1,6},{2,5},{3,4},{4,3},{5,2},{6,1},{7,0},{8,15},{9,14},{10,... | collective-permute-start | bytes 294920 | tf_op jit(solution)/shard_map/ppermute | solution.py:252
  325.1 6.7 %collective-permute-start.43 = (f32[96,384]{1,0:T(8,128)S(1)}, f32[96,384]{1,0:T(8,128)S(1)}, u32[]{:S(2)}, u32[]{:S(2)}) collective-permute-start(f32[96,384]{1,0:T(8,128)S(1)} %get-tuple-element.206), channel_id=1, source_target_pairs={{0,8},{8,0},{16,24},{24,16},{1,9},{9,1},{17,25},{25,17},{2,10},{10... | collective-permute-start | bytes 442376 | tf_op jit(solution)/shard_map/ppermute | solution.py:252
  326.6 8.8 %collective-permute-start.44 = (f32[96,384]{1,0:T(8,128)S(1)}, f32[96,384]{1,0:T(8,128)S(1)}, u32[]{:S(2)}, u32[]{:S(2)}) collective-permute-start(f32[96,384]{1,0:T(8,128)S(1)} %get-tuple-element.207), channel_id=1, source_target_pairs={{0,16},{8,24},{16,0},{24,8},{1,17},{9,25},{17,1},{25,9},{2,18},{10... | collective-permute-start | bytes 442376 | tf_op jit(solution)/shard_map/ppermute | solution.py:252
  328.2 7.2 %collective-permute-start.45 = (f32[96,384]{1,0:T(8,128)S(1)}, f32[96,384]{1,0:T(8,128)S(1)}, u32[]{:S(2)}, u32[]{:S(2)}) collective-permute-start(f32[96,384]{1,0:T(8,128)S(1)} %get-tuple-element.208), channel_id=1, source_target_pairs={{0,24},{8,16},{16,8},{24,0},{1,25},{9,17},{17,9},{25,1},{2,26},{10... | collective-permute-start | bytes 442376 | tf_op jit(solution)/shard_map/ppermute | solution.py:252
  335.6 4.7 %collective-permute-start.46 = (f32[2,48,96]{2,1,0:T(8,128)S(1)}, f32[2,48,96]{2,1,0:T(8,128)S(1)}, u32[]{:S(2)}, u32[]{:S(2)}) collective-permute-start(f32[2,48,96]{2,1,0:T(8,128)S(1)} %get-tuple-element.210), channel_id=1, source_target_pairs={{0,2},{1,3},{2,0},{3,1},{4,6},{5,7},{6,4},{7,5},{8,10},{9,11},{10,... | collective-permute-start | bytes 110600 | tf_op jit(solution)/shard_map/ppermute | solution.py:252
  336.9 6.0 %collective-permute-start.47 = (f32[2,48,96]{2,1,0:T(8,128)S(1)}, f32[2,48,96]{2,1,0:T(8,128)S(1)}, u32[]{:S(2)}, u32[]{:S(2)}) collective-permute-start(f32[2,48,96]{2,1,0:T(8,128)S(1)} %get-tuple-element.211), channel_id=1, source_target_pairs={{0,4},{1,5},{2,6},{3,7},{4,0},{5,1},{6,2},{7,3},{8,12},{9,13},{10,... | collective-permute-start | bytes 110600 | tf_op jit(solution)/shard_map/ppermute | solution.py:252
  338.6 5.9 %collective-permute-start.48 = (f32[2,48,96]{2,1,0:T(8,128)S(1)}, f32[2,48,96]{2,1,0:T(8,128)S(1)}, u32[]{:S(2)}, u32[]{:S(2)}) collective-permute-start(f32[2,48,96]{2,1,0:T(8,128)S(1)} %get-tuple-element.212), channel_id=1, source_target_pairs={{0,6},{1,7},{2,4},{3,5},{4,2},{5,3},{6,0},{7,1},{8,14},{9,15},{10,... | collective-permute-start | bytes 110600 | tf_op jit(solution)/shard_map/ppermute | solution.py:252
  (35 other events, 610.3 us)

commit v5 on v4

--- a/solution.py
+++ b/solution.py
@@ -99,7 +99,7 @@
                 pltpu.VMEM((modes, rows), BF16),
                 pltpu.VMEM((parts * j_count, rows), BF16),
                 pltpu.VMEM((rows, step * LANES), BF16),
-                pltpu.VMEM((parts * j_count * ROWS, LANES), F32),
+                pltpu.VMEM((parts * j_count * ROWS + ROWS, LANES), F32),
             ],
         ),
         out_shape=[
@@ -195,8 +195,8 @@
         input_output_aliases={} if fresh else {4 + len(pieces): 0, 5 + len(pieces): 1},
         compiler_params=pltpu.CompilerParams(vmem_limit_bytes=VMEM // 2),
         cost_estimate=pl.CostEstimate(
-            flops=int(1 * 6 * modes * modes * j_count * LANES),
-            bytes_accessed=int(1 * (2 * modes * j_count * LANES + 16 * modes * modes)),
+            flops=6 * modes * modes * j_count * LANES,
+            bytes_accessed=2 * modes * j_count * LANES + 16 * modes * modes,
             transcendentals=0,
         ),
         name="gram",

time: 346 us -> 346 us (level)
  transfers between devices with their start and end apart: 49 -> 49, of which waited for: 15 -> 14; matrix products, arithmetic and copies ran while one was open for 2% -> 2% of each run, Pallas kernels for 20% -> 20%
where the time goes in v5:
time: 346 us; the launch traced here: 345 us
  waiting for transfers between devices  144 us (42%)
  starting transfers between devices  98.8 us (29%)
  Pallas kernels  78.9 us (23%)
  local copies, waits for them, and re-layouts  17.5 us (5%)
  between operations  5.96 us (2%)
    ppermute x49, waiting for transfers between devices, swap(): return lax.ppermute(x, axis, [(i, i ^ distance) for i in range(size)])  144 us
    ppermute x49, starting transfers between devices, swap(): return lax.ppermute(x, axis, [(i, i ^ distance) for i in range(size)])  98.8 us
    pallas_call x4, Pallas kernels, rotate(): pl.pallas_call(functools.partial(rotate_kernel, parts, modes // parts, j_...  44.1 us
    pallas_call x5, Pallas kernels, gram(): pl.pallas_call(functools.partial(gram_kernel, parts, c_counts, fresh), gr...  34.3 us
    unnamed x69, local copies, waits for them, and re-layouts  9.65 us
  transfers between devices with their start and end apart: 49, of which 14 were waited for; matrix products, arithmetic and copies ran while one was open for 2% of the time, Pallas kernels for 20%

profile of v5, /device:TPU:0, one launch (start us, length us, event | category | flops | bytes accessed | tf_op | source)
XLA Modules:
  0.0 345.1 jit_solution(14163503339810110450)
XLA Ops:
  0.0 6.9 %rotate.4 = (bf16[48,16,128]{2,1,0:T(8,128)(2,1)}, bf16[48,16,128]{2,1,0:T(8,128)(2,1)}, bf16[48,16,128]{2,1,0:T(8,128)(2,1)}, bf16[48,16,128]{2,1,0:T(8,128)(2,...) custom-call(s32[1,3]{1,0:T(1,128)} %index.7, ...), custom_call_target="tpu_custom_call" | custom-call | flops 1 | bytes 1 | tf_op jit(solution)/shard_map/rotate/pallas_call | solution.py:83
  7.4 3.7 %collective-permute-start.3 = (bf16[48,16,128]{2,1,0:T(8,128)(2,1)}, bf16[48,16,128]{2,1,0:T(8,128)(2,1)S(1)}, u32[]{:S(2)}, u32[]{:S(2)}) collective-permute-start(bf16[48,16,128]{2,1,0:T(8,128)(2,1)} %get-tuple-element.114), channel_id=1, source_target_pairs={{0,5},{1,4},{2,7},{3,6},{4,1},{5,0},{6,3},{7,2},{8,13},{9,12},{10,... | collective-permute-start | bytes 589832 | tf_op jit(solution)/shard_map/ppermute | solution.py:252
  12.2 2.5 collective-permute-start.2
  15.3 1.9 collective-permute-start.24
  17.2 16.2 %collective-permute-done.3.rest_10_ = bf16[48,16,128]{2,1,0:T(8,128)(2,1)S(1)} collective-permute-done((bf16[48,16,128]{2,1,0:T(8,128)(2,1)}, bf16[48,16,128]{2,1,0:T(8,128)(2,1)S(1)}, u32[]{:S(2)}, u32[]{:S(2)}) %collective-permute-start.3) | collective-permute-done | bytes 196640 | tf_op jit(solution)/shard_map/ppermute | solution.py:252
  34.8 10.2 %rotate.5 = (bf16[48,32,128]{2,1,0:T(8,128)(2,1)}, bf16[48,32,128]{2,1,0:T(8,128)(2,1)}, bf16[48,32,128]{2,1,0:T(8,128)(2,1)}, bf16[48,32,128]{2,1,0:T(8,128)(2,...) custom-call(s32[1,3]{1,0:T(1,128)} %index.7, ...), custom_call_target="tpu_custom_call" | custom-call | flops 1 | bytes 1 | tf_op jit(solution)/shard_map/rotate/pallas_call | solution.py:83
  45.1 3.4 collective-permute-start.8
  51.3 15.3 %collective-permute-done.8.rest_11_ = bf16[48,32,128]{2,1,0:T(8,128)(2,1)S(1)} collective-permute-done((bf16[48,32,128]{2,1,0:T(8,128)(2,1)}, bf16[48,32,128]{2,1,0:T(8,128)(2,1)S(1)}, u32[]{:S(2)}, u32[]{:S(2)}) %collective-permute-start.8) | collective-permute-done | bytes 393248 | tf_op jit(solution)/shard_map/ppermute | solution.py:252
  66.7 2.2 collective-permute-start.7
  69.9 13.4 %rotate.6 = (bf16[24,48,128]{2,1,0:T(8,128)(2,1)}, bf16[24,48,128]{2,1,0:T(8,128)(2,1)}, bf16[24,48,128]{2,1,0:T(8,128)(2,1)}, bf16[24,48,128]{2,1,0:T(8,128)(2,...) custom-call(s32[1,3]{1,0:T(1,128)} %index.7, ...), custom_call_target="tpu_custom_call" | custom-call | flops 1 | bytes 1 | tf_op jit(solution)/shard_map/rotate/pallas_call | solution.py:83
  83.4 18.3 %collective-permute-done.31.rest_7_ = bf16[48,32,128]{2,1,0:T(8,128)(2,1)S(1)} collective-permute-done((bf16[48,32,128]{2,1,0:T(8,128)(2,1)}, bf16[48,32,128]{2,1,0:T(8,128)(2,1)S(1)}, u32[]{:S(2)}, u32[]{:S(2)}) %collective-permute-start.31) | collective-permute-done | bytes 393248 | tf_op jit(solution)/shard_map/ppermute | solution.py:252
  101.8 1.9 collective-permute-start.26
  110.0 14.8 %collective-permute-start.20 = (bf16[24,48,128]{2,1,0:T(8,128)(2,1)}, bf16[24,48,128]{2,1,0:T(8,128)(2,1)}, u32[]{:S(2)}, u32[]{:S(2)}) collective-permute-start(bf16[24,48,128]{2,1,0:T(8,128)(2,1)} %get-tuple-element.152), channel_id=1, source_target_pairs={{0,4},{1,5},{2,6},{3,7},{4,0},{5,1},{6,2},{7,3},{8,12},{9,13},{10,... | collective-permute-start | bytes 884744 | tf_op jit(solution)/shard_map/ppermute | solution.py:252
  124.8 1.6 collective-permute-start.14
  126.4 16.0 %collective-permute-done.17.rest_5_ = bf16[24,48,128]{2,1,0:T(8,128)(2,1)S(1)} collective-permute-done((bf16[24,48,128]{2,1,0:T(8,128)(2,1)}, bf16[24,48,128]{2,1,0:T(8,128)(2,1)S(1)}, u32[]{:S(2)}, u32[]{:S(2)}) %collective-permute-start.17) | collective-permute-done | bytes 294944 | tf_op jit(solution)/shard_map/ppermute | solution.py:252
  142.4 2.2 collective-permute-start.11
  146.4 15.4 %collective-permute-done.20.rest_4_ = bf16[24,48,128]{2,1,0:T(8,128)(2,1)} collective-permute-done((bf16[24,48,128]{2,1,0:T(8,128)(2,1)}, bf16[24,48,128]{2,1,0:T(8,128)(2,1)}, u32[]{:S(2)}, u32[]{:S(2)}) %collective-permute-start.20) | collective-permute-done | bytes 294944 | tf_op jit(solution)/shard_map/ppermute | solution.py:252
  161.8 6.9 %collective-permute-start.27 = (bf16[24,48,128]{2,1,0:T(8,128)(2,1)}, bf16[24,48,128]{2,1,0:T(8,128)(2,1)}, u32[]{:S(2)}, u32[]{:S(2)}) collective-permute-start(bf16[24,48,128]{2,1,0:T(8,128)(2,1)} %get-tuple-element.164), channel_id=1, source_target_pairs={{0,2},{1,3},{2,0},{3,1},{4,6},{5,7},{6,4},{7,5},{8,10},{9,11},{10,... | collective-permute-start | bytes 884744 | tf_op jit(solution)/shard_map/ppermute | solution.py:252
  168.7 6.8 %collective-permute-start.21 = (bf16[24,48,128]{2,1,0:T(8,128)(2,1)}, bf16[24,48,128]{2,1,0:T(8,128)(2,1)}, u32[]{:S(2)}, u32[]{:S(2)}) collective-permute-start(bf16[24,48,128]{2,1,0:T(8,128)(2,1)} %get-tuple-element.153), channel_id=1, source_target_pairs={{0,4},{1,5},{2,6},{3,7},{4,0},{5,1},{6,2},{7,3},{8,12},{9,13},{10,... | collective-permute-start | bytes 884744 | tf_op jit(solution)/shard_map/ppermute | solution.py:252
  175.5 1.6 collective-permute-start.15
  177.1 16.1 %collective-permute-done.18.rest_5_ = bf16[24,48,128]{2,1,0:T(8,128)(2,1)} collective-permute-done((bf16[24,48,128]{2,1,0:T(8,128)(2,1)}, bf16[24,48,128]{2,1,0:T(8,128)(2,1)}, u32[]{:S(2)}, u32[]{:S(2)}) %collective-permute-start.18) | collective-permute-done | bytes 294944 | tf_op jit(solution)/shard_map/ppermute | solution.py:252
  193.2 2.2 collective-permute-start.12
  195.4 1.7 constant_dynamic-slice_fusion.6
  197.1 2.3 gather_fusion
  200.6 13.6 %rotate.7 = (bf16[40,48,128]{2,1,0:T(8,128)(2,1)}, bf16[40,48,128]{2,1,0:T(8,128)(2,1)}, bf16[40,48,128]{2,1,0:T(8,128)(2,1)}, bf16[40,48,128]{2,1,0:T(8,128)(2,...) custom-call(s32[1,3]{1,0:T(1,128)} %index.7, ...), custom_call_target="tpu_custom_call" | custom-call | flops 1 | bytes 1 | tf_op jit(solution)/shard_map/rotate/pallas_call | solution.py:83
  214.3 2.0 collective-permute-start.28
  216.6 3.1 collective-permute-start.19
  227.1 10.5 %gram.5 = (f32[2,192,384]{2,1,0:T(8,128)S(1)}, f32[2,192,384]{2,1,0:T(8,128)S(1)}) custom-call(f32[1,2]{1,0:T(1,128)S(1)} %copy-done.22, bf16[384,384]{1,0:T(8,128)(2,1)S(1)} %bitcast.11, f32[3,384]{1,0:T(4,128)S(1)} %pad_maximum_fusion.row_ref, f32[48,3]{1,0:T(8,128)S(1)} %bitcast.16, bf16[48,16,128]{2,1,0:T(8,128)(2,1)S(1)} %copy-done.6, ...), custom_call_target="tpu_custom_call" | custom-call | flops 5435817984 | bytes 7077888 | tf_op jit(solution)/shard_map/gram/pallas_call | solution.py:175
  237.9 7.9 %collective-permute-done.34.rest_3_ = bf16[40,48,128]{2,1,0:T(8,128)(2,1)S(1)} collective-permute-done((bf16[40,48,128]{2,1,0:T(8,128)(2,1)}, bf16[40,48,128]{2,1,0:T(8,128)(2,1)S(1)}, u32[]{:S(2)}, u32[]{:S(2)}) %collective-permute-start.34) | collective-permute-done | bytes 491552 | tf_op jit(solution)/shard_map/ppermute | solution.py:252
  245.8 2.8 collective-permute-start.16
  248.6 8.3 %collective-permute-done.28.rest_2_ = bf16[40,48,128]{2,1,0:T(8,128)(2,1)S(1)} collective-permute-done((bf16[40,48,128]{2,1,0:T(8,128)(2,1)}, bf16[40,48,128]{2,1,0:T(8,128)(2,1)S(1)}, u32[]{:S(2)}, u32[]{:S(2)}) %collective-permute-start.28) | collective-permute-done | bytes 491552 | tf_op jit(solution)/shard_map/ppermute | solution.py:252
  256.9 1.9 collective-permute-start.13
  258.9 6.2 %gram.6 = (f32[2,192,384]{2,1,0:T(8,128)S(1)}, f32[2,192,384]{2,1,0:T(8,128)S(1)}) custom-call(f32[1,2]{1,0:T(1,128)S(1)} %copy-done.22, bf16[384,384]{1,0:T(8,128)(2,1)S(1)} %bitcast.12, f32[3,384]{1,0:T(4,128)S(1)} %pad_maximum_fusion.row_ref, f32[48,3]{1,0:T(8,128)S(1)} %bitcast.17, ...), custom_call_target="tpu_custom_call", output_to_operand_aliasing={{0}: (12, {}), {1}: (13, {})} | custom-call | flops 2717908992 | bytes 4718592 | tf_op jit(solution)/shard_map/gram/pallas_call | solution.py:175
  265.2 16.9 %collective-permute-done.19.rest_5_ = bf16[40,48,128]{2,1,0:T(8,128)(2,1)S(1)} collective-permute-done((bf16[40,48,128]{2,1,0:T(8,128)(2,1)}, bf16[40,48,128]{2,1,0:T(8,128)(2,1)S(1)}, u32[]{:S(2)}, u32[]{:S(2)}) %collective-permute-start.19) | collective-permute-done | bytes 491552 | tf_op jit(solution)/shard_map/ppermute | solution.py:252
  283.0 6.3 %gram.7 = (f32[2,192,384]{2,1,0:T(8,128)S(1)}, f32[2,192,384]{2,1,0:T(8,128)S(1)}) custom-call(f32[1,2]{1,0:T(1,128)S(1)} %copy-done.22, bf16[384,384]{1,0:T(8,128)(2,1)S(1)} %bitcast.13, f32[3,384]{1,0:T(4,128)S(1)} %pad_maximum_fusion.row_ref, f32[48,3]{1,0:T(8,128)S(1)} %bitcast.18, ...), custom_call_target="tpu_custom_call", output_to_operand_aliasing={{0}: (12, {}), {1}: (13, {})} | custom-call | flops 2717908992 | bytes 4718592 | tf_op jit(solution)/shard_map/gram/pallas_call | solution.py:175
  289.3 6.0 %collective-permute-start.36 = (bf16[8,48,128]{2,1,0:T(8,128)(2,1)S(1)}, bf16[8,48,128]{2,1,0:T(8,128)(2,1)S(1)}, u32[]{:S(2)}, u32[]{:S(2)}) collective-permute-start(bf16[8,48,128]{2,1,0:T(8,128)(2,1)S(1)} %copy-done.31), channel_id=1, source_target_pairs={{0,4},{1,5},{2,6},{3,7},{4,0},{5,1},{6,2},{7,3},{8,12},{9,13},{10,... | collective-permute-start | bytes 294920 | tf_op jit(solution)/shard_map/ppermute | solution.py:252
  295.3 12.1 %collective-permute-start.37 = (bf16[8,48,128]{2,1,0:T(8,128)(2,1)S(1)}, bf16[8,48,128]{2,1,0:T(8,128)(2,1)S(1)}, u32[]{:S(2)}, u32[]{:S(2)}) collective-permute-start(bf16[8,48,128]{2,1,0:T(8,128)(2,1)S(1)} %copy-done.30), channel_id=1, source_target_pairs={{0,5},{1,4},{2,7},{3,6},{4,1},{5,0},{6,3},{7,2},{8,13},{9,12},{10,... | collective-permute-start | bytes 294920 | tf_op jit(solution)/shard_map/ppermute | solution.py:252
  307.4 2.4 collective-permute-start.38
  311.3 9.1 %gram.8 = (f32[2,192,384]{2,1,0:T(8,128)S(1)}, f32[2,192,384]{2,1,0:T(8,128)S(1)}) custom-call(f32[1,2]{1,0:T(1,128)S(1)} %copy-done.22, bf16[384,384]{1,0:T(8,128)(2,1)S(1)} %bitcast.14, f32[3,384]{1,0:T(4,128)S(1)} %pad_maximum_fusion.row_ref, f32[48,3]{1,0:T(8,128)S(1)} %bitcast.19, ...), custom_call_target="tpu_custom_call", output_to_operand_aliasing={{0}: (12, {}), {1}: (13, {})} | custom-call | flops 4529848320 | bytes 6291456 | tf_op jit(solution)/shard_map/gram/pallas_call | solution.py:175
  320.5 2.2 gram.9
  322.8 1.9 collective-permute-done.42.got_ref
  325.0 1.6 collective-permute-start.43
  326.6 1.5 collective-permute-start.44
  328.6 3.1 collective-permute-done.43.rest_1_
  331.7 3.7 %collective-permute-done.44.rest_2_ = f32[96,384]{1,0:T(8,128)S(1)} collective-permute-done((f32[96,384]{1,0:T(8,128)S(1)}, f32[96,384]{1,0:T(8,128)S(1)}, u32[]{:S(2)}, u32[]{:S(2)}) %collective-permute-start.44) | collective-permute-done | bytes 147488 | tf_op jit(solution)/shard_map/ppermute | solution.py:252
  336.8 1.8 collective-permute-start.47
  340.1 2.8 collective-permute-done.47
  342.9 1.6 collective-permute-done.48
  (145 shorter events, 26.2 us)
Async XLA Ops:
  6.9 7.7 %collective-permute-start = (bf16[48,16,128]{2,1,0:T(8,128)(2,1)}, bf16[48,16,128]{2,1,0:T(8,128)(2,1)S(1)}, u32[]{:S(2)}, u32[]{:S(2)}) collective-permute-start(bf16[48,16,128]{2,1,0:T(8,128)(2,1)} %get-tuple-element.109), channel_id=1, source_target_pairs={{0,1},{1,0},{2,3},{3,2},{4,5},{5,4},{6,7},{7,6},{8,9},{9,8},{10,11... | collective-permute-start | bytes 589832 | tf_op jit(solution)/shard_map/ppermute | solution.py:252
  7.4 26.0 %collective-permute-start.3 = (bf16[48,16,128]{2,1,0:T(8,128)(2,1)}, bf16[48,16,128]{2,1,0:T(8,128)(2,1)S(1)}, u32[]{:S(2)}, u32[]{:S(2)}) collective-permute-start(bf16[48,16,128]{2,1,0:T(8,128)(2,1)} %get-tuple-element.114), channel_id=1, source_target_pairs={{0,5},{1,4},{2,7},{3,6},{4,1},{5,0},{6,3},{7,2},{8,13},{9,12},{10,... | collective-permute-start | bytes 589832 | tf_op jit(solution)/shard_map/ppermute | solution.py:252
  11.1 33.9 %collective-permute-start.1 = (bf16[48,16,128]{2,1,0:T(8,128)(2,1)}, bf16[48,16,128]{2,1,0:T(8,128)(2,1)S(1)}, u32[]{:S(2)}, u32[]{:S(2)}) collective-permute-start(bf16[48,16,128]{2,1,0:T(8,128)(2,1)} %get-tuple-element.112), channel_id=1, source_target_pairs={{0,7},{1,6},{2,5},{3,4},{4,3},{5,2},{6,1},{7,0},{8,15},{9,14},{10,... | collective-permute-start | bytes 589832 | tf_op jit(solution)/shard_map/ppermute | solution.py:252
  12.2 36.3 %collective-permute-start.2 = (bf16[48,16,128]{2,1,0:T(8,128)(2,1)}, bf16[48,16,128]{2,1,0:T(8,128)(2,1)S(1)}, u32[]{:S(2)}, u32[]{:S(2)}) collective-permute-start(bf16[48,16,128]{2,1,0:T(8,128)(2,1)} %get-tuple-element.113), channel_id=1, source_target_pairs={{0,6},{1,7},{2,4},{3,5},{4,2},{5,3},{6,0},{7,1},{8,14},{9,15},{10,... | collective-permute-start | bytes 589832 | tf_op jit(solution)/shard_map/ppermute | solution.py:252
  14.6 33.8 %collective-permute-start.4 = (bf16[48,16,128]{2,1,0:T(8,128)(2,1)}, bf16[48,16,128]{2,1,0:T(8,128)(2,1)S(1)}, u32[]{:S(2)}, u32[]{:S(2)}) collective-permute-start(bf16[48,16,128]{2,1,0:T(8,128)(2,1)} %get-tuple-element.115), channel_id=1, source_target_pairs={{0,4},{1,5},{2,6},{3,7},{4,0},{5,1},{6,2},{7,3},{8,12},{9,13},{10,... | collective-permute-start | bytes 589832 | tf_op jit(solution)/shard_map/ppermute | solution.py:252
  15.3 33.3 %collective-permute-start.24 = (bf16[48,16,128]{2,1,0:T(8,128)(2,1)}, bf16[48,16,128]{2,1,0:T(8,128)(2,1)S(1)}, u32[]{:S(2)}, u32[]{:S(2)}) collective-permute-start(bf16[48,16,128]{2,1,0:T(8,128)(2,1)} %get-tuple-element.161), channel_id=1, source_target_pairs={{0,2},{1,3},{2,0},{3,1},{4,6},{5,7},{6,4},{7,5},{8,10},{9,11},{10,... | collective-permute-start | bytes 589832 | tf_op jit(solution)/shard_map/ppermute | solution.py:252
  34.1 14.8 %collective-permute-start.30 = (bf16[48,16,128]{2,1,0:T(8,128)(2,1)}, bf16[48,16,128]{2,1,0:T(8,128)(2,1)S(1)}, u32[]{:S(2)}, u32[]{:S(2)}) collective-permute-start(bf16[48,16,128]{2,1,0:T(8,128)(2,1)} %get-tuple-element.172), channel_id=1, source_target_pairs={{0,3},{1,2},{2,1},{3,0},{4,7},{5,6},{6,5},{7,4},{8,11},{9,10},{10,... | collective-permute-start | bytes 589832 | tf_op jit(solution)/shard_map/ppermute | solution.py:252
  45.1 21.6 %collective-permute-start.8 = (bf16[48,32,128]{2,1,0:T(8,128)(2,1)}, bf16[48,32,128]{2,1,0:T(8,128)(2,1)S(1)}, u32[]{:S(2)}, u32[]{:S(2)}) collective-permute-start(bf16[48,32,128]{2,1,0:T(8,128)(2,1)} %get-tuple-element.124), channel_id=1, source_target_pairs={{0,5},{1,4},{2,7},{3,6},{4,1},{5,0},{6,3},{7,2},{8,13},{9,12},{10,... | collective-permute-start | bytes 1179656 | tf_op jit(solution)/shard_map/ppermute | solution.py:252
  48.5 20.4 %collective-permute-start.5 = (bf16[48,32,128]{2,1,0:T(8,128)(2,1)}, bf16[48,32,128]{2,1,0:T(8,128)(2,1)S(1)}, u32[]{:S(2)}, u32[]{:S(2)}) collective-permute-start(bf16[48,32,128]{2,1,0:T(8,128)(2,1)} %get-tuple-element.116), channel_id=1, source_target_pairs={{0,1},{1,0},{2,3},{3,2},{4,5},{5,4},{6,7},{7,6},{8,9},{9,8},{10,11... | collective-permute-start | bytes 1179656 | tf_op jit(solution)/shard_map/ppermute | solution.py:252
  48.6 34.8 %collective-permute-start.25 = (bf16[48,32,128]{2,1,0:T(8,128)(2,1)}, bf16[48,32,128]{2,1,0:T(8,128)(2,1)S(1)}, u32[]{:S(2)}, u32[]{:S(2)}) collective-permute-start(bf16[48,32,128]{2,1,0:T(8,128)(2,1)} %get-tuple-element.162), channel_id=1, source_target_pairs={{0,2},{1,3},{2,0},{3,1},{4,6},{5,7},{6,4},{7,5},{8,10},{9,11},{10,... | collective-permute-start | bytes 1179656 | tf_op jit(solution)/shard_map/ppermute | solution.py:252
  49.6 52.2 %collective-permute-start.31 = (bf16[48,32,128]{2,1,0:T(8,128)(2,1)}, bf16[48,32,128]{2,1,0:T(8,128)(2,1)S(1)}, u32[]{:S(2)}, u32[]{:S(2)}) collective-permute-start(bf16[48,32,128]{2,1,0:T(8,128)(2,1)} %get-tuple-element.173), channel_id=1, source_target_pairs={{0,3},{1,2},{2,1},{3,0},{4,7},{5,6},{6,5},{7,4},{8,11},{9,10},{10,... | collective-permute-start | bytes 1179656 | tf_op jit(solution)/shard_map/ppermute | solution.py:252
  51.1 50.7 %collective-permute-start.9 = (bf16[48,32,128]{2,1,0:T(8,128)(2,1)}, bf16[48,32,128]{2,1,0:T(8,128)(2,1)S(1)}, u32[]{:S(2)}, u32[]{:S(2)}) collective-permute-start(bf16[48,32,128]{2,1,0:T(8,128)(2,1)} %get-tuple-element.126), channel_id=1, source_target_pairs={{0,4},{1,5},{2,6},{3,7},{4,0},{5,1},{6,2},{7,3},{8,12},{9,13},{10,... | collective-permute-start | bytes 1179656 | tf_op jit(solution)/shard_map/ppermute | solution.py:252
  66.7 43.3 %collective-permute-start.7 = (bf16[48,32,128]{2,1,0:T(8,128)(2,1)}, bf16[48,32,128]{2,1,0:T(8,128)(2,1)S(1)}, u32[]{:S(2)}, u32[]{:S(2)}) collective-permute-start(bf16[48,32,128]{2,1,0:T(8,128)(2,1)} %get-tuple-element.122), channel_id=1, source_target_pairs={{0,6},{1,7},{2,4},{3,5},{4,2},{5,3},{6,0},{7,1},{8,14},{9,15},{10,... | collective-permute-start | bytes 1179656 | tf_op jit(solution)/shard_map/ppermute | solution.py:252
  68.9 41.1 %collective-permute-start.6 = (bf16[48,32,128]{2,1,0:T(8,128)(2,1)}, bf16[48,32,128]{2,1,0:T(8,128)(2,1)S(1)}, u32[]{:S(2)}, u32[]{:S(2)}) collective-permute-start(bf16[48,32,128]{2,1,0:T(8,128)(2,1)} %get-tuple-element.120), channel_id=1, source_target_pairs={{0,7},{1,6},{2,5},{3,4},{4,3},{5,2},{6,1},{7,0},{8,15},{9,14},{10,... | collective-permute-start | bytes 1179656 | tf_op jit(solution)/shard_map/ppermute | solution.py:252
  83.4 59.1 %collective-permute-start.17 = (bf16[24,48,128]{2,1,0:T(8,128)(2,1)}, bf16[24,48,128]{2,1,0:T(8,128)(2,1)S(1)}, u32[]{:S(2)}, u32[]{:S(2)}) collective-permute-start(bf16[24,48,128]{2,1,0:T(8,128)(2,1)} %get-tuple-element.146), channel_id=1, source_target_pairs={{0,5},{1,4},{2,7},{3,6},{4,1},{5,0},{6,3},{7,2},{8,13},{9,12},{10,... | collective-permute-start | bytes 884744 | tf_op jit(solution)/shard_map/ppermute | solution.py:252
  101.8 42.9 %collective-permute-start.32 = (bf16[24,48,128]{2,1,0:T(8,128)(2,1)}, bf16[24,48,128]{2,1,0:T(8,128)(2,1)S(1)}, u32[]{:S(2)}, u32[]{:S(2)}) collective-permute-start(bf16[24,48,128]{2,1,0:T(8,128)(2,1)} %get-tuple-element.174), channel_id=1, source_target_pairs={{0,3},{1,2},{2,1},{3,0},{4,7},{5,6},{6,5},{7,4},{8,11},{9,10},{10,... | collective-permute-start | bytes 884744 | tf_op jit(solution)/shard_map/ppermute | solution.py:252
  101.8 43.0 %collective-permute-start.26 = (bf16[24,48,128]{2,1,0:T(8,128)(2,1)}, bf16[24,48,128]{2,1,0:T(8,128)(2,1)}, u32[]{:S(2)}, u32[]{:S(2)}) collective-permute-start(bf16[24,48,128]{2,1,0:T(8,128)(2,1)} %get-tuple-element.163), channel_id=1, source_target_pairs={{0,2},{1,3},{2,0},{3,1},{4,6},{5,7},{6,4},{7,5},{8,10},{9,11},{10,... | collective-permute-start | bytes 884744 | tf_op jit(solution)/shard_map/ppermute | solution.py:252
  110.0 51.8 %collective-permute-start.20 = (bf16[24,48,128]{2,1,0:T(8,128)(2,1)}, bf16[24,48,128]{2,1,0:T(8,128)(2,1)}, u32[]{:S(2)}, u32[]{:S(2)}) collective-permute-start(bf16[24,48,128]{2,1,0:T(8,128)(2,1)} %get-tuple-element.152), channel_id=1, source_target_pairs={{0,4},{1,5},{2,6},{3,7},{4,0},{5,1},{6,2},{7,3},{8,12},{9,13},{10,... | collective-permute-start | bytes 884744 | tf_op jit(solution)/shard_map/ppermute | solution.py:252
  124.8 37.0 %collective-permute-start.14 = (bf16[24,48,128]{2,1,0:T(8,128)(2,1)}, bf16[24,48,128]{2,1,0:T(8,128)(2,1)}, u32[]{:S(2)}, u32[]{:S(2)}) collective-permute-start(bf16[24,48,128]{2,1,0:T(8,128)(2,1)} %get-tuple-element.140), channel_id=1, source_target_pairs={{0,6},{1,7},{2,4},{3,5},{4,2},{5,3},{6,0},{7,1},{8,14},{9,15},{10,... | collective-permute-start | bytes 884744 | tf_op jit(solution)/shard_map/ppermute | solution.py:252
  142.4 26.3 %collective-permute-start.11 = (bf16[24,48,128]{2,1,0:T(8,128)(2,1)}, bf16[24,48,128]{2,1,0:T(8,128)(2,1)}, u32[]{:S(2)}, u32[]{:S(2)}) collective-permute-start(bf16[24,48,128]{2,1,0:T(8,128)(2,1)} %get-tuple-element.134), channel_id=1, source_target_pairs={{0,7},{1,6},{2,5},{3,4},{4,3},{5,2},{6,1},{7,0},{8,15},{9,14},{10,... | collective-permute-start | bytes 884744 | tf_op jit(solution)/shard_map/ppermute | solution.py:252
  144.7 30.8 %collective-permute-start.10 = (bf16[24,48,128]{2,1,0:T(8,128)(2,1)}, bf16[24,48,128]{2,1,0:T(8,128)(2,1)}, u32[]{:S(2)}, u32[]{:S(2)}) collective-permute-start(bf16[24,48,128]{2,1,0:T(8,128)(2,1)} %get-tuple-element.127), channel_id=1, source_target_pairs={{0,1},{1,0},{2,3},{3,2},{4,5},{5,4},{6,7},{7,6},{8,9},{9,8},{10,11... | collective-permute-start | bytes 884744 | tf_op jit(solution)/shard_map/ppermute | solution.py:252
  144.8 48.4 %collective-permute-start.18 = (bf16[24,48,128]{2,1,0:T(8,128)(2,1)}, bf16[24,48,128]{2,1,0:T(8,128)(2,1)}, u32[]{:S(2)}, u32[]{:S(2)}) collective-permute-start(bf16[24,48,128]{2,1,0:T(8,128)(2,1)} %get-tuple-element.147), channel_id=1, source_target_pairs={{0,5},{1,4},{2,7},{3,6},{4,1},{5,0},{6,3},{7,2},{8,13},{9,12},{10,... | collective-permute-start | bytes 884744 | tf_op jit(solution)/shard_map/ppermute | solution.py:252
  161.8 52.5 %collective-permute-start.33 = (bf16[24,48,128]{2,1,0:T(8,128)(2,1)}, bf16[24,48,128]{2,1,0:T(8,128)(2,1)}, u32[]{:S(2)}, u32[]{:S(2)}) collective-permute-start(bf16[24,48,128]{2,1,0:T(8,128)(2,1)} %get-tuple-element.175), channel_id=1, source_target_pairs={{0,3},{1,2},{2,1},{3,0},{4,7},{5,6},{6,5},{7,4},{8,11},{9,10},{10,... | collective-permute-start | bytes 884744 | tf_op jit(solution)/shard_map/ppermute | solution.py:252
  161.8 52.5 %collective-permute-start.27 = (bf16[24,48,128]{2,1,0:T(8,128)(2,1)}, bf16[24,48,128]{2,1,0:T(8,128)(2,1)}, u32[]{:S(2)}, u32[]{:S(2)}) collective-permute-start(bf16[24,48,128]{2,1,0:T(8,128)(2,1)} %get-tuple-element.164), channel_id=1, source_target_pairs={{0,2},{1,3},{2,0},{3,1},{4,6},{5,7},{6,4},{7,5},{8,10},{9,11},{10,... | collective-permute-start | bytes 884744 | tf_op jit(solution)/shard_map/ppermute | solution.py:252
  168.7 45.5 %collective-permute-start.21 = (bf16[24,48,128]{2,1,0:T(8,128)(2,1)}, bf16[24,48,128]{2,1,0:T(8,128)(2,1)}, u32[]{:S(2)}, u32[]{:S(2)}) collective-permute-start(bf16[24,48,128]{2,1,0:T(8,128)(2,1)} %get-tuple-element.153), channel_id=1, source_target_pairs={{0,4},{1,5},{2,6},{3,7},{4,0},{5,1},{6,2},{7,3},{8,12},{9,13},{10,... | collective-permute-start | bytes 884744 | tf_op jit(solution)/shard_map/ppermute | solution.py:252
  175.5 40.9 %collective-permute-start.15 = (bf16[24,48,128]{2,1,0:T(8,128)(2,1)}, bf16[24,48,128]{2,1,0:T(8,128)(2,1)}, u32[]{:S(2)}, u32[]{:S(2)}) collective-permute-start(bf16[24,48,128]{2,1,0:T(8,128)(2,1)} %get-tuple-element.141), channel_id=1, source_target_pairs={{0,6},{1,7},{2,4},{3,5},{4,2},{5,3},{6,0},{7,1},{8,14},{9,15},{10,... | collective-permute-start | bytes 884744 | tf_op jit(solution)/shard_map/ppermute | solution.py:252
  193.2 23.4 %collective-permute-start.12 = (bf16[24,48,128]{2,1,0:T(8,128)(2,1)}, bf16[24,48,128]{2,1,0:T(8,128)(2,1)}, u32[]{:S(2)}, u32[]{:S(2)}) collective-permute-start(bf16[24,48,128]{2,1,0:T(8,128)(2,1)} %get-tuple-element.135), channel_id=1, source_target_pairs={{0,7},{1,6},{2,5},{3,4},{4,3},{5,2},{6,1},{7,0},{8,15},{9,14},{10,... | collective-permute-start | bytes 884744 | tf_op jit(solution)/shard_map/ppermute | solution.py:252
  214.2 23.5 %collective-permute-start.41 = (bf16[24,48,128]{2,1,0:T(8,128)(2,1)}, bf16[24,48,128]{2,1,0:T(8,128)(2,1)S(1)}, u32[]{:S(2)}, u32[]{:S(2)}) collective-permute-start(bf16[24,48,128]{2,1,0:T(8,128)(2,1)} %get-tuple-element.191), channel_id=1, source_target_pairs={{0,1},{1,0},{2,3},{3,2},{4,5},{5,4},{6,7},{7,6},{8,9},{9,8},{10,11... | collective-permute-start | bytes 884744 | tf_op jit(solution)/shard_map/ppermute | solution.py:252
  214.3 31.5 %collective-permute-start.34 = (bf16[40,48,128]{2,1,0:T(8,128)(2,1)}, bf16[40,48,128]{2,1,0:T(8,128)(2,1)S(1)}, u32[]{:S(2)}, u32[]{:S(2)}) collective-permute-start(bf16[40,48,128]{2,1,0:T(8,128)(2,1)} %get-tuple-element.176), channel_id=1, source_target_pairs={{0,3},{1,2},{2,1},{3,0},{4,7},{5,6},{6,5},{7,4},{8,11},{9,10},{10,... | collective-permute-start | bytes 1474568 | tf_op jit(solution)/shard_map/ppermute | solution.py:252
  214.3 42.6 %collective-permute-start.28 = (bf16[40,48,128]{2,1,0:T(8,128)(2,1)}, bf16[40,48,128]{2,1,0:T(8,128)(2,1)S(1)}, u32[]{:S(2)}, u32[]{:S(2)}) collective-permute-start(bf16[40,48,128]{2,1,0:T(8,128)(2,1)} %get-tuple-element.165), channel_id=1, source_target_pairs={{0,2},{1,3},{2,0},{3,1},{4,6},{5,7},{6,4},{7,5},{8,10},{9,11},{10,... | collective-permute-start | bytes 1474568 | tf_op jit(solution)/shard_map/ppermute | solution.py:252
  216.4 48.7 %collective-permute-start.22 = (bf16[40,48,128]{2,1,0:T(8,128)(2,1)}, bf16[40,48,128]{2,1,0:T(8,128)(2,1)S(1)}, u32[]{:S(2)}, u32[]{:S(2)}) collective-permute-start(bf16[40,48,128]{2,1,0:T(8,128)(2,1)} %get-tuple-element.154), channel_id=1, source_target_pairs={{0,4},{1,5},{2,6},{3,7},{4,0},{5,1},{6,2},{7,3},{8,12},{9,13},{10,... | collective-permute-start | bytes 1474568 | tf_op jit(solution)/shard_map/ppermute | solution.py:252
  216.6 65.5 %collective-permute-start.19 = (bf16[40,48,128]{2,1,0:T(8,128)(2,1)}, bf16[40,48,128]{2,1,0:T(8,128)(2,1)S(1)}, u32[]{:S(2)}, u32[]{:S(2)}) collective-permute-start(bf16[40,48,128]{2,1,0:T(8,128)(2,1)} %get-tuple-element.148), channel_id=1, source_target_pairs={{0,5},{1,4},{2,7},{3,6},{4,1},{5,0},{6,3},{7,2},{8,13},{9,12},{10,... | collective-permute-start | bytes 1474568 | tf_op jit(solution)/shard_map/ppermute | solution.py:252
  237.6 69.7 %collective-permute-start.40 = (bf16[40,48,128]{2,1,0:T(8,128)(2,1)S(1)}, bf16[40,48,128]{2,1,0:T(8,128)(2,1)S(1)}, u32[]{:S(2)}, u32[]{:S(2)}) collective-permute-start(bf16[40,48,128]{2,1,0:T(8,128)(2,1)S(1)} %copy-done.24), channel_id=1, source_target_pairs={{0,1},{1,0},{2,3},{3,2},{4,5},{5,4},{6,7},{7,6},{8,9},{9,8},{10,11... | collective-permute-start | bytes 1474568 | tf_op jit(solution)/shard_map/ppermute | solution.py:252
  245.8 43.5 %collective-permute-start.16 = (bf16[40,48,128]{2,1,0:T(8,128)(2,1)S(1)}, bf16[40,48,128]{2,1,0:T(8,128)(2,1)S(1)}, u32[]{:S(2)}, u32[]{:S(2)}) collective-permute-start(bf16[40,48,128]{2,1,0:T(8,128)(2,1)S(1)} %copy-done.26), channel_id=1, source_target_pairs={{0,6},{1,7},{2,4},{3,5},{4,2},{5,3},{6,0},{7,1},{8,14},{9,15},{10,... | collective-permute-start | bytes 1474568 | tf_op jit(solution)/shard_map/ppermute | solution.py:252
  256.9 38.4 %collective-permute-start.13 = (bf16[40,48,128]{2,1,0:T(8,128)(2,1)S(1)}, bf16[40,48,128]{2,1,0:T(8,128)(2,1)S(1)}, u32[]{:S(2)}, u32[]{:S(2)}) collective-permute-start(bf16[40,48,128]{2,1,0:T(8,128)(2,1)S(1)} %copy-done.25), channel_id=1, source_target_pairs={{0,7},{1,6},{2,5},{3,4},{4,3},{5,2},{6,1},{7,0},{8,15},{9,14},{10,... | collective-permute-start | bytes 1474568 | tf_op jit(solution)/shard_map/ppermute | solution.py:252
  265.2 44.6 %collective-permute-start.35 = (bf16[8,48,128]{2,1,0:T(8,128)(2,1)S(1)}, bf16[8,48,128]{2,1,0:T(8,128)(2,1)S(1)}, u32[]{:S(2)}, u32[]{:S(2)}) collective-permute-start(bf16[8,48,128]{2,1,0:T(8,128)(2,1)S(1)} %copy-done.33), channel_id=1, source_target_pairs={{0,3},{1,2},{2,1},{3,0},{4,7},{5,6},{6,5},{7,4},{8,11},{9,10},{10,... | collective-permute-start | bytes 294920 | tf_op jit(solution)/shard_map/ppermute | solution.py:252
  282.1 27.7 %collective-permute-start.29 = (bf16[8,48,128]{2,1,0:T(8,128)(2,1)S(1)}, bf16[8,48,128]{2,1,0:T(8,128)(2,1)S(1)}, u32[]{:S(2)}, u32[]{:S(2)}) collective-permute-start(bf16[8,48,128]{2,1,0:T(8,128)(2,1)S(1)} %copy-done.32), channel_id=1, source_target_pairs={{0,2},{1,3},{2,0},{3,1},{4,6},{5,7},{6,4},{7,5},{8,10},{9,11},{10,... | collective-permute-start | bytes 294920 | tf_op jit(solution)/shard_map/ppermute | solution.py:252
  289.3 31.1 %collective-permute-start.36 = (bf16[8,48,128]{2,1,0:T(8,128)(2,1)S(1)}, bf16[8,48,128]{2,1,0:T(8,128)(2,1)S(1)}, u32[]{:S(2)}, u32[]{:S(2)}) collective-permute-start(bf16[8,48,128]{2,1,0:T(8,128)(2,1)S(1)} %copy-done.31), channel_id=1, source_target_pairs={{0,4},{1,5},{2,6},{3,7},{4,0},{5,1},{6,2},{7,3},{8,12},{9,13},{10,... | collective-permute-start | bytes 294920 | tf_op jit(solution)/shard_map/ppermute | solution.py:252
  295.3 25.1 %collective-permute-start.37 = (bf16[8,48,128]{2,1,0:T(8,128)(2,1)S(1)}, bf16[8,48,128]{2,1,0:T(8,128)(2,1)S(1)}, u32[]{:S(2)}, u32[]{:S(2)}) collective-permute-start(bf16[8,48,128]{2,1,0:T(8,128)(2,1)S(1)} %copy-done.30), channel_id=1, source_target_pairs={{0,5},{1,4},{2,7},{3,6},{4,1},{5,0},{6,3},{7,2},{8,13},{9,12},{10,... | collective-permute-start | bytes 294920 | tf_op jit(solution)/shard_map/ppermute | solution.py:252
  307.4 13.1 %collective-permute-start.38 = (bf16[8,48,128]{2,1,0:T(8,128)(2,1)S(1)}, bf16[8,48,128]{2,1,0:T(8,128)(2,1)S(1)}, u32[]{:S(2)}, u32[]{:S(2)}) collective-permute-start(bf16[8,48,128]{2,1,0:T(8,128)(2,1)S(1)} %copy-done.29), channel_id=1, source_target_pairs={{0,6},{1,7},{2,4},{3,5},{4,2},{5,3},{6,0},{7,1},{8,14},{9,15},{10,... | collective-permute-start | bytes 294920 | tf_op jit(solution)/shard_map/ppermute | solution.py:252
  309.8 10.7 %collective-permute-start.23 = (bf16[8,48,128]{2,1,0:T(8,128)(2,1)S(1)}, bf16[8,48,128]{2,1,0:T(8,128)(2,1)S(1)}, u32[]{:S(2)}, u32[]{:S(2)}) collective-permute-start(bf16[8,48,128]{2,1,0:T(8,128)(2,1)S(1)} %copy-done.28), channel_id=1, source_target_pairs={{0,1},{1,0},{2,3},{3,2},{4,5},{5,4},{6,7},{7,6},{8,9},{9,8},{10,11... | collective-permute-start | bytes 294920 | tf_op jit(solution)/shard_map/ppermute | solution.py:252
  309.8 10.7 %collective-permute-start.39 = (bf16[8,48,128]{2,1,0:T(8,128)(2,1)S(1)}, bf16[8,48,128]{2,1,0:T(8,128)(2,1)S(1)}, u32[]{:S(2)}, u32[]{:S(2)}) collective-permute-start(bf16[8,48,128]{2,1,0:T(8,128)(2,1)S(1)} %copy-done.27), channel_id=1, source_target_pairs={{0,7},{1,6},{2,5},{3,4},{4,3},{5,2},{6,1},{7,0},{8,15},{9,14},{10,... | collective-permute-start | bytes 294920 | tf_op jit(solution)/shard_map/ppermute | solution.py:252
  325.0 6.6 %collective-permute-start.43 = (f32[96,384]{1,0:T(8,128)S(1)}, f32[96,384]{1,0:T(8,128)S(1)}, u32[]{:S(2)}, u32[]{:S(2)}) collective-permute-start(f32[96,384]{1,0:T(8,128)S(1)} %get-tuple-element.206), channel_id=1, source_target_pairs={{0,8},{8,0},{16,24},{24,16},{1,9},{9,1},{17,25},{25,17},{2,10},{10... | collective-permute-start | bytes 442376 | tf_op jit(solution)/shard_map/ppermute | solution.py:252
  326.6 8.8 %collective-permute-start.44 = (f32[96,384]{1,0:T(8,128)S(1)}, f32[96,384]{1,0:T(8,128)S(1)}, u32[]{:S(2)}, u32[]{:S(2)}) collective-permute-start(f32[96,384]{1,0:T(8,128)S(1)} %get-tuple-element.207), channel_id=1, source_target_pairs={{0,16},{8,24},{16,0},{24,8},{1,17},{9,25},{17,1},{25,9},{2,18},{10... | collective-permute-start | bytes 442376 | tf_op jit(solution)/shard_map/ppermute | solution.py:252
  328.2 7.2 %collective-permute-start.45 = (f32[96,384]{1,0:T(8,128)S(1)}, f32[96,384]{1,0:T(8,128)S(1)}, u32[]{:S(2)}, u32[]{:S(2)}) collective-permute-start(f32[96,384]{1,0:T(8,128)S(1)} %get-tuple-element.208), channel_id=1, source_target_pairs={{0,24},{8,16},{16,8},{24,0},{1,25},{9,17},{17,9},{25,1},{2,26},{10... | collective-permute-start | bytes 442376 | tf_op jit(solution)/shard_map/ppermute | solution.py:252
  335.6 4.6 %collective-permute-start.46 = (f32[2,48,96]{2,1,0:T(8,128)S(1)}, f32[2,48,96]{2,1,0:T(8,128)S(1)}, u32[]{:S(2)}, u32[]{:S(2)}) collective-permute-start(f32[2,48,96]{2,1,0:T(8,128)S(1)} %get-tuple-element.210), channel_id=1, source_target_pairs={{0,2},{1,3},{2,0},{3,1},{4,6},{5,7},{6,4},{7,5},{8,10},{9,11},{10,... | collective-permute-start | bytes 110600 | tf_op jit(solution)/shard_map/ppermute | solution.py:252
  336.8 6.0 %collective-permute-start.47 = (f32[2,48,96]{2,1,0:T(8,128)S(1)}, f32[2,48,96]{2,1,0:T(8,128)S(1)}, u32[]{:S(2)}, u32[]{:S(2)}) collective-permute-start(f32[2,48,96]{2,1,0:T(8,128)S(1)} %get-tuple-element.211), channel_id=1, source_target_pairs={{0,4},{1,5},{2,6},{3,7},{4,0},{5,1},{6,2},{7,3},{8,12},{9,13},{10,... | collective-permute-start | bytes 110600 | tf_op jit(solution)/shard_map/ppermute | solution.py:252
  338.6 5.9 %collective-permute-start.48 = (f32[2,48,96]{2,1,0:T(8,128)S(1)}, f32[2,48,96]{2,1,0:T(8,128)S(1)}, u32[]{:S(2)}, u32[]{:S(2)}) collective-permute-start(f32[2,48,96]{2,1,0:T(8,128)S(1)} %get-tuple-element.212), channel_id=1, source_target_pairs={{0,6},{1,7},{2,4},{3,5},{4,2},{5,3},{6,0},{7,1},{8,14},{9,15},{10,... | collective-permute-start | bytes 110600 | tf_op jit(solution)/shard_map/ppermute | solution.py:252
  (35 other events, 610.2 us)

commit v6 on v5

--- a/solution.py
+++ b/solution.py
@@ -314,12 +314,12 @@
             tile, j_low, j_count, used = sums.pop(0)
             arrived = [[sent[block][s] for block, _ in used] for s in range(parts)]
             offsets = [offset for _, offset in used]
-            total = gram(arrived, offsets, three, rows, cols, probes, total, tile, j_low, j_count, 8)
+            total = gram(arrived, offsets, three, rows, cols, probes, total, tile, j_low, j_count, 16 if j_count % 16 == 0 and j_low % 16 == 0 else 8)
     keep, give = total
     blocks = to_pairs(keep, swap(give, "mode", parts, 1), pairs)
     blocks = [b if s == 0 else swap(b, "pair", pairs, s) for s, b in enumerate(blocks)]
     blocks = to_modes(blocks, parts // 2)
-    blocks = [b if s == 0 else swap(b, "mode", parts, 2 * s) for s, b in enumerate(blocks)]
+    blocks = [b if s == 0 else swap(b, "mode", parts, 2 * s) for s, b in list(enumerate(blocks))[::-1]]
     local = jnp.transpose(sum(blocks), (1, 0, 2))
     row_count, _, col_count = local.shape
     row_ids = place * row_count + jnp.arange(row_count, dtype=jnp.int32)

time: 346 us -> 344 us (level)
  transfers between devices with their start and end apart: 49 -> 49, of which waited for: 14 -> 15; matrix products, arithmetic and copies ran while one was open for 2% -> 2% of each run, Pallas kernels for 20% -> 20%
where the time goes in v6:
time: 344 us
  waiting for transfers between devices  143 us (42%)
  starting transfers between devices  98.8 us (29%)
  Pallas kernels  78 us (23%)
  local copies, waits for them, and re-layouts  17.6 us (5%)
  between operations  5.96 us (2%)
    ppermute x49, waiting for transfers between devices, swap(): return lax.ppermute(x, axis, [(i, i ^ distance) for i in range(size)])  143 us
    ppermute x49, starting transfers between devices, swap(): return lax.ppermute(x, axis, [(i, i ^ distance) for i in range(size)])  98.8 us
    pallas_call x4, Pallas kernels, rotate(): pl.pallas_call(functools.partial(rotate_kernel, parts, modes // parts, j_...  44.1 us
    pallas_call x5, Pallas kernels, gram(): pl.pallas_call(functools.partial(gram_kernel, parts, c_counts, fresh), gr...  33.5 us
    unnamed x69, local copies, waits for them, and re-layouts  9.65 us
  transfers between devices with their start and end apart: 49, of which 15 were waited for; matrix products, arithmetic and copies ran while one was open for 2% of the time, Pallas kernels for 20%

profile of v6, /device:TPU:0, one launch (start us, length us, event | category | flops | bytes accessed | tf_op | source)
XLA Modules:
  0.0 343.7 jit_solution(5888434605066001710)
XLA Ops:
  0.0 6.9 %rotate.4 = (bf16[48,16,128]{2,1,0:T(8,128)(2,1)}, bf16[48,16,128]{2,1,0:T(8,128)(2,1)}, bf16[48,16,128]{2,1,0:T(8,128)(2,1)}, bf16[48,16,128]{2,1,0:T(8,128)(2,...) custom-call(s32[1,3]{1,0:T(1,128)} %index.7, ...), custom_call_target="tpu_custom_call" | custom-call | flops 1 | bytes 1 | tf_op jit(solution)/shard_map/rotate/pallas_call | solution.py:83
  7.4 3.7 %collective-permute-start.3 = (bf16[48,16,128]{2,1,0:T(8,128)(2,1)}, bf16[48,16,128]{2,1,0:T(8,128)(2,1)S(1)}, u32[]{:S(2)}, u32[]{:S(2)}) collective-permute-start(bf16[48,16,128]{2,1,0:T(8,128)(2,1)} %get-tuple-element.114), channel_id=1, source_target_pairs={{0,5},{1,4},{2,7},{3,6},{4,1},{5,0},{6,3},{7,2},{8,13},{9,12},{10,... | collective-permute-start | bytes 589832 | tf_op jit(solution)/shard_map/ppermute | solution.py:252
  12.2 2.5 collective-permute-start.2
  15.3 1.9 collective-permute-start.24
  17.2 16.2 %collective-permute-done.3.rest_10_ = bf16[48,16,128]{2,1,0:T(8,128)(2,1)S(1)} collective-permute-done((bf16[48,16,128]{2,1,0:T(8,128)(2,1)}, bf16[48,16,128]{2,1,0:T(8,128)(2,1)S(1)}, u32[]{:S(2)}, u32[]{:S(2)}) %collective-permute-start.3) | collective-permute-done | bytes 196640 | tf_op jit(solution)/shard_map/ppermute | solution.py:252
  34.8 10.2 %rotate.5 = (bf16[48,32,128]{2,1,0:T(8,128)(2,1)}, bf16[48,32,128]{2,1,0:T(8,128)(2,1)}, bf16[48,32,128]{2,1,0:T(8,128)(2,1)}, bf16[48,32,128]{2,1,0:T(8,128)(2,...) custom-call(s32[1,3]{1,0:T(1,128)} %index.7, ...), custom_call_target="tpu_custom_call" | custom-call | flops 1 | bytes 1 | tf_op jit(solution)/shard_map/rotate/pallas_call | solution.py:83
  45.1 3.4 collective-permute-start.8
  51.3 15.3 %collective-permute-done.8.rest_11_ = bf16[48,32,128]{2,1,0:T(8,128)(2,1)S(1)} collective-permute-done((bf16[48,32,128]{2,1,0:T(8,128)(2,1)}, bf16[48,32,128]{2,1,0:T(8,128)(2,1)S(1)}, u32[]{:S(2)}, u32[]{:S(2)}) %collective-permute-start.8) | collective-permute-done | bytes 393248 | tf_op jit(solution)/shard_map/ppermute | solution.py:252
  66.7 2.2 collective-permute-start.7
  69.9 13.4 %rotate.6 = (bf16[24,48,128]{2,1,0:T(8,128)(2,1)}, bf16[24,48,128]{2,1,0:T(8,128)(2,1)}, bf16[24,48,128]{2,1,0:T(8,128)(2,1)}, bf16[24,48,128]{2,1,0:T(8,128)(2,...) custom-call(s32[1,3]{1,0:T(1,128)} %index.7, ...), custom_call_target="tpu_custom_call" | custom-call | flops 1 | bytes 1 | tf_op jit(solution)/shard_map/rotate/pallas_call | solution.py:83
  83.4 18.3 %collective-permute-done.31.rest_7_ = bf16[48,32,128]{2,1,0:T(8,128)(2,1)S(1)} collective-permute-done((bf16[48,32,128]{2,1,0:T(8,128)(2,1)}, bf16[48,32,128]{2,1,0:T(8,128)(2,1)S(1)}, u32[]{:S(2)}, u32[]{:S(2)}) %collective-permute-start.31) | collective-permute-done | bytes 393248 | tf_op jit(solution)/shard_map/ppermute | solution.py:252
  101.8 1.9 collective-permute-start.26
  110.0 14.8 %collective-permute-start.20 = (bf16[24,48,128]{2,1,0:T(8,128)(2,1)}, bf16[24,48,128]{2,1,0:T(8,128)(2,1)}, u32[]{:S(2)}, u32[]{:S(2)}) collective-permute-start(bf16[24,48,128]{2,1,0:T(8,128)(2,1)} %get-tuple-element.152), channel_id=1, source_target_pairs={{0,4},{1,5},{2,6},{3,7},{4,0},{5,1},{6,2},{7,3},{8,12},{9,13},{10,... | collective-permute-start | bytes 884744 | tf_op jit(solution)/shard_map/ppermute | solution.py:252
  124.8 1.6 collective-permute-start.14
  126.4 16.0 %collective-permute-done.17.rest_5_ = bf16[24,48,128]{2,1,0:T(8,128)(2,1)S(1)} collective-permute-done((bf16[24,48,128]{2,1,0:T(8,128)(2,1)}, bf16[24,48,128]{2,1,0:T(8,128)(2,1)S(1)}, u32[]{:S(2)}, u32[]{:S(2)}) %collective-permute-start.17) | collective-permute-done | bytes 294944 | tf_op jit(solution)/shard_map/ppermute | solution.py:252
  142.4 2.2 collective-permute-start.11
  146.4 15.4 %collective-permute-done.20.rest_4_ = bf16[24,48,128]{2,1,0:T(8,128)(2,1)} collective-permute-done((bf16[24,48,128]{2,1,0:T(8,128)(2,1)}, bf16[24,48,128]{2,1,0:T(8,128)(2,1)}, u32[]{:S(2)}, u32[]{:S(2)}) %collective-permute-start.20) | collective-permute-done | bytes 294944 | tf_op jit(solution)/shard_map/ppermute | solution.py:252
  161.8 6.9 %collective-permute-start.27 = (bf16[24,48,128]{2,1,0:T(8,128)(2,1)}, bf16[24,48,128]{2,1,0:T(8,128)(2,1)}, u32[]{:S(2)}, u32[]{:S(2)}) collective-permute-start(bf16[24,48,128]{2,1,0:T(8,128)(2,1)} %get-tuple-element.164), channel_id=1, source_target_pairs={{0,2},{1,3},{2,0},{3,1},{4,6},{5,7},{6,4},{7,5},{8,10},{9,11},{10,... | collective-permute-start | bytes 884744 | tf_op jit(solution)/shard_map/ppermute | solution.py:252
  168.7 6.8 %collective-permute-start.21 = (bf16[24,48,128]{2,1,0:T(8,128)(2,1)}, bf16[24,48,128]{2,1,0:T(8,128)(2,1)}, u32[]{:S(2)}, u32[]{:S(2)}) collective-permute-start(bf16[24,48,128]{2,1,0:T(8,128)(2,1)} %get-tuple-element.153), channel_id=1, source_target_pairs={{0,4},{1,5},{2,6},{3,7},{4,0},{5,1},{6,2},{7,3},{8,12},{9,13},{10,... | collective-permute-start | bytes 884744 | tf_op jit(solution)/shard_map/ppermute | solution.py:252
  175.5 1.6 collective-permute-start.15
  177.1 16.1 %collective-permute-done.18.rest_5_ = bf16[24,48,128]{2,1,0:T(8,128)(2,1)} collective-permute-done((bf16[24,48,128]{2,1,0:T(8,128)(2,1)}, bf16[24,48,128]{2,1,0:T(8,128)(2,1)}, u32[]{:S(2)}, u32[]{:S(2)}) %collective-permute-start.18) | collective-permute-done | bytes 294944 | tf_op jit(solution)/shard_map/ppermute | solution.py:252
  193.2 2.2 collective-permute-start.12
  195.4 1.7 constant_dynamic-slice_fusion.6
  197.1 2.3 gather_fusion
  200.6 13.6 %rotate.7 = (bf16[40,48,128]{2,1,0:T(8,128)(2,1)}, bf16[40,48,128]{2,1,0:T(8,128)(2,1)}, bf16[40,48,128]{2,1,0:T(8,128)(2,1)}, bf16[40,48,128]{2,1,0:T(8,128)(2,...) custom-call(s32[1,3]{1,0:T(1,128)} %index.7, ...), custom_call_target="tpu_custom_call" | custom-call | flops 1 | bytes 1 | tf_op jit(solution)/shard_map/rotate/pallas_call | solution.py:83
  214.3 2.0 collective-permute-start.28
  216.6 3.1 collective-permute-start.19
  227.1 9.9 %gram.5 = (f32[2,192,384]{2,1,0:T(8,128)S(1)}, f32[2,192,384]{2,1,0:T(8,128)S(1)}) custom-call(f32[1,2]{1,0:T(1,128)S(1)} %copy-done.22, bf16[384,384]{1,0:T(8,128)(2,1)S(1)} %bitcast.11, f32[3,384]{1,0:T(4,128)S(1)} %pad_maximum_fusion.row_ref, f32[48,3]{1,0:T(8,128)S(1)} %bitcast.16, bf16[48,16,128]{2,1,0:T(8,128)(2,1)S(1)} %copy-done.6, ...), custom_call_target="tpu_custom_call" | custom-call | flops 5435817984 | bytes 7077888 | tf_op jit(solution)/shard_map/gram/pallas_call | solution.py:175
  237.3 8.6 %collective-permute-done.34.rest_3_ = bf16[40,48,128]{2,1,0:T(8,128)(2,1)S(1)} collective-permute-done((bf16[40,48,128]{2,1,0:T(8,128)(2,1)}, bf16[40,48,128]{2,1,0:T(8,128)(2,1)S(1)}, u32[]{:S(2)}, u32[]{:S(2)}) %collective-permute-start.34) | collective-permute-done | bytes 491552 | tf_op jit(solution)/shard_map/ppermute | solution.py:252
  245.8 2.8 collective-permute-start.16
  248.6 8.3 %collective-permute-done.28.rest_2_ = bf16[40,48,128]{2,1,0:T(8,128)(2,1)S(1)} collective-permute-done((bf16[40,48,128]{2,1,0:T(8,128)(2,1)}, bf16[40,48,128]{2,1,0:T(8,128)(2,1)S(1)}, u32[]{:S(2)}, u32[]{:S(2)}) %collective-permute-start.28) | collective-permute-done | bytes 491552 | tf_op jit(solution)/shard_map/ppermute | solution.py:252
  256.9 1.9 collective-permute-start.13
  258.9 6.2 %gram.6 = (f32[2,192,384]{2,1,0:T(8,128)S(1)}, f32[2,192,384]{2,1,0:T(8,128)S(1)}) custom-call(f32[1,2]{1,0:T(1,128)S(1)} %copy-done.22, bf16[384,384]{1,0:T(8,128)(2,1)S(1)} %bitcast.12, f32[3,384]{1,0:T(4,128)S(1)} %pad_maximum_fusion.row_ref, f32[48,3]{1,0:T(8,128)S(1)} %bitcast.17, ...), custom_call_target="tpu_custom_call", output_to_operand_aliasing={{0}: (12, {}), {1}: (13, {})} | custom-call | flops 2717908992 | bytes 4718592 | tf_op jit(solution)/shard_map/gram/pallas_call | solution.py:175
  265.2 16.9 %collective-permute-done.19.rest_5_ = bf16[40,48,128]{2,1,0:T(8,128)(2,1)S(1)} collective-permute-done((bf16[40,48,128]{2,1,0:T(8,128)(2,1)}, bf16[40,48,128]{2,1,0:T(8,128)(2,1)S(1)}, u32[]{:S(2)}, u32[]{:S(2)}) %collective-permute-start.19) | collective-permute-done | bytes 491552 | tf_op jit(solution)/shard_map/ppermute | solution.py:252
  283.0 6.3 %gram.7 = (f32[2,192,384]{2,1,0:T(8,128)S(1)}, f32[2,192,384]{2,1,0:T(8,128)S(1)}) custom-call(f32[1,2]{1,0:T(1,128)S(1)} %copy-done.22, bf16[384,384]{1,0:T(8,128)(2,1)S(1)} %bitcast.13, f32[3,384]{1,0:T(4,128)S(1)} %pad_maximum_fusion.row_ref, f32[48,3]{1,0:T(8,128)S(1)} %bitcast.18, ...), custom_call_target="tpu_custom_call", output_to_operand_aliasing={{0}: (12, {}), {1}: (13, {})} | custom-call | flops 2717908992 | bytes 4718592 | tf_op jit(solution)/shard_map/gram/pallas_call | solution.py:175
  289.3 6.0 %collective-permute-start.36 = (bf16[8,48,128]{2,1,0:T(8,128)(2,1)S(1)}, bf16[8,48,128]{2,1,0:T(8,128)(2,1)S(1)}, u32[]{:S(2)}, u32[]{:S(2)}) collective-permute-start(bf16[8,48,128]{2,1,0:T(8,128)(2,1)S(1)} %copy-done.31), channel_id=1, source_target_pairs={{0,4},{1,5},{2,6},{3,7},{4,0},{5,1},{6,2},{7,3},{8,12},{9,13},{10,... | collective-permute-start | bytes 294920 | tf_op jit(solution)/shard_map/ppermute | solution.py:252
  295.3 12.1 %collective-permute-start.37 = (bf16[8,48,128]{2,1,0:T(8,128)(2,1)S(1)}, bf16[8,48,128]{2,1,0:T(8,128)(2,1)S(1)}, u32[]{:S(2)}, u32[]{:S(2)}) collective-permute-start(bf16[8,48,128]{2,1,0:T(8,128)(2,1)S(1)} %copy-done.30), channel_id=1, source_target_pairs={{0,5},{1,4},{2,7},{3,6},{4,1},{5,0},{6,3},{7,2},{8,13},{9,12},{10,... | collective-permute-start | bytes 294920 | tf_op jit(solution)/shard_map/ppermute | solution.py:252
  307.4 2.4 collective-permute-start.38
  309.8 1.5 collective-permute-start.39
  311.3 8.9 %gram.8 = (f32[2,192,384]{2,1,0:T(8,128)S(1)}, f32[2,192,384]{2,1,0:T(8,128)S(1)}) custom-call(f32[1,2]{1,0:T(1,128)S(1)} %copy-done.22, bf16[384,384]{1,0:T(8,128)(2,1)S(1)} %bitcast.14, f32[3,384]{1,0:T(4,128)S(1)} %pad_maximum_fusion.row_ref, f32[48,3]{1,0:T(8,128)S(1)} %bitcast.19, ...), custom_call_target="tpu_custom_call", output_to_operand_aliasing={{0}: (12, {}), {1}: (13, {})} | custom-call | flops 4529848320 | bytes 6291456 | tf_op jit(solution)/shard_map/gram/pallas_call | solution.py:175
  320.3 2.2 gram.9
  322.6 1.9 collective-permute-done.42.got_ref
  324.8 1.6 collective-permute-start.43
  326.4 1.5 collective-permute-start.44
  328.4 3.1 collective-permute-done.43.rest_1_
  331.4 3.7 %collective-permute-done.44.rest_2_ = f32[96,384]{1,0:T(8,128)S(1)} collective-permute-done((f32[96,384]{1,0:T(8,128)S(1)}, f32[96,384]{1,0:T(8,128)S(1)}, u32[]{:S(2)}, u32[]{:S(2)}) %collective-permute-start.44) | collective-permute-done | bytes 147488 | tf_op jit(solution)/shard_map/ppermute | solution.py:252
  335.3 2.5 collective-permute-start.46
  339.9 1.5 collective-permute-done.46
  (145 shorter events, 25.6 us)
Async XLA Ops:
  6.9 7.7 %collective-permute-start = (bf16[48,16,128]{2,1,0:T(8,128)(2,1)}, bf16[48,16,128]{2,1,0:T(8,128)(2,1)S(1)}, u32[]{:S(2)}, u32[]{:S(2)}) collective-permute-start(bf16[48,16,128]{2,1,0:T(8,128)(2,1)} %get-tuple-element.109), channel_id=1, source_target_pairs={{0,1},{1,0},{2,3},{3,2},{4,5},{5,4},{6,7},{7,6},{8,9},{9,8},{10,11... | collective-permute-start | bytes 589832 | tf_op jit(solution)/shard_map/ppermute | solution.py:252
  7.4 26.0 %collective-permute-start.3 = (bf16[48,16,128]{2,1,0:T(8,128)(2,1)}, bf16[48,16,128]{2,1,0:T(8,128)(2,1)S(1)}, u32[]{:S(2)}, u32[]{:S(2)}) collective-permute-start(bf16[48,16,128]{2,1,0:T(8,128)(2,1)} %get-tuple-element.114), channel_id=1, source_target_pairs={{0,5},{1,4},{2,7},{3,6},{4,1},{5,0},{6,3},{7,2},{8,13},{9,12},{10,... | collective-permute-start | bytes 589832 | tf_op jit(solution)/shard_map/ppermute | solution.py:252
  11.1 33.9 %collective-permute-start.1 = (bf16[48,16,128]{2,1,0:T(8,128)(2,1)}, bf16[48,16,128]{2,1,0:T(8,128)(2,1)S(1)}, u32[]{:S(2)}, u32[]{:S(2)}) collective-permute-start(bf16[48,16,128]{2,1,0:T(8,128)(2,1)} %get-tuple-element.112), channel_id=1, source_target_pairs={{0,7},{1,6},{2,5},{3,4},{4,3},{5,2},{6,1},{7,0},{8,15},{9,14},{10,... | collective-permute-start | bytes 589832 | tf_op jit(solution)/shard_map/ppermute | solution.py:252
  12.2 36.3 %collective-permute-start.2 = (bf16[48,16,128]{2,1,0:T(8,128)(2,1)}, bf16[48,16,128]{2,1,0:T(8,128)(2,1)S(1)}, u32[]{:S(2)}, u32[]{:S(2)}) collective-permute-start(bf16[48,16,128]{2,1,0:T(8,128)(2,1)} %get-tuple-element.113), channel_id=1, source_target_pairs={{0,6},{1,7},{2,4},{3,5},{4,2},{5,3},{6,0},{7,1},{8,14},{9,15},{10,... | collective-permute-start | bytes 589832 | tf_op jit(solution)/shard_map/ppermute | solution.py:252
  14.6 33.8 %collective-permute-start.4 = (bf16[48,16,128]{2,1,0:T(8,128)(2,1)}, bf16[48,16,128]{2,1,0:T(8,128)(2,1)S(1)}, u32[]{:S(2)}, u32[]{:S(2)}) collective-permute-start(bf16[48,16,128]{2,1,0:T(8,128)(2,1)} %get-tuple-element.115), channel_id=1, source_target_pairs={{0,4},{1,5},{2,6},{3,7},{4,0},{5,1},{6,2},{7,3},{8,12},{9,13},{10,... | collective-permute-start | bytes 589832 | tf_op jit(solution)/shard_map/ppermute | solution.py:252
  15.3 33.3 %collective-permute-start.24 = (bf16[48,16,128]{2,1,0:T(8,128)(2,1)}, bf16[48,16,128]{2,1,0:T(8,128)(2,1)S(1)}, u32[]{:S(2)}, u32[]{:S(2)}) collective-permute-start(bf16[48,16,128]{2,1,0:T(8,128)(2,1)} %get-tuple-element.161), channel_id=1, source_target_pairs={{0,2},{1,3},{2,0},{3,1},{4,6},{5,7},{6,4},{7,5},{8,10},{9,11},{10,... | collective-permute-start | bytes 589832 | tf_op jit(solution)/shard_map/ppermute | solution.py:252
  34.1 14.8 %collective-permute-start.30 = (bf16[48,16,128]{2,1,0:T(8,128)(2,1)}, bf16[48,16,128]{2,1,0:T(8,128)(2,1)S(1)}, u32[]{:S(2)}, u32[]{:S(2)}) collective-permute-start(bf16[48,16,128]{2,1,0:T(8,128)(2,1)} %get-tuple-element.172), channel_id=1, source_target_pairs={{0,3},{1,2},{2,1},{3,0},{4,7},{5,6},{6,5},{7,4},{8,11},{9,10},{10,... | collective-permute-start | bytes 589832 | tf_op jit(solution)/shard_map/ppermute | solution.py:252
  45.1 21.6 %collective-permute-start.8 = (bf16[48,32,128]{2,1,0:T(8,128)(2,1)}, bf16[48,32,128]{2,1,0:T(8,128)(2,1)S(1)}, u32[]{:S(2)}, u32[]{:S(2)}) collective-permute-start(bf16[48,32,128]{2,1,0:T(8,128)(2,1)} %get-tuple-element.124), channel_id=1, source_target_pairs={{0,5},{1,4},{2,7},{3,6},{4,1},{5,0},{6,3},{7,2},{8,13},{9,12},{10,... | collective-permute-start | bytes 1179656 | tf_op jit(solution)/shard_map/ppermute | solution.py:252
  48.5 20.4 %collective-permute-start.5 = (bf16[48,32,128]{2,1,0:T(8,128)(2,1)}, bf16[48,32,128]{2,1,0:T(8,128)(2,1)S(1)}, u32[]{:S(2)}, u32[]{:S(2)}) collective-permute-start(bf16[48,32,128]{2,1,0:T(8,128)(2,1)} %get-tuple-element.116), channel_id=1, source_target_pairs={{0,1},{1,0},{2,3},{3,2},{4,5},{5,4},{6,7},{7,6},{8,9},{9,8},{10,11... | collective-permute-start | bytes 1179656 | tf_op jit(solution)/shard_map/ppermute | solution.py:252
  48.6 34.8 %collective-permute-start.25 = (bf16[48,32,128]{2,1,0:T(8,128)(2,1)}, bf16[48,32,128]{2,1,0:T(8,128)(2,1)S(1)}, u32[]{:S(2)}, u32[]{:S(2)}) collective-permute-start(bf16[48,32,128]{2,1,0:T(8,128)(2,1)} %get-tuple-element.162), channel_id=1, source_target_pairs={{0,2},{1,3},{2,0},{3,1},{4,6},{5,7},{6,4},{7,5},{8,10},{9,11},{10,... | collective-permute-start | bytes 1179656 | tf_op jit(solution)/shard_map/ppermute | solution.py:252
  49.6 52.2 %collective-permute-start.31 = (bf16[48,32,128]{2,1,0:T(8,128)(2,1)}, bf16[48,32,128]{2,1,0:T(8,128)(2,1)S(1)}, u32[]{:S(2)}, u32[]{:S(2)}) collective-permute-start(bf16[48,32,128]{2,1,0:T(8,128)(2,1)} %get-tuple-element.173), channel_id=1, source_target_pairs={{0,3},{1,2},{2,1},{3,0},{4,7},{5,6},{6,5},{7,4},{8,11},{9,10},{10,... | collective-permute-start | bytes 1179656 | tf_op jit(solution)/shard_map/ppermute | solution.py:252
  51.1 50.7 %collective-permute-start.9 = (bf16[48,32,128]{2,1,0:T(8,128)(2,1)}, bf16[48,32,128]{2,1,0:T(8,128)(2,1)S(1)}, u32[]{:S(2)}, u32[]{:S(2)}) collective-permute-start(bf16[48,32,128]{2,1,0:T(8,128)(2,1)} %get-tuple-element.126), channel_id=1, source_target_pairs={{0,4},{1,5},{2,6},{3,7},{4,0},{5,1},{6,2},{7,3},{8,12},{9,13},{10,... | collective-permute-start | bytes 1179656 | tf_op jit(solution)/shard_map/ppermute | solution.py:252
  66.7 43.3 %collective-permute-start.7 = (bf16[48,32,128]{2,1,0:T(8,128)(2,1)}, bf16[48,32,128]{2,1,0:T(8,128)(2,1)S(1)}, u32[]{:S(2)}, u32[]{:S(2)}) collective-permute-start(bf16[48,32,128]{2,1,0:T(8,128)(2,1)} %get-tuple-element.122), channel_id=1, source_target_pairs={{0,6},{1,7},{2,4},{3,5},{4,2},{5,3},{6,0},{7,1},{8,14},{9,15},{10,... | collective-permute-start | bytes 1179656 | tf_op jit(solution)/shard_map/ppermute | solution.py:252
  68.9 41.1 %collective-permute-start.6 = (bf16[48,32,128]{2,1,0:T(8,128)(2,1)}, bf16[48,32,128]{2,1,0:T(8,128)(2,1)S(1)}, u32[]{:S(2)}, u32[]{:S(2)}) collective-permute-start(bf16[48,32,128]{2,1,0:T(8,128)(2,1)} %get-tuple-element.120), channel_id=1, source_target_pairs={{0,7},{1,6},{2,5},{3,4},{4,3},{5,2},{6,1},{7,0},{8,15},{9,14},{10,... | collective-permute-start | bytes 1179656 | tf_op jit(solution)/shard_map/ppermute | solution.py:252
  83.4 59.1 %collective-permute-start.17 = (bf16[24,48,128]{2,1,0:T(8,128)(2,1)}, bf16[24,48,128]{2,1,0:T(8,128)(2,1)S(1)}, u32[]{:S(2)}, u32[]{:S(2)}) collective-permute-start(bf16[24,48,128]{2,1,0:T(8,128)(2,1)} %get-tuple-element.146), channel_id=1, source_target_pairs={{0,5},{1,4},{2,7},{3,6},{4,1},{5,0},{6,3},{7,2},{8,13},{9,12},{10,... | collective-permute-start | bytes 884744 | tf_op jit(solution)/shard_map/ppermute | solution.py:252
  101.8 42.9 %collective-permute-start.32 = (bf16[24,48,128]{2,1,0:T(8,128)(2,1)}, bf16[24,48,128]{2,1,0:T(8,128)(2,1)S(1)}, u32[]{:S(2)}, u32[]{:S(2)}) collective-permute-start(bf16[24,48,128]{2,1,0:T(8,128)(2,1)} %get-tuple-element.174), channel_id=1, source_target_pairs={{0,3},{1,2},{2,1},{3,0},{4,7},{5,6},{6,5},{7,4},{8,11},{9,10},{10,... | collective-permute-start | bytes 884744 | tf_op jit(solution)/shard_map/ppermute | solution.py:252
  101.8 43.0 %collective-permute-start.26 = (bf16[24,48,128]{2,1,0:T(8,128)(2,1)}, bf16[24,48,128]{2,1,0:T(8,128)(2,1)}, u32[]{:S(2)}, u32[]{:S(2)}) collective-permute-start(bf16[24,48,128]{2,1,0:T(8,128)(2,1)} %get-tuple-element.163), channel_id=1, source_target_pairs={{0,2},{1,3},{2,0},{3,1},{4,6},{5,7},{6,4},{7,5},{8,10},{9,11},{10,... | collective-permute-start | bytes 884744 | tf_op jit(solution)/shard_map/ppermute | solution.py:252
  110.0 51.8 %collective-permute-start.20 = (bf16[24,48,128]{2,1,0:T(8,128)(2,1)}, bf16[24,48,128]{2,1,0:T(8,128)(2,1)}, u32[]{:S(2)}, u32[]{:S(2)}) collective-permute-start(bf16[24,48,128]{2,1,0:T(8,128)(2,1)} %get-tuple-element.152), channel_id=1, source_target_pairs={{0,4},{1,5},{2,6},{3,7},{4,0},{5,1},{6,2},{7,3},{8,12},{9,13},{10,... | collective-permute-start | bytes 884744 | tf_op jit(solution)/shard_map/ppermute | solution.py:252
  124.8 37.0 %collective-permute-start.14 = (bf16[24,48,128]{2,1,0:T(8,128)(2,1)}, bf16[24,48,128]{2,1,0:T(8,128)(2,1)}, u32[]{:S(2)}, u32[]{:S(2)}) collective-permute-start(bf16[24,48,128]{2,1,0:T(8,128)(2,1)} %get-tuple-element.140), channel_id=1, source_target_pairs={{0,6},{1,7},{2,4},{3,5},{4,2},{5,3},{6,0},{7,1},{8,14},{9,15},{10,... | collective-permute-start | bytes 884744 | tf_op jit(solution)/shard_map/ppermute | solution.py:252
  142.4 26.3 %collective-permute-start.11 = (bf16[24,48,128]{2,1,0:T(8,128)(2,1)}, bf16[24,48,128]{2,1,0:T(8,128)(2,1)}, u32[]{:S(2)}, u32[]{:S(2)}) collective-permute-start(bf16[24,48,128]{2,1,0:T(8,128)(2,1)} %get-tuple-element.134), channel_id=1, source_target_pairs={{0,7},{1,6},{2,5},{3,4},{4,3},{5,2},{6,1},{7,0},{8,15},{9,14},{10,... | collective-permute-start | bytes 884744 | tf_op jit(solution)/shard_map/ppermute | solution.py:252
  144.7 30.8 %collective-permute-start.10 = (bf16[24,48,128]{2,1,0:T(8,128)(2,1)}, bf16[24,48,128]{2,1,0:T(8,128)(2,1)}, u32[]{:S(2)}, u32[]{:S(2)}) collective-permute-start(bf16[24,48,128]{2,1,0:T(8,128)(2,1)} %get-tuple-element.127), channel_id=1, source_target_pairs={{0,1},{1,0},{2,3},{3,2},{4,5},{5,4},{6,7},{7,6},{8,9},{9,8},{10,11... | collective-permute-start | bytes 884744 | tf_op jit(solution)/shard_map/ppermute | solution.py:252
  144.8 48.4 %collective-permute-start.18 = (bf16[24,48,128]{2,1,0:T(8,128)(2,1)}, bf16[24,48,128]{2,1,0:T(8,128)(2,1)}, u32[]{:S(2)}, u32[]{:S(2)}) collective-permute-start(bf16[24,48,128]{2,1,0:T(8,128)(2,1)} %get-tuple-element.147), channel_id=1, source_target_pairs={{0,5},{1,4},{2,7},{3,6},{4,1},{5,0},{6,3},{7,2},{8,13},{9,12},{10,... | collective-permute-start | bytes 884744 | tf_op jit(solution)/shard_map/ppermute | solution.py:252
  161.8 52.5 %collective-permute-start.33 = (bf16[24,48,128]{2,1,0:T(8,128)(2,1)}, bf16[24,48,128]{2,1,0:T(8,128)(2,1)}, u32[]{:S(2)}, u32[]{:S(2)}) collective-permute-start(bf16[24,48,128]{2,1,0:T(8,128)(2,1)} %get-tuple-element.175), channel_id=1, source_target_pairs={{0,3},{1,2},{2,1},{3,0},{4,7},{5,6},{6,5},{7,4},{8,11},{9,10},{10,... | collective-permute-start | bytes 884744 | tf_op jit(solution)/shard_map/ppermute | solution.py:252
  161.8 52.5 %collective-permute-start.27 = (bf16[24,48,128]{2,1,0:T(8,128)(2,1)}, bf16[24,48,128]{2,1,0:T(8,128)(2,1)}, u32[]{:S(2)}, u32[]{:S(2)}) collective-permute-start(bf16[24,48,128]{2,1,0:T(8,128)(2,1)} %get-tuple-element.164), channel_id=1, source_target_pairs={{0,2},{1,3},{2,0},{3,1},{4,6},{5,7},{6,4},{7,5},{8,10},{9,11},{10,... | collective-permute-start | bytes 884744 | tf_op jit(solution)/shard_map/ppermute | solution.py:252
  168.7 45.5 %collective-permute-start.21 = (bf16[24,48,128]{2,1,0:T(8,128)(2,1)}, bf16[24,48,128]{2,1,0:T(8,128)(2,1)}, u32[]{:S(2)}, u32[]{:S(2)}) collective-permute-start(bf16[24,48,128]{2,1,0:T(8,128)(2,1)} %get-tuple-element.153), channel_id=1, source_target_pairs={{0,4},{1,5},{2,6},{3,7},{4,0},{5,1},{6,2},{7,3},{8,12},{9,13},{10,... | collective-permute-start | bytes 884744 | tf_op jit(solution)/shard_map/ppermute | solution.py:252
  175.5 40.9 %collective-permute-start.15 = (bf16[24,48,128]{2,1,0:T(8,128)(2,1)}, bf16[24,48,128]{2,1,0:T(8,128)(2,1)}, u32[]{:S(2)}, u32[]{:S(2)}) collective-permute-start(bf16[24,48,128]{2,1,0:T(8,128)(2,1)} %get-tuple-element.141), channel_id=1, source_target_pairs={{0,6},{1,7},{2,4},{3,5},{4,2},{5,3},{6,0},{7,1},{8,14},{9,15},{10,... | collective-permute-start | bytes 884744 | tf_op jit(solution)/shard_map/ppermute | solution.py:252
  193.2 23.4 %collective-permute-start.12 = (bf16[24,48,128]{2,1,0:T(8,128)(2,1)}, bf16[24,48,128]{2,1,0:T(8,128)(2,1)}, u32[]{:S(2)}, u32[]{:S(2)}) collective-permute-start(bf16[24,48,128]{2,1,0:T(8,128)(2,1)} %get-tuple-element.135), channel_id=1, source_target_pairs={{0,7},{1,6},{2,5},{3,4},{4,3},{5,2},{6,1},{7,0},{8,15},{9,14},{10,... | collective-permute-start | bytes 884744 | tf_op jit(solution)/shard_map/ppermute | solution.py:252
  214.2 22.8 %collective-permute-start.41 = (bf16[24,48,128]{2,1,0:T(8,128)(2,1)}, bf16[24,48,128]{2,1,0:T(8,128)(2,1)S(1)}, u32[]{:S(2)}, u32[]{:S(2)}) collective-permute-start(bf16[24,48,128]{2,1,0:T(8,128)(2,1)} %get-tuple-element.191), channel_id=1, source_target_pairs={{0,1},{1,0},{2,3},{3,2},{4,5},{5,4},{6,7},{7,6},{8,9},{9,8},{10,11... | collective-permute-start | bytes 884744 | tf_op jit(solution)/shard_map/ppermute | solution.py:252
  214.3 31.5 %collective-permute-start.34 = (bf16[40,48,128]{2,1,0:T(8,128)(2,1)}, bf16[40,48,128]{2,1,0:T(8,128)(2,1)S(1)}, u32[]{:S(2)}, u32[]{:S(2)}) collective-permute-start(bf16[40,48,128]{2,1,0:T(8,128)(2,1)} %get-tuple-element.176), channel_id=1, source_target_pairs={{0,3},{1,2},{2,1},{3,0},{4,7},{5,6},{6,5},{7,4},{8,11},{9,10},{10,... | collective-permute-start | bytes 1474568 | tf_op jit(solution)/shard_map/ppermute | solution.py:252
  214.3 42.6 %collective-permute-start.28 = (bf16[40,48,128]{2,1,0:T(8,128)(2,1)}, bf16[40,48,128]{2,1,0:T(8,128)(2,1)S(1)}, u32[]{:S(2)}, u32[]{:S(2)}) collective-permute-start(bf16[40,48,128]{2,1,0:T(8,128)(2,1)} %get-tuple-element.165), channel_id=1, source_target_pairs={{0,2},{1,3},{2,0},{3,1},{4,6},{5,7},{6,4},{7,5},{8,10},{9,11},{10,... | collective-permute-start | bytes 1474568 | tf_op jit(solution)/shard_map/ppermute | solution.py:252
  216.4 48.7 %collective-permute-start.22 = (bf16[40,48,128]{2,1,0:T(8,128)(2,1)}, bf16[40,48,128]{2,1,0:T(8,128)(2,1)S(1)}, u32[]{:S(2)}, u32[]{:S(2)}) collective-permute-start(bf16[40,48,128]{2,1,0:T(8,128)(2,1)} %get-tuple-element.154), channel_id=1, source_target_pairs={{0,4},{1,5},{2,6},{3,7},{4,0},{5,1},{6,2},{7,3},{8,12},{9,13},{10,... | collective-permute-start | bytes 1474568 | tf_op jit(solution)/shard_map/ppermute | solution.py:252
  216.6 65.5 %collective-permute-start.19 = (bf16[40,48,128]{2,1,0:T(8,128)(2,1)}, bf16[40,48,128]{2,1,0:T(8,128)(2,1)S(1)}, u32[]{:S(2)}, u32[]{:S(2)}) collective-permute-start(bf16[40,48,128]{2,1,0:T(8,128)(2,1)} %get-tuple-element.148), channel_id=1, source_target_pairs={{0,5},{1,4},{2,7},{3,6},{4,1},{5,0},{6,3},{7,2},{8,13},{9,12},{10,... | collective-permute-start | bytes 1474568 | tf_op jit(solution)/shard_map/ppermute | solution.py:252
  237.0 70.3 %collective-permute-start.40 = (bf16[40,48,128]{2,1,0:T(8,128)(2,1)S(1)}, bf16[40,48,128]{2,1,0:T(8,128)(2,1)S(1)}, u32[]{:S(2)}, u32[]{:S(2)}) collective-permute-start(bf16[40,48,128]{2,1,0:T(8,128)(2,1)S(1)} %copy-done.24), channel_id=1, source_target_pairs={{0,1},{1,0},{2,3},{3,2},{4,5},{5,4},{6,7},{7,6},{8,9},{9,8},{10,11... | collective-permute-start | bytes 1474568 | tf_op jit(solution)/shard_map/ppermute | solution.py:252
  245.8 43.5 %collective-permute-start.16 = (bf16[40,48,128]{2,1,0:T(8,128)(2,1)S(1)}, bf16[40,48,128]{2,1,0:T(8,128)(2,1)S(1)}, u32[]{:S(2)}, u32[]{:S(2)}) collective-permute-start(bf16[40,48,128]{2,1,0:T(8,128)(2,1)S(1)} %copy-done.26), channel_id=1, source_target_pairs={{0,6},{1,7},{2,4},{3,5},{4,2},{5,3},{6,0},{7,1},{8,14},{9,15},{10,... | collective-permute-start | bytes 1474568 | tf_op jit(solution)/shard_map/ppermute | solution.py:252
  256.9 38.4 %collective-permute-start.13 = (bf16[40,48,128]{2,1,0:T(8,128)(2,1)S(1)}, bf16[40,48,128]{2,1,0:T(8,128)(2,1)S(1)}, u32[]{:S(2)}, u32[]{:S(2)}) collective-permute-start(bf16[40,48,128]{2,1,0:T(8,128)(2,1)S(1)} %copy-done.25), channel_id=1, source_target_pairs={{0,7},{1,6},{2,5},{3,4},{4,3},{5,2},{6,1},{7,0},{8,15},{9,14},{10,... | collective-permute-start | bytes 1474568 | tf_op jit(solution)/shard_map/ppermute | solution.py:252
  265.2 44.6 %collective-permute-start.35 = (bf16[8,48,128]{2,1,0:T(8,128)(2,1)S(1)}, bf16[8,48,128]{2,1,0:T(8,128)(2,1)S(1)}, u32[]{:S(2)}, u32[]{:S(2)}) collective-permute-start(bf16[8,48,128]{2,1,0:T(8,128)(2,1)S(1)} %copy-done.33), channel_id=1, source_target_pairs={{0,3},{1,2},{2,1},{3,0},{4,7},{5,6},{6,5},{7,4},{8,11},{9,10},{10,... | collective-permute-start | bytes 294920 | tf_op jit(solution)/shard_map/ppermute | solution.py:252
  282.1 27.7 %collective-permute-start.29 = (bf16[8,48,128]{2,1,0:T(8,128)(2,1)S(1)}, bf16[8,48,128]{2,1,0:T(8,128)(2,1)S(1)}, u32[]{:S(2)}, u32[]{:S(2)}) collective-permute-start(bf16[8,48,128]{2,1,0:T(8,128)(2,1)S(1)} %copy-done.32), channel_id=1, source_target_pairs={{0,2},{1,3},{2,0},{3,1},{4,6},{5,7},{6,4},{7,5},{8,10},{9,11},{10,... | collective-permute-start | bytes 294920 | tf_op jit(solution)/shard_map/ppermute | solution.py:252
  289.3 30.9 %collective-permute-start.36 = (bf16[8,48,128]{2,1,0:T(8,128)(2,1)S(1)}, bf16[8,48,128]{2,1,0:T(8,128)(2,1)S(1)}, u32[]{:S(2)}, u32[]{:S(2)}) collective-permute-start(bf16[8,48,128]{2,1,0:T(8,128)(2,1)S(1)} %copy-done.31), channel_id=1, source_target_pairs={{0,4},{1,5},{2,6},{3,7},{4,0},{5,1},{6,2},{7,3},{8,12},{9,13},{10,... | collective-permute-start | bytes 294920 | tf_op jit(solution)/shard_map/ppermute | solution.py:252
  295.3 24.9 %collective-permute-start.37 = (bf16[8,48,128]{2,1,0:T(8,128)(2,1)S(1)}, bf16[8,48,128]{2,1,0:T(8,128)(2,1)S(1)}, u32[]{:S(2)}, u32[]{:S(2)}) collective-permute-start(bf16[8,48,128]{2,1,0:T(8,128)(2,1)S(1)} %copy-done.30), channel_id=1, source_target_pairs={{0,5},{1,4},{2,7},{3,6},{4,1},{5,0},{6,3},{7,2},{8,13},{9,12},{10,... | collective-permute-start | bytes 294920 | tf_op jit(solution)/shard_map/ppermute | solution.py:252
  307.4 12.9 %collective-permute-start.38 = (bf16[8,48,128]{2,1,0:T(8,128)(2,1)S(1)}, bf16[8,48,128]{2,1,0:T(8,128)(2,1)S(1)}, u32[]{:S(2)}, u32[]{:S(2)}) collective-permute-start(bf16[8,48,128]{2,1,0:T(8,128)(2,1)S(1)} %copy-done.29), channel_id=1, source_target_pairs={{0,6},{1,7},{2,4},{3,5},{4,2},{5,3},{6,0},{7,1},{8,14},{9,15},{10,... | collective-permute-start | bytes 294920 | tf_op jit(solution)/shard_map/ppermute | solution.py:252
  309.8 10.4 %collective-permute-start.23 = (bf16[8,48,128]{2,1,0:T(8,128)(2,1)S(1)}, bf16[8,48,128]{2,1,0:T(8,128)(2,1)S(1)}, u32[]{:S(2)}, u32[]{:S(2)}) collective-permute-start(bf16[8,48,128]{2,1,0:T(8,128)(2,1)S(1)} %copy-done.28), channel_id=1, source_target_pairs={{0,1},{1,0},{2,3},{3,2},{4,5},{5,4},{6,7},{7,6},{8,9},{9,8},{10,11... | collective-permute-start | bytes 294920 | tf_op jit(solution)/shard_map/ppermute | solution.py:252
  309.8 10.4 %collective-permute-start.39 = (bf16[8,48,128]{2,1,0:T(8,128)(2,1)S(1)}, bf16[8,48,128]{2,1,0:T(8,128)(2,1)S(1)}, u32[]{:S(2)}, u32[]{:S(2)}) collective-permute-start(bf16[8,48,128]{2,1,0:T(8,128)(2,1)S(1)} %copy-done.27), channel_id=1, source_target_pairs={{0,7},{1,6},{2,5},{3,4},{4,3},{5,2},{6,1},{7,0},{8,15},{9,14},{10,... | collective-permute-start | bytes 294920 | tf_op jit(solution)/shard_map/ppermute | solution.py:252
  324.8 6.6 %collective-permute-start.43 = (f32[96,384]{1,0:T(8,128)S(1)}, f32[96,384]{1,0:T(8,128)S(1)}, u32[]{:S(2)}, u32[]{:S(2)}) collective-permute-start(f32[96,384]{1,0:T(8,128)S(1)} %get-tuple-element.206), channel_id=1, source_target_pairs={{0,8},{8,0},{16,24},{24,16},{1,9},{9,1},{17,25},{25,17},{2,10},{10... | collective-permute-start | bytes 442376 | tf_op jit(solution)/shard_map/ppermute | solution.py:252
  326.4 8.8 %collective-permute-start.44 = (f32[96,384]{1,0:T(8,128)S(1)}, f32[96,384]{1,0:T(8,128)S(1)}, u32[]{:S(2)}, u32[]{:S(2)}) collective-permute-start(f32[96,384]{1,0:T(8,128)S(1)} %get-tuple-element.207), channel_id=1, source_target_pairs={{0,16},{8,24},{16,0},{24,8},{1,17},{9,25},{17,1},{25,9},{2,18},{10... | collective-permute-start | bytes 442376 | tf_op jit(solution)/shard_map/ppermute | solution.py:252
  327.9 7.2 %collective-permute-start.45 = (f32[96,384]{1,0:T(8,128)S(1)}, f32[96,384]{1,0:T(8,128)S(1)}, u32[]{:S(2)}, u32[]{:S(2)}) collective-permute-start(f32[96,384]{1,0:T(8,128)S(1)} %get-tuple-element.208), channel_id=1, source_target_pairs={{0,24},{8,16},{16,8},{24,0},{1,25},{9,17},{17,9},{25,1},{2,26},{10... | collective-permute-start | bytes 442376 | tf_op jit(solution)/shard_map/ppermute | solution.py:252
  335.3 6.1 %collective-permute-start.46 = (f32[2,48,96]{2,1,0:T(8,128)S(1)}, f32[2,48,96]{2,1,0:T(8,128)S(1)}, u32[]{:S(2)}, u32[]{:S(2)}) collective-permute-start(f32[2,48,96]{2,1,0:T(8,128)S(1)} %get-tuple-element.209), channel_id=1, source_target_pairs={{0,6},{1,7},{2,4},{3,5},{4,2},{5,3},{6,0},{7,1},{8,14},{9,15},{10,... | collective-permute-start | bytes 110600 | tf_op jit(solution)/shard_map/ppermute | solution.py:252
  337.8 5.1 %collective-permute-start.47 = (f32[2,48,96]{2,1,0:T(8,128)S(1)}, f32[2,48,96]{2,1,0:T(8,128)S(1)}, u32[]{:S(2)}, u32[]{:S(2)}) collective-permute-start(f32[2,48,96]{2,1,0:T(8,128)S(1)} %get-tuple-element.210), channel_id=1, source_target_pairs={{0,4},{1,5},{2,6},{3,7},{4,0},{5,1},{6,2},{7,3},{8,12},{9,13},{10,... | collective-permute-start | bytes 110600 | tf_op jit(solution)/shard_map/ppermute | solution.py:252
  338.3 4.7 %collective-permute-start.48 = (f32[2,48,96]{2,1,0:T(8,128)S(1)}, f32[2,48,96]{2,1,0:T(8,128)S(1)}, u32[]{:S(2)}, u32[]{:S(2)}) collective-permute-start(f32[2,48,96]{2,1,0:T(8,128)S(1)} %get-tuple-element.211), channel_id=1, source_target_pairs={{0,2},{1,3},{2,0},{3,1},{4,6},{5,7},{6,4},{7,5},{8,10},{9,11},{10,... | collective-permute-start | bytes 110600 | tf_op jit(solution)/shard_map/ppermute | solution.py:252
  (35 other events, 609.3 us)
